TPU v7x, 32 devices: a whole 2x2x4 slice. The times are simulated.
32 devices in a mesh: groups: 2 (over y), tiles: 4 (over z), depth: 2 (over x), sub: 2 (over core).
Axes of the slice: x: 2, y: 2, z: 4, core: 2. Of those that a mesh axis runs over, the one named last changes fastest.
Arguments:
- state_init: float32 [8, 4, 16, 4096], P('groups', 'depth', 'tiles', 'sub'), parts along dimension 0, may hold values from -6 to 6
- cotangent: float32 [8, 4, 16, 4096], P('groups', 'depth', 'tiles', 'sub'), parts along dimension 0, may hold values from -6 to 6
- level_count: int32 [16, 4096], P('tiles', 'sub'), may hold values from 0 to 4, as said below
- west_east: int32 [16, 2], P('tiles'), may hold values from -1 to 15, as said below
- south_north: int32 [16, 2], P('tiles'), may hold values from -1 to 3, as said below
- weight_in: bfloat16 [128, 12], replicated, may hold values from -1.75 to 1.75
- bias_in: float32 [128], replicated, may hold values from -3 to 3
- weight_mid: bfloat16 [128, 128], replicated, may hold values from -0.5 to 0.5
- bias_mid: float32 [128], replicated, may hold values from -3 to 3
- weight_out: bfloat16 [4, 128], replicated, may hold values from -0.5 to 0.5
- bias_out: float32 [4], replicated, may hold values from -3 to 3
- mix_horizontal: float32 [4], replicated, may hold values from 0.03 to 0.12
- mix_vertical: float32 [4], P('depth'), may hold values from 0.05 to 0.25
Outputs:
- final_state: float32 [8, 4, 16, 4096], P('groups', 'depth', 'tiles', 'sub'), parts along dimension 0
- initial_cot: float32 [8, 4, 16, 4096], P('groups', 'depth', 'tiles', 'sub'), parts along dimension 0
- grad_weight_in: float32 [256, 12], P('groups'), parts along dimension 0
- grad_bias_in: float32 [256], P('groups'), parts along dimension 0
- grad_weight_mid: float32 [256, 128], P('groups'), parts along dimension 0
- grad_bias_mid: float32 [256], P('groups'), parts along dimension 0
- grad_weight_out: float32 [8, 128], P('groups'), parts along dimension 0
- grad_bias_out: float32 [8], P('groups'), parts along dimension 0
There are 2 independent parts, one for each index of `groups`. A program takes and returns all parts, laid end to end along the dimension named above; an argument that names none is the same for every part. Nothing has to cross between parts.
Inputs may be any that keep to these rules, and one draw needn't show every extreme that they name: Level k of column c of slot g is ocean where k < level_count[g, c]; 0 is land. A slot that holds no ocean tile is 0 in every column. `west_east`: entry [g, 0] is the slot of the tile that borders slot g on the west and [g, 1] the one on the east, or -1 where there is none, where the edge between them is closed, or where either of the two holds no ocean tile. The relation is mutual: b is the west neighbour of g exactly when g is the east neighbour of b, and a tile never borders itself. Call slots t * 4 to t * 4 + 3 a group; of the tiles of one group, at most 2 are west or east neighbours of tiles of one other group, and some pair of groups reaches 2 in every draw. `south_north`: entry [g, 0] gives the tile on the south of slot g and [g, 1] the one on the north, as a position among the slots of the same group (the tile in slot g - g % 4 + entry), or -1 where there is none, where the edge between them is closed, or where either of the two holds no ocean tile. The relation is mutual.
All inputs are finite; a program needn't handle non-finite values.
Results may differ from a plain program's by a relative error of at most 0.0088.
Values sent between devices are 32-bit elements; how exact they have to be, the bound alone decides.
No kernel may reach another device: no remote copies, remote signals or barrier semaphores. Data moves between devices by JAX's collectives and lax.ppermute only.
A program may use at most 64 MiB of HBM per device.

v0:
```python
import functools
import math

import jax
import jax.numpy as jnp
from jax import lax
from jax.experimental import pallas as pl
from jax.experimental.pallas import tpu as pltpu
from jax.sharding import PartitionSpec as P

TCOL = 64
LANES = 128
CHUNK = 256
BF = jnp.bfloat16
F32 = jnp.float32
VMEM_BYTES = 40 * 1024 * 1024
NT = (((1,), (1,)), ((), ()))


def dot(left, right):
    return jnp.dot(left, right, preferred_element_type=F32)


def dot_nt(left, right):
    return lax.dot_general(left, right, NT, preferred_element_type=F32)


def iota(shape, axis):
    return lax.broadcasted_iota(jnp.int32, shape, axis)


def wide(block, copies):
    return jnp.concatenate([block] * copies, axis=1)


def pack_columns(first, last):
    place = iota((8, LANES), 1) & 63
    packed = jnp.zeros((8, LANES), F32)
    for v in range(first.shape[1] // LANES):
        span = slice(v * LANES, (v + 1) * LANES)
        low = pltpu.roll(first[:, span], v, 1) if v else first[:, span]
        high = pltpu.roll(last[:, span], v + 17, 1)
        packed = jnp.where(place == v, low, packed)
        packed = jnp.where(place == 16 + v, high, packed)
    return packed


def pack_lines(first, last):
    cells = first.shape[1]
    lane = iota((8, LANES), 1)
    return jnp.where(lane < TCOL, first[:, :LANES], last[:, cells - LANES :])


def spread_columns(east_pack, west_pack, cells):
    count = cells // LANES
    east = jnp.concatenate([pltpu.roll(east_pack, 63 - v, 1) for v in range(count)], axis=1)
    west = jnp.concatenate([pltpu.roll(west_pack, 48 - v, 1) for v in range(count)], axis=1)
    return east, west


def packs_for(slot, we, sn, pools, partner, slots):
    here = lax.axis_index("tiles")
    half = lax.axis_index("sub")

    def column_pack(tile):
        safe = jnp.maximum(tile, 0)
        owner = lax.div(safe, slots)
        inside = lax.rem(safe, slots)
        where_from = jnp.bitwise_xor(here, owner)
        found = pools[0][inside]
        for k in range(1, len(pools)):
            found = jnp.where(where_from == k, pools[k][inside], found)
        return jnp.where(tile >= 0, found, 0.0)

    def line_pack(other):
        found = partner[jnp.maximum(other, 0)]
        return jnp.where(other >= 0, found, 0.0)

    west = column_pack(we[slot, 0])
    east = column_pack(we[slot, 1])
    south = line_pack(jnp.where(half == 0, sn[slot, 0], slot))
    north = line_pack(jnp.where(half == 0, slot, sn[slot, 1]))
    lane = iota((8, LANES), 1)
    lines = jnp.where(lane < TCOL, pltpu.roll(south, TCOL, 1), pltpu.roll(north, TCOL, 1))
    return east, west, lines


def halo_fields(packs, cells):
    east_pack, west_pack, lines = packs
    east, west = spread_columns(east_pack, west_pack, cells)
    return east, west, wide(lines, cells // LANES)


def places(cells):
    lane = iota((8, cells), 1)
    column = lane & (TCOL - 1)
    return column == TCOL - 1, column == 0, lane >= cells - TCOL, lane < TCOL


def neighbours(x, packs):
    cells = x.shape[1]
    east_halo, west_halo, lines = halo_fields(packs, cells)
    at_east, at_west, at_north, at_south = places(cells)
    east = jnp.where(at_east, east_halo, pltpu.roll(x, cells - 1, 1))
    west = jnp.where(at_west, west_halo, pltpu.roll(x, 1, 1))
    north = jnp.where(at_north, lines, pltpu.roll(x, cells - TCOL, 1))
    south = jnp.where(at_south, lines, pltpu.roll(x, TCOL, 1))
    return east, west, north, south


def halo_sum(packs, cells):
    east_halo, west_halo, lines = halo_fields(packs, cells)
    at_east, at_west, at_north, at_south = places(cells)
    columns = jnp.where(at_east, east_halo, jnp.where(at_west, west_halo, 0.0))
    return columns + jnp.where(at_north | at_south, lines, 0.0)


def pull_back(e_east, e_west, e_north, e_south):
    cells = e_east.shape[1]
    at_east, at_west, at_north, at_south = places(cells)
    return (
        jnp.where(at_west, 0.0, pltpu.roll(e_east, 1, 1))
        + jnp.where(at_east, 0.0, pltpu.roll(e_west, cells - 1, 1))
    ) + (
        jnp.where(at_south, 0.0, pltpu.roll(e_north, TCOL, 1))
        + jnp.where(at_north, 0.0, pltpu.roll(e_south, cells - TCOL, 1))
    )


def level_sends(even, odd):
    top = iota(even.shape, 0) < 4
    down = jnp.where(top, pltpu.roll(even, 4, 0), odd)
    up = jnp.where(top, even, pltpu.roll(odd, 4, 0))
    return down, up


def half_send(x, parity):
    top = iota(x.shape, 0) < 4
    turned = pltpu.roll(x, 4, 0)
    if parity == 0:
        return jnp.where(top, turned, 0.0), jnp.where(top, x, 0.0)
    return jnp.where(top, 0.0, x), jnp.where(top, 0.0, turned)


def level_halo(above, below, odd):
    depth = lax.axis_index("depth")
    last = lax.axis_size("depth") - 1
    above = jnp.where(depth > 0, above, 0.0)
    below = jnp.where(depth < last, below, 0.0)
    top = iota(above.shape, 0) < 4
    straight = jnp.where(top, above, below)
    turned = pltpu.roll(jnp.where(top, below, above), 4, 0)
    return jnp.where((iota(above.shape, 0) < 4) == (odd == 0), straight, turned)


def prep_kernel(mix_v, state, cot, count, x_out, g_out, mask_out, columns, lines, *sends):
    slots = state.shape[2]
    cells = state.shape[3]
    depth = lax.axis_index("depth")
    row = iota((8, cells), 0)
    level = 2 * depth + jnp.where(row < 4, 0, 1)
    mv = jnp.where(iota((8, cells), 0) < 4, mix_v[0], mix_v[1])
    for s in range(slots):
        for l in range(2):
            for f in range(4):
                r = 4 * l + f
                x_out[s, r : r + 1, :] = state[f, l, s : s + 1, :]
                g_out[s, r : r + 1, :] = cot[f, l, s : s + 1, :]
        deep = jnp.broadcast_to(count[s : s + 1, :], (8, cells))
        mask = jnp.where(level < deep, 1.0, 0.0)
        x = mask * x_out[s]
        x_out[s] = x
        g_out[s] = mask * g_out[s]
        mask_out[s] = mask
        columns[s] = pack_columns(x, x)
        lines[s] = pack_lines(x, x)
    for i in range(slots // 2):
        for kind in range(2):
            if kind == 0:
                even, odd = x_out[2 * i], x_out[2 * i + 1]
            else:
                even, odd = mv * g_out[2 * i], mv * g_out[2 * i + 1]
            down, up = level_sends(even, odd)
            if len(sends) == 1:
                sends[0][kind, i] = jnp.where(depth == 0, down, up)
            else:
                sends[0][kind, i] = down
                sends[1][kind, i] = up


def weight_kernel(
    mix_h, mix_v, bias_out, w_in, b_in, w_mid, b_mid, w_out, in_all, in_back, mid_all, mid_back,
    bias_mid, out_all, out_back, rows
):
    hidden = w_mid.shape[0]
    feature = w_in.shape[1]
    high = b_in[...].astype(BF).astype(F32)
    low = b_in[...] - high
    row = iota((32, hidden), 0)
    halves = []
    for l in range(2):
        r = iota((32, feature), 0)
        c = iota((32, feature), 1)
        chosen = (r < 24) & (((r >> 2) & 1) == l) & ((r >> 3) * 4 + (r & 3) == c)
        part = dot_nt(jnp.where(chosen, 1.0, 0.0).astype(BF), w_in[...])
        part = jnp.where(row == 24, high, jnp.where(row == 25, low, part))
        halves.append(part)
    both = jnp.concatenate(halves, axis=1)
    in_back[...] = both.astype(BF)
    padded = jnp.concatenate([both, jnp.zeros((96, 2 * hidden), F32)], axis=0)
    in_all[...] = padded.T[:, :32].astype(BF)
    middle = w_mid[...].astype(F32)
    turned = middle.T
    zero = jnp.zeros((hidden, hidden), F32)
    for source, target in ((middle, mid_all), (turned, mid_back)):
        target[...] = jnp.concatenate(
            [jnp.concatenate([source, zero], axis=1), jnp.concatenate([zero, source], axis=1)],
            axis=0,
        ).astype(BF)
    column = jnp.broadcast_to(b_mid[...], (hidden, hidden)).T
    bias_mid[...] = jnp.concatenate([column, column], axis=0)
    out = w_out[...].astype(F32)
    empty = jnp.zeros((4, hidden), F32)
    upper = jnp.concatenate([out, empty], axis=0)
    lower = jnp.concatenate([empty, out], axis=0)
    wide_out = jnp.concatenate(
        [jnp.concatenate([upper, lower], axis=1), jnp.zeros((120, 2 * hidden), F32)], axis=0
    )
    out_all[...] = wide_out[:16].astype(BF)
    out_back[...] = wide_out.T[:, :16].astype(BF)
    r8 = iota((8, LANES), 0)
    f8 = r8 & 3

    def by_field(scalars):
        return jnp.where(
            f8 == 0,
            scalars[0],
            jnp.where(f8 == 1, scalars[1], jnp.where(f8 == 2, scalars[2], scalars[3])),
        )

    rows[0] = by_field(mix_h)
    rows[1] = jnp.where(r8 < 4, mix_v[0], mix_v[1])
    rows[2] = by_field(bias_out)


def stencil(x, packs):
    east, west, north, south = neighbours(x, packs)
    diffuse = (east + west) + (north + south) - 4.0 * x
    cells = x.shape[1]
    ones = jnp.where(iota((8, cells), 0) < 2, 1.0, 0.0)
    features = jnp.concatenate([x, east - west, north - south, ones], axis=0).astype(BF)
    return diffuse, features


def write_sends(sends, kind, value, slot):
    depth = lax.axis_index("depth")

    def put(ref, part, parity):
        if parity == 0:
            ref[kind, 0] = part
        else:
            ref[kind, 0] = ref[kind, 0] + part

    for parity in range(2):

        @pl.when(lax.rem(slot, 2) == parity)
        def _():
            down, up = half_send(value, parity)
            if len(sends) == 1:
                put(sends[0], jnp.where(depth == 0, down, up), parity)
            else:
                put(sends[0], down, parity)
                put(sends[1], up, parity)


def forward_kernel(
    peers, we, sn, x_in, mask, above, below, partner, in_all, mid_all, bias_mid, out_all, rows,
    *rest
):
    pools = rest[:peers]
    x_out, first_out, second_out, feature_out, columns, lines, closure = rest[peers:]
    slot = pl.program_id(0)
    slots = pools[0].shape[0]
    x = x_in[0]
    cells = x.shape[1]
    many = cells // LANES
    packs = packs_for(slot, we, sn, pools, partner, slots)
    diffuse, features = stencil(x, packs)
    feature_out[0] = features
    bias = wide(bias_mid[...], CHUNK // LANES)
    for start in range(0, cells, CHUNK):
        span = slice(start, start + CHUNK)
        first = jnp.tanh(dot(in_all[...], feature_out[0, :, span])).astype(BF)
        first_out[0, :, span] = first
        second = jnp.tanh(dot(mid_all[...], first) + bias).astype(BF)
        second_out[0, :, span] = second
        closure[:, span] = dot(out_all[...], second)[:8]
    mh, mv, bo = (wide(rows[k], many) for k in range(3))
    vertical = pltpu.roll(x, 4, 0) + level_halo(above[0, 0], below[0, 0], lax.rem(slot, 2))
    x_new = mask[0] * (x + mh * diffuse + mv * (vertical - 2.0 * x) + (closure[...] + bo))
    x_out[0] = x_new
    columns[0] = pack_columns(x_new, x_new)
    lines[0] = pack_lines(x_new, x_new)


def backward_tail(slot, g, grad_feature, remote, rows, base, columns, lines):
    cells = g.shape[1]
    many = cells // LANES
    mh = wide(rows[0], many)
    mv = wide(rows[1], many)
    along = mh * g
    e_east = along + grad_feature[8:16]
    e_west = along - grad_feature[8:16]
    e_north = along + grad_feature[16:24]
    e_south = along - grad_feature[16:24]
    spread = mv * g
    vertical = pltpu.roll(spread, 4, 0) - 2.0 * spread
    if remote is not None:
        vertical = vertical + remote
    base[0] = (
        (g + grad_feature[0:8])
        + (pull_back(e_east, e_west, e_north, e_south) - 4.0 * along)
        + vertical
    )
    columns[0] = pack_columns(e_west, e_east)
    lines[0] = pack_lines(e_south, e_north)
    return spread


def add_terms(slot, start, second_grad, first, small, others, grad, mid, low, bias):
    hidden = mid.shape[0]
    part = dot_nt(second_grad[:hidden], first[:hidden]) + dot_nt(
        second_grad[hidden:], first[hidden:]
    )
    wings = dot_nt(small, others)
    total = grad[:, :LANES]
    for v in range(1, grad.shape[1] // LANES):
        total = total + grad[:, v * LANES : (v + 1) * LANES]

    @pl.when(slot == 0)
    def _():
        if start is None:
            mid[...] = part
            low[...] = wings
            bias[...] = total
        else:
            mid[...] = start[0][...] + part
            low[...] = start[1][...] + wings
            bias[...] = start[2][...] + total

    @pl.when(slot > 0)
    def _():
        mid[...] += part
        low[...] += wings
        bias[...] += total


def grad_rows(g):
    cells = g.shape[1]
    return jnp.concatenate([g, jnp.zeros((8, cells), F32)], axis=0).astype(BF)


def turn_kernel(
    peers, we, sn, x_in, mask, g_in, above, below, partner, in_all, mid_all, bias_mid, out_all,
    rows, out_back, mid_back, in_back, *rest
):
    pools = rest[:peers]
    (
        x_out, base, columns, lines, mid, low, bias_total,
        closure, first_all, small, trio, grad_feature,
    ) = rest[peers:]
    slot = pl.program_id(0)
    slots = pools[0].shape[0]
    x = x_in[0]
    g = g_in[0]
    cells = x.shape[1]
    many = cells // LANES
    wide2 = bias_mid.shape[0]
    packs = packs_for(slot, we, sn, pools, partner, slots)
    diffuse, features = stencil(x, packs)
    small[:32] = features
    small[32:] = grad_rows(g)
    bias = wide(bias_mid[...], CHUNK // LANES)
    for start in range(0, cells, CHUNK):
        span = slice(start, start + CHUNK)
        first = jnp.tanh(dot(in_all[...], small[:32, span]))
        first_rounded = first.astype(BF)
        first_all[:, span] = first_rounded
        second = jnp.tanh(dot(mid_all[...], first_rounded) + bias)
        second_rounded = second.astype(BF)
        trio[2 * wide2 :, span] = second_rounded
        closure[:, span] = dot(out_all[...], second_rounded)[:8]
        second_grad = dot(out_back[...], small[32:, span]) * (1.0 - second * second)
        second_grad = second_grad.astype(BF)
        trio[wide2 : 2 * wide2, span] = second_grad
        first_grad = dot(mid_back[...], second_grad) * (1.0 - first * first)
        first_grad = first_grad.astype(BF)
        trio[:wide2, span] = first_grad
        grad_feature[:, span] = dot(in_back[...], first_grad)
    add_terms(
        slot, None, trio[wide2 : 2 * wide2], first_all[...], small[...], trio[...], g, mid, low,
        bias_total,
    )
    mh, mv, bo = (wide(rows[k], many) for k in range(3))
    x_out[0] = mask[0] * (
        x + mh * diffuse + mv * (pltpu.roll(x, 4, 0) - 2.0 * x) + (closure[...] + bo)
    )
    remote = level_halo(above[0, 0], below[0, 0], lax.rem(slot, 2))
    backward_tail(slot, g, grad_feature[...], remote, rows, base, columns, lines)


def fold_terms(mid, low, bias, keep, send):
    hidden = mid.shape[0]
    top = iota((8, hidden), 0)

    def block(r, c):
        return low[8 * r : 8 * r + 8, c * hidden : (c + 1) * hidden]

    pieces = [mid[...]]
    for kind in range(3):
        pieces.append(block(kind, 0) + pltpu.roll(block(kind, 1), 4, 0))
    bias_in = block(3, 0) + block(3, 1)
    bias_mid = block(3, 2) + block(3, 3)
    pieces.append(jnp.where(top == 0, bias_in, pltpu.roll(bias_mid, 1, 0)))
    total = bias[...]
    pieces.append(
        jnp.where(
            top < 4,
            block(4, 4) + pltpu.roll(block(4, 5), 4, 0),
            total + pltpu.roll(total, 4, 0),
        )
    )
    pieces.append(jnp.zeros((8, hidden), F32))
    packed = jnp.concatenate(pieces, axis=0)
    half = packed.shape[0] // 2
    core = lax.axis_index("sub")
    keep[...] = jnp.where(core == 0, packed[:half], packed[half:])
    send[...] = jnp.where(core == 0, packed[half:], packed[:half])


def back_kernel(
    peers, we, sn, base_in, mask, x_in, partner, first_in, second_in, feature_in, rows, out_back,
    mid_back, in_back, mid_late, low_late, bias_late, *rest
):
    pools = rest[:peers]
    outs = rest[peers:]
    base, columns, lines, keep, send = outs[:5]
    sends = outs[5:-6]
    mid, low, bias_total, small, trio, grad_feature = outs[-6:]
    slot = pl.program_id(0)
    slots = pools[0].shape[0]
    cells = base_in.shape[2]
    wide2 = mid_back.shape[0]
    packs = packs_for(slot, we, sn, pools, partner, slots)
    g = mask[0] * (base_in[0] + halo_sum(packs, cells))
    small[:32] = feature_in[0]
    small[32:] = grad_rows(g)
    for start in range(0, cells, CHUNK):
        span = slice(start, start + CHUNK)
        second = second_in[0, :, span]
        first = first_in[0, :, span]
        trio[2 * wide2 :, span] = second
        second = second.astype(F32)
        first = first.astype(F32)
        second_grad = dot(out_back[...], small[32:, span]) * (1.0 - second * second)
        second_grad = second_grad.astype(BF)
        trio[wide2 : 2 * wide2, span] = second_grad
        first_grad = dot(mid_back[...], second_grad) * (1.0 - first * first)
        first_grad = first_grad.astype(BF)
        trio[:wide2, span] = first_grad
        grad_feature[:, span] = dot(in_back[...], first_grad)
    add_terms(
        slot, (mid_late, low_late, bias_late), trio[wide2 : 2 * wide2], first_in[0], small[...],
        trio[...], g, mid, low, bias_total,
    )
    spread = backward_tail(slot, g, grad_feature[...], None, rows, base, columns, lines)
    write_sends(sends, 0, x_in[0], slot)
    write_sends(sends, 1, spread, slot)

    @pl.when(slot == slots - 1)
    def _():
        fold_terms(mid, low, bias_total, keep, send)


def finish_kernel(we, sn, base_in, mask, x_in, above, below, partner, rows, *rest):
    pools = rest[:-2]
    final, initial = rest[-2:]
    slots, _, cells = base_in.shape
    many = cells // LANES
    mv = wide(rows[1], many)
    for s in range(slots):
        packs = packs_for(s, we, sn, pools, partner, slots)
        halo = level_halo(above[0, s // 2], below[0, s // 2], s % 2)
        last = x_in[s] + mask[s] * (mv * halo)
        spread = level_halo(above[1, s // 2], below[1, s // 2], s % 2)
        early = mask[s] * ((base_in[s] + spread) + halo_sum(packs, cells))
        for l in range(2):
            for f in range(4):
                r = 4 * l + f
                final[f, l, s : s + 1, :] = last[r : r + 1]
                initial[f, l, s : s + 1, :] = early[r : r + 1]


def grads_kernel(scale, low, high, w_in, b_in, w_mid, b_mid, w_out, b_out):
    hidden = w_mid.shape[0]
    packed = jnp.concatenate([low[...], high[...]], axis=0) * scale
    w_mid[...] = packed[:hidden]
    tail = packed[hidden:]
    rows = jnp.concatenate([tail[0:4], tail[8:12], tail[16:20]], axis=0)
    square = jnp.concatenate([rows, jnp.zeros((hidden - rows.shape[0], hidden), F32)], axis=0)
    w_in[...] = square.T[:, : w_in.shape[1]]
    b_in[...] = tail[24:25]
    b_mid[...] = tail[25:26]
    w_out[...] = tail[32:36]
    sums = jnp.sum(tail[36:40], axis=1, keepdims=True)
    b_out[...] = jnp.broadcast_to(sums, (4, hidden))


def vmem():
    return pl.BlockSpec(memory_space=pltpu.VMEM)


def smem():
    return pl.BlockSpec(memory_space=pltpu.SMEM)


def shape(dims, dtype=F32):
    return jax.ShapeDtypeStruct(tuple(dims), dtype)


PARAMS = pltpu.CompilerParams(vmem_limit_bytes=VMEM_BYTES)


def per_slot(dims):
    return pl.BlockSpec((1,) + tuple(dims), lambda s, we, sn: (s,) + (0,) * len(dims))


def whole(dims):
    return pl.BlockSpec(tuple(dims), lambda s, we, sn: (0,) * len(dims))


def level_block(kind, cells):
    return pl.BlockSpec((1, 1, 8, cells), lambda s, we, sn: (kind, s // 2, 0, 0))


def xor_pairs(axis, k):
    return [(i, i ^ k) for i in range(lax.axis_size(axis))]


def from_peers(packs):
    return [packs] + [
        lax.ppermute(packs, "tiles", xor_pairs("tiles", k))
        for k in range(1, lax.axis_size("tiles"))
    ]


def from_partner(lines):
    return lax.ppermute(lines, "sub", xor_pairs("sub", 1))


def from_levels(sends):
    depth = lax.axis_size("depth")
    if len(sends) == 1:
        other = lax.ppermute(sends[0], "depth", [(0, 1), (1, 0)])
        return other, other
    down = [(i, i + 1) for i in range(depth - 1)]
    return (
        lax.ppermute(sends[0], "depth", down),
        lax.ppermute(sends[1], "depth", [(j, i) for i, j in down]),
    )


def tree_sum(parts):
    while len(parts) > 1:
        parts = [parts[i] + parts[i + 1] for i in range(0, len(parts), 2)]
    return parts[0]


def sum_over(array, axis):
    return tree_sum(
        [array]
        + [lax.ppermute(array, axis, xor_pairs(axis, k)) for k in range(1, lax.axis_size(axis))]
    )


def body(
    state_init,
    cotangent,
    level_count,
    west_east,
    south_north,
    weight_in,
    bias_in,
    weight_mid,
    bias_mid,
    weight_out,
    bias_out,
    mix_horizontal,
    mix_vertical,
):
    fields, levels, slots, cells = state_init.shape
    hidden = weight_mid.shape[0]
    both = 2 * hidden
    peers = lax.axis_size("tiles")
    field = shape((slots, 8, cells))
    pack = shape((slots, 8, LANES))
    sends = [shape((2, slots // 2, 8, cells))] * (1 if lax.axis_size("depth") == 2 else 2)

    x_zero, g_late, mask, columns, lines, *levels_out = pl.pallas_call(
        prep_kernel,
        in_specs=[smem()] + [vmem()] * 3,
        out_specs=[vmem()] * (5 + len(sends)),
        out_shape=[field, field, field, pack, pack] + sends,
        compiler_params=PARAMS,
    )(mix_vertical, state_init, cotangent, level_count)
    above, below = from_levels(levels_out)
    pools = from_peers(columns)
    partner = from_partner(lines)

    in_all, in_back, mid_all, mid_back, mid_bias, out_all, out_back, rows = pl.pallas_call(
        weight_kernel,
        in_specs=[smem()] * 3 + [vmem()] * 5,
        out_specs=[vmem()] * 8,
        out_shape=[
            shape((both, 32), BF),
            shape((32, both), BF),
            shape((both, both), BF),
            shape((both, both), BF),
            shape((both, hidden)),
            shape((16, both), BF),
            shape((both, 16), BF),
            shape((3, 8, LANES)),
        ],
        compiler_params=PARAMS,
    )(
        mix_horizontal,
        mix_vertical,
        bias_out,
        weight_in,
        bias_in.reshape(1, hidden),
        weight_mid,
        bias_mid.reshape(1, hidden),
        weight_out,
    )

    one = per_slot((8, cells))
    pack_all = whole((slots, 8, LANES))
    pack_one = per_slot((8, LANES))
    forward_weights = [
        whole((both, 32)),
        whole((both, both)),
        whole((both, hidden)),
        whole((16, both)),
        whole((3, 8, LANES)),
    ]
    backward_weights = [whole((both, 16)), whole((both, both)), whole((32, both))]
    low_shape = (48, 3 * both)
    term_specs = [whole((hidden, hidden)), whole(low_shape), whole((8, LANES))]
    term_shapes = [shape((hidden, hidden)), shape(low_shape), shape((8, LANES))]

    x_one, first, second, features, columns, lines = pl.pallas_call(
        functools.partial(forward_kernel, peers),
        grid_spec=pltpu.PrefetchScalarGridSpec(
            num_scalar_prefetch=2,
            grid=(slots,),
            in_specs=[one, one, level_block(0, cells), level_block(0, cells), pack_all]
            + forward_weights
            + [pack_all] * peers,
            out_specs=[
                one,
                per_slot((both, cells)),
                per_slot((both, cells)),
                per_slot((32, cells)),
                pack_one,
                pack_one,
            ],
            scratch_shapes=[pltpu.VMEM((8, cells), F32)],
        ),
        out_shape=[
            field,
            shape((slots, both, cells), BF),
            shape((slots, both, cells), BF),
            shape((slots, 32, cells), BF),
            pack,
            pack,
        ],
        compiler_params=PARAMS,
    )(
        west_east, south_north, x_zero, mask, above, below, partner, in_all, mid_all, mid_bias,
        out_all, rows, *pools,
    )
    pools = from_peers(columns)
    partner = from_partner(lines)

    x_two, base, columns, lines, *terms = pl.pallas_call(
        functools.partial(turn_kernel, peers),
        grid_spec=pltpu.PrefetchScalarGridSpec(
            num_scalar_prefetch=2,
            grid=(slots,),
            in_specs=[one, one, one, level_block(1, cells), level_block(1, cells), pack_all]
            + forward_weights
            + backward_weights
            + [pack_all] * peers,
            out_specs=[one, one, pack_one, pack_one] + term_specs,
            scratch_shapes=[
                pltpu.VMEM((8, cells), F32),
                pltpu.VMEM((both, cells), BF),
                pltpu.VMEM((48, cells), BF),
                pltpu.VMEM((3 * both, cells), BF),
                pltpu.VMEM((32, cells), F32),
            ],
        ),
        out_shape=[field, field, pack, pack] + term_shapes,
        compiler_params=PARAMS,
    )(
        west_east, south_north, x_one, mask, g_late, above, below, partner, in_all, mid_all,
        mid_bias, out_all, rows, out_back, mid_back, in_back, *pools,
    )
    pools = from_peers(columns)
    partner = from_partner(lines)

    half = (hidden + 48) // 2
    send_block = pl.BlockSpec((2, 1, 8, cells), lambda s, we, sn: (0, s // 2, 0, 0))
    base, columns, lines, keep, give, *levels_out = pl.pallas_call(
        functools.partial(back_kernel, peers),
        grid_spec=pltpu.PrefetchScalarGridSpec(
            num_scalar_prefetch=2,
            grid=(slots,),
            in_specs=[
                one,
                one,
                one,
                pack_all,
                per_slot((both, cells)),
                per_slot((both, cells)),
                per_slot((32, cells)),
                whole((3, 8, LANES)),
            ]
            + backward_weights
            + term_specs
            + [pack_all] * peers,
            out_specs=[one, pack_one, pack_one, whole((half, hidden)), whole((half, hidden))]
            + [send_block] * len(sends),
            scratch_shapes=[
                pltpu.VMEM((hidden, hidden), F32),
                pltpu.VMEM(low_shape, F32),
                pltpu.VMEM((8, LANES), F32),
                pltpu.VMEM((48, cells), BF),
                pltpu.VMEM((3 * both, cells), BF),
                pltpu.VMEM((32, cells), F32),
            ],
        ),
        out_shape=[field, pack, pack, shape((half, hidden)), shape((half, hidden))] + sends,
        compiler_params=PARAMS,
    )(
        west_east, south_north, base, mask, x_one, partner, first, second, features, rows,
        out_back, mid_back, in_back, *terms, *pools,
    )
    total = keep + lax.ppermute(give, "sub", xor_pairs("sub", 1))
    above, below = from_levels(levels_out)
    pools = from_peers(columns)
    partner = from_partner(lines)
    total = sum_over(sum_over(total, "depth"), "tiles")

    final_state, initial_cot = pl.pallas_call(
        finish_kernel,
        in_specs=[smem(), smem()] + [vmem()] * (7 + peers),
        out_specs=[vmem()] * 2,
        out_shape=[shape(state_init.shape)] * 2,
        compiler_params=PARAMS,
    )(west_east, south_north, base, mask, x_two, above, below, partner, rows, *pools)

    other = lax.ppermute(total, "sub", xor_pairs("sub", 1))
    core = lax.axis_index("sub")
    count = (
        levels
        * lax.axis_size("depth")
        * slots
        * lax.axis_size("tiles")
        * cells
        * lax.axis_size("sub")
    )
    low = jnp.where(core == 0, total, other)
    high = jnp.where(core == 0, other, total)
    w_in, b_in, w_mid, b_mid, w_out, b_out = pl.pallas_call(
        functools.partial(grads_kernel, 1.0 / math.sqrt(count)),
        in_specs=[vmem()] * 2,
        out_specs=[vmem()] * 6,
        out_shape=[
            shape(weight_in.shape),
            shape((1, hidden)),
            shape((hidden, hidden)),
            shape((1, hidden)),
            shape(weight_out.shape),
            shape((4, hidden)),
        ],
        compiler_params=PARAMS,
    )(low, high)
    return (
        final_state,
        initial_cot,
        w_in,
        b_in.reshape(hidden),
        w_mid,
        b_mid.reshape(hidden),
        w_out,
        b_out[:, 0],
    )


def solution(mesh):
    return jax.shard_map(
        body,
        mesh=mesh,
        in_specs=(
            P("groups", "depth", "tiles", "sub"),
            P("groups", "depth", "tiles", "sub"),
            P("tiles", "sub"),
            P("tiles", None),
            P("tiles", None),
            P(),
            P(),
            P(),
            P(),
            P(),
            P(),
            P(),
            P("depth"),
        ),
        out_specs=(
            P("groups", "depth", "tiles", "sub"),
            P("groups", "depth", "tiles", "sub"),
            P("groups", None),
            P("groups"),
            P("groups", None),
            P("groups"),
            P("groups", None),
            P("groups"),
        ),
        check_vma=False,
    )
```

profile of v0, /device:TPU:0, one launch (start us, length us, event | category | flops | bytes accessed | tf_op | source)
XLA Modules:
  0.0 129.8 jit_solution(17921220124288024644)
XLA Ops:
  0.6 0.9 copy-done
  1.6 0.9 copy-done.1
  3.9 0.8 shard_map.188
  4.8 3.0 %collective-permute-start = (f32[2,2,8,2048]{3,2,1,0:T(8,128)S(1)}, f32[2,2,8,2048]{3,2,1,0:T(8,128)S(1)}, u32[]{:S(2)}, u32[]{:S(2)}) collective-permute-start(f32[2,2,8,2048]{3,2,1,0:T(8,128)S(1)} %get-tuple-element.51), channel_id=1, source_target_pairs={{0,2},{2,0},{1,3},{3,1},{4,6},{6,4},{5,7},{7,5},{8,10},{10,8},{9,1... | collective-permute-start | bytes 786440 | tf_op jit(solution)/shard_map/ppermute | solution.py:564
  7.8 1.6 %collective-permute-start.2 = (f32[4,8,128]{2,1,0:T(8,128)S(1)}, f32[4,8,128]{2,1,0:T(8,128)S(1)}, u32[]{:S(2)}, u32[]{:S(2)}) collective-permute-start(f32[4,8,128]{2,1,0:T(8,128)S(1)} %get-tuple-element.58.rest_0_), channel_id=1, source_target_pairs={{0,4},{4,0},{8,12},{12,8},{1,5},{5,1},{9,13},{13,9},{2,6},{6,2},{1... | collective-permute-start | bytes 49160 | tf_op jit(solution)/shard_map/ppermute | solution.py:552
  9.4 2.6 %collective-permute-start.3 = (f32[4,8,128]{2,1,0:T(8,128)S(1)}, f32[4,8,128]{2,1,0:T(8,128)S(1)}, u32[]{:S(2)}, u32[]{:S(2)}) collective-permute-start(f32[4,8,128]{2,1,0:T(8,128)S(1)} %get-tuple-element.58.rest_0_), channel_id=1, source_target_pairs={{0,8},{4,12},{8,0},{12,4},{1,9},{5,13},{9,1},{13,5},{2,10},{6,14},... | collective-permute-start | bytes 49160 | tf_op jit(solution)/shard_map/ppermute | solution.py:552
  19.2 0.8 shard_map.189
  20.1 14.1 %shard_map.190 = (f32[4,8,2048]{2,1,0:T(8,128)S(1)}, bf16[4,256,2048]{2,1,0:T(8,128)(2,1)S(1)}, bf16[4,256,2048]{2,1,0:T(8,128)(2,1)S(1)}, bf16[4,32,2048]{2,1,0...) custom-call(s32[4,2]{1,0:T(4,128)S(1)} %copy.38.we, s32[4,2]{1,0:T(4,128)S(1)} %copy.39.sn, ...), custom_call_target="tpu_custom_call" | custom-call | tf_op jit(solution)/shard_map/pallas_call | solution.py:661
  34.9 3.5 %collective-permute-start.7 = (f32[4,8,128]{2,1,0:T(8,128)S(1)}, f32[4,8,128]{2,1,0:T(8,128)S(1)}, u32[]{:S(2)}, u32[]{:S(2)}) collective-permute-start(f32[4,8,128]{2,1,0:T(8,128)S(1)} %get-tuple-element.65.rest_0_), channel_id=1, source_target_pairs={{0,8},{4,12},{8,0},{12,4},{1,9},{5,13},{9,1},{13,5},{2,10},{6,14},... | collective-permute-start | bytes 49160 | tf_op jit(solution)/shard_map/ppermute | solution.py:552
  38.7 1.5 %collective-permute-done.7.rest_2_ = f32[4,8,128]{2,1,0:T(8,128)S(1)} collective-permute-done((f32[4,8,128]{2,1,0:T(8,128)S(1)}, f32[4,8,128]{2,1,0:T(8,128)S(1)}, u32[]{:S(2)}, u32[]{:S(2)}) %collective-permute-start.7) | collective-permute-done | bytes 16416 | tf_op jit(solution)/shard_map/ppermute | solution.py:552
  40.1 3.8 %collective-permute-done.8.rest_3_ = f32[4,8,128]{2,1,0:T(8,128)S(1)} collective-permute-done((f32[4,8,128]{2,1,0:T(8,128)S(1)}, f32[4,8,128]{2,1,0:T(8,128)S(1)}, u32[]{:S(2)}, u32[]{:S(2)}) %collective-permute-start.8) | collective-permute-done | bytes 16416 | tf_op jit(solution)/shard_map/ppermute | solution.py:552
  44.0 30.9 %shard_map.191 = (f32[4,8,2048]{2,1,0:T(8,128)S(1)}, f32[4,8,2048]{2,1,0:T(8,128)S(1)}, f32[4,8,128]{2,1,0:T(8,128)S(1)}, f32[4,8,128]{2,1,0:T(8,128)S(1)}, f32[...) custom-call(s32[4,2]{1,0:T(4,128)S(1)} %copy.38.we, s32[4,2]{1,0:T(4,128)S(1)} %copy.39.sn, ...), custom_call_target="tpu_custom_call" | custom-call | tf_op jit(solution)/shard_map/pallas_call | solution.py:695
  75.8 3.6 %collective-permute-start.12 = (f32[4,8,128]{2,1,0:T(8,128)S(1)}, f32[4,8,128]{2,1,0:T(8,128)S(1)}, u32[]{:S(2)}, u32[]{:S(2)}) collective-permute-start(f32[4,8,128]{2,1,0:T(8,128)S(1)} %get-tuple-element.74.rest_0_), channel_id=1, source_target_pairs={{0,12},{4,8},{8,4},{12,0},{1,13},{5,9},{9,5},{13,1},{2,14},{6,10},... | collective-permute-start | bytes 49160 | tf_op jit(solution)/shard_map/ppermute | solution.py:552
  79.7 1.6 %collective-permute-done.12.rest_3_ = f32[4,8,128]{2,1,0:T(8,128)S(1)} collective-permute-done((f32[4,8,128]{2,1,0:T(8,128)S(1)}, f32[4,8,128]{2,1,0:T(8,128)S(1)}, u32[]{:S(2)}, u32[]{:S(2)}) %collective-permute-start.12) | collective-permute-done | bytes 16416 | tf_op jit(solution)/shard_map/ppermute | solution.py:552
  81.3 18.9 %shard_map.192 = (f32[4,8,2048]{2,1,0:T(8,128)S(1)}, f32[4,8,128]{2,1,0:T(8,128)S(1)}, f32[4,8,128]{2,1,0:T(8,128)S(1)}, f32[88,128]{1,0:T(8,128)S(1)}, f32[88,1...) custom-call(s32[4,2]{1,0:T(4,128)S(1)} %copy.38.we, s32[4,2]{1,0:T(4,128)S(1)} %copy.39.sn, ...), custom_call_target="tpu_custom_call" | custom-call | tf_op jit(solution)/shard_map/pallas_call | solution.py:724
  100.3 1.2 collective-permute-done.18
  102.1 3.6 %collective-permute-done.19 = f32[88,128]{1,0:T(8,128)S(1)} collective-permute-done((f32[88,128]{1,0:T(8,128)S(1)}, f32[88,128]{1,0:T(8,128)S(1)}, u32[]{:S(2)}, u32[]{:S(2)}) %collective-permute-start.19) | collective-permute-done | bytes 45088 | tf_op jit(solution)/shard_map/ppermute | solution.py:582
  106.1 3.8 %collective-permute-start.21 = (f32[88,128]{1,0:T(8,128)S(1)}, f32[88,128]{1,0:T(8,128)S(1)}, u32[]{:S(2)}, u32[]{:S(2)}) collective-permute-start(f32[88,128]{1,0:T(8,128)S(1)} %add.16), channel_id=1, source_target_pairs={{0,8},{4,12},{8,0},{12,4},{1,9},{5,13},{9,1},{13,5},{2,10},{6,14},... | collective-permute-start | bytes 135176 | tf_op jit(solution)/shard_map/ppermute | solution.py:582
  110.1 2.3 %collective-permute-done.21 = f32[88,128]{1,0:T(8,128)S(1)} collective-permute-done((f32[88,128]{1,0:T(8,128)S(1)}, f32[88,128]{1,0:T(8,128)S(1)}, u32[]{:S(2)}, u32[]{:S(2)}) %collective-permute-start.21) | collective-permute-done | bytes 45088 | tf_op jit(solution)/shard_map/ppermute | solution.py:582
  112.4 3.3 %collective-permute-done.22 = f32[88,128]{1,0:T(8,128)S(1)} collective-permute-done((f32[88,128]{1,0:T(8,128)S(1)}, f32[88,128]{1,0:T(8,128)S(1)}, u32[]{:S(2)}, u32[]{:S(2)}) %collective-permute-start.22) | collective-permute-done | bytes 45088 | tf_op jit(solution)/shard_map/ppermute | solution.py:582
  115.9 1.0 collective-permute-start.16
  116.9 3.3 %collective-permute-start.17 = (f32[4,8,128]{2,1,0:T(8,128)S(1)}, f32[4,8,128]{2,1,0:T(8,128)S(1)}, u32[]{:S(2)}, u32[]{:S(2)}) collective-permute-start(f32[4,8,128]{2,1,0:T(8,128)S(1)} %get-tuple-element.79.rest_0_), channel_id=1, source_target_pairs={{0,12},{4,8},{8,4},{12,0},{1,13},{5,9},{9,5},{13,1},{2,14},{6,10},... | collective-permute-start | bytes 49160 | tf_op jit(solution)/shard_map/ppermute | solution.py:552
  122.8 5.3 %collective-permute-done.13.above.below = f32[2,2,8,2048]{3,2,1,0:T(8,128)S(1)} collective-permute-done((f32[2,2,8,2048]{3,2,1,0:T(8,128)S(1)}, f32[2,2,8,2048]{3,2,1,0:T(8,128)S(1)}, u32[]{:S(2)}, u32[]{:S(2)}) %collective-permute-start.13) | collective-permute-done | bytes 262176 | tf_op jit(solution)/shard_map/ppermute | solution.py:564
  128.1 1.7 %shard_map.193 = (f32[4,2,4,2048]{3,2,1,0:T(4,128)}, f32[4,2,4,2048]{3,2,1,0:T(4,128)}) custom-call(s32[4,2]{1,0:T(4,128)S(1)} %copy.38.we, s32[4,2]{1,0:T(4,128)S(1)} %copy.39.sn, f32[4,8,2048]{2,1,0:T(8,128)S(1)} %get-tuple-element.75.base_in, f32[4,8,2048]{2,1,0:T(8,128)S(1)} %get-tuple-element.50.mask, f32[4,8,2048]{2,1,0:T(8,128)S(1)} %get-tuple-element.76.x_in, ...), custom_call_target="tpu_custom_call" | custom-call | tf_op jit(solution)/shard_map/pallas_call | solution.py:765
  (62 shorter events, 14.8 us)
Async XLA Ops:
  4.8 15.3 %collective-permute-start = (f32[2,2,8,2048]{3,2,1,0:T(8,128)S(1)}, f32[2,2,8,2048]{3,2,1,0:T(8,128)S(1)}, u32[]{:S(2)}, u32[]{:S(2)}) collective-permute-start(f32[2,2,8,2048]{3,2,1,0:T(8,128)S(1)} %get-tuple-element.51), channel_id=1, source_target_pairs={{0,2},{2,0},{1,3},{3,1},{4,6},{6,4},{5,7},{7,5},{8,10},{10,8},{9,1... | collective-permute-start | bytes 786440 | tf_op jit(solution)/shard_map/ppermute | solution.py:564
  7.8 12.3 %collective-permute-start.2 = (f32[4,8,128]{2,1,0:T(8,128)S(1)}, f32[4,8,128]{2,1,0:T(8,128)S(1)}, u32[]{:S(2)}, u32[]{:S(2)}) collective-permute-start(f32[4,8,128]{2,1,0:T(8,128)S(1)} %get-tuple-element.58.rest_0_), channel_id=1, source_target_pairs={{0,4},{4,0},{8,12},{12,8},{1,5},{5,1},{9,13},{13,9},{2,6},{6,2},{1... | collective-permute-start | bytes 49160 | tf_op jit(solution)/shard_map/ppermute | solution.py:552
  9.4 10.7 %collective-permute-start.3 = (f32[4,8,128]{2,1,0:T(8,128)S(1)}, f32[4,8,128]{2,1,0:T(8,128)S(1)}, u32[]{:S(2)}, u32[]{:S(2)}) collective-permute-start(f32[4,8,128]{2,1,0:T(8,128)S(1)} %get-tuple-element.58.rest_0_), channel_id=1, source_target_pairs={{0,8},{4,12},{8,0},{12,4},{1,9},{5,13},{9,1},{13,5},{2,10},{6,14},... | collective-permute-start | bytes 49160 | tf_op jit(solution)/shard_map/ppermute | solution.py:552
  11.9 8.1 %collective-permute-start.4 = (f32[4,8,128]{2,1,0:T(8,128)S(1)}, f32[4,8,128]{2,1,0:T(8,128)S(1)}, u32[]{:S(2)}, u32[]{:S(2)}) collective-permute-start(f32[4,8,128]{2,1,0:T(8,128)S(1)} %get-tuple-element.58.rest_0_), channel_id=1, source_target_pairs={{0,12},{4,8},{8,4},{12,0},{1,13},{5,9},{9,5},{13,1},{2,14},{6,10},... | collective-permute-start | bytes 49160 | tf_op jit(solution)/shard_map/ppermute | solution.py:552
  12.2 7.9 %collective-permute-start.1 = (f32[4,8,128]{2,1,0:T(8,128)S(1)}, f32[4,8,128]{2,1,0:T(8,128)S(1)}, u32[]{:S(2)}, u32[]{:S(2)}) collective-permute-start(f32[4,8,128]{2,1,0:T(8,128)S(1)} %get-tuple-element.52), channel_id=1, source_target_pairs={{0,1},{1,0},{2,3},{3,2},{4,5},{5,4},{6,7},{7,6},{8,9},{9,8},{10,11... | collective-permute-start | bytes 49160 | tf_op jit(solution)/shard_map/ppermute | solution.py:558
  34.2 4.4 %collective-permute-start.6 = (f32[4,8,128]{2,1,0:T(8,128)S(1)}, f32[4,8,128]{2,1,0:T(8,128)S(1)}, u32[]{:S(2)}, u32[]{:S(2)}) collective-permute-start(f32[4,8,128]{2,1,0:T(8,128)S(1)} %get-tuple-element.65.rest_0_), channel_id=1, source_target_pairs={{0,4},{4,0},{8,12},{12,8},{1,5},{5,1},{9,13},{13,9},{2,6},{6,2},{1... | collective-permute-start | bytes 49160 | tf_op jit(solution)/shard_map/ppermute | solution.py:552
  34.9 5.2 %collective-permute-start.7 = (f32[4,8,128]{2,1,0:T(8,128)S(1)}, f32[4,8,128]{2,1,0:T(8,128)S(1)}, u32[]{:S(2)}, u32[]{:S(2)}) collective-permute-start(f32[4,8,128]{2,1,0:T(8,128)S(1)} %get-tuple-element.65.rest_0_), channel_id=1, source_target_pairs={{0,8},{4,12},{8,0},{12,4},{1,9},{5,13},{9,1},{13,5},{2,10},{6,14},... | collective-permute-start | bytes 49160 | tf_op jit(solution)/shard_map/ppermute | solution.py:552
  38.4 5.5 %collective-permute-start.8 = (f32[4,8,128]{2,1,0:T(8,128)S(1)}, f32[4,8,128]{2,1,0:T(8,128)S(1)}, u32[]{:S(2)}, u32[]{:S(2)}) collective-permute-start(f32[4,8,128]{2,1,0:T(8,128)S(1)} %get-tuple-element.65.rest_0_), channel_id=1, source_target_pairs={{0,12},{4,8},{8,4},{12,0},{1,13},{5,9},{9,5},{13,1},{2,14},{6,10},... | collective-permute-start | bytes 49160 | tf_op jit(solution)/shard_map/ppermute | solution.py:552
  38.6 5.3 %collective-permute-start.5 = (f32[4,8,128]{2,1,0:T(8,128)S(1)}, f32[4,8,128]{2,1,0:T(8,128)S(1)}, u32[]{:S(2)}, u32[]{:S(2)}) collective-permute-start(f32[4,8,128]{2,1,0:T(8,128)S(1)} %get-tuple-element.61), channel_id=1, source_target_pairs={{0,1},{1,0},{2,3},{3,2},{4,5},{5,4},{6,7},{7,6},{8,9},{9,8},{10,11... | collective-permute-start | bytes 49160 | tf_op jit(solution)/shard_map/ppermute | solution.py:558
  74.9 4.5 %collective-permute-start.10 = (f32[4,8,128]{2,1,0:T(8,128)S(1)}, f32[4,8,128]{2,1,0:T(8,128)S(1)}, u32[]{:S(2)}, u32[]{:S(2)}) collective-permute-start(f32[4,8,128]{2,1,0:T(8,128)S(1)} %get-tuple-element.74.rest_0_), channel_id=1, source_target_pairs={{0,4},{4,0},{8,12},{12,8},{1,5},{5,1},{9,13},{13,9},{2,6},{6,2},{1... | collective-permute-start | bytes 49160 | tf_op jit(solution)/shard_map/ppermute | solution.py:552
  75.0 4.7 %collective-permute-start.11 = (f32[4,8,128]{2,1,0:T(8,128)S(1)}, f32[4,8,128]{2,1,0:T(8,128)S(1)}, u32[]{:S(2)}, u32[]{:S(2)}) collective-permute-start(f32[4,8,128]{2,1,0:T(8,128)S(1)} %get-tuple-element.74.rest_0_), channel_id=1, source_target_pairs={{0,8},{4,12},{8,0},{12,4},{1,9},{5,13},{9,1},{13,5},{2,10},{6,14},... | collective-permute-start | bytes 49160 | tf_op jit(solution)/shard_map/ppermute | solution.py:552
  75.8 5.5 %collective-permute-start.12 = (f32[4,8,128]{2,1,0:T(8,128)S(1)}, f32[4,8,128]{2,1,0:T(8,128)S(1)}, u32[]{:S(2)}, u32[]{:S(2)}) collective-permute-start(f32[4,8,128]{2,1,0:T(8,128)S(1)} %get-tuple-element.74.rest_0_), channel_id=1, source_target_pairs={{0,12},{4,8},{8,4},{12,0},{1,13},{5,9},{9,5},{13,1},{2,14},{6,10},... | collective-permute-start | bytes 49160 | tf_op jit(solution)/shard_map/ppermute | solution.py:552
  79.4 1.9 %collective-permute-start.9 = (f32[4,8,128]{2,1,0:T(8,128)S(1)}, f32[4,8,128]{2,1,0:T(8,128)S(1)}, u32[]{:S(2)}, u32[]{:S(2)}) collective-permute-start(f32[4,8,128]{2,1,0:T(8,128)S(1)} %get-tuple-element.67), channel_id=1, source_target_pairs={{0,1},{1,0},{2,3},{3,2},{4,5},{5,4},{6,7},{7,6},{8,9},{9,8},{10,11... | collective-permute-start | bytes 49160 | tf_op jit(solution)/shard_map/ppermute | solution.py:558
  100.2 1.3 collective-permute-start.18
  101.5 4.1 %collective-permute-start.19 = (f32[88,128]{1,0:T(8,128)S(1)}, f32[88,128]{1,0:T(8,128)S(1)}, u32[]{:S(2)}, u32[]{:S(2)}) collective-permute-start(f32[88,128]{1,0:T(8,128)S(1)} %add.15), channel_id=1, source_target_pairs={{0,2},{2,0},{1,3},{3,1},{4,6},{6,4},{5,7},{7,5},{8,10},{10,8},{9,1... | collective-permute-start | bytes 135176 | tf_op jit(solution)/shard_map/ppermute | solution.py:582
  105.7 4.5 %collective-permute-start.20 = (f32[88,128]{1,0:T(8,128)S(1)}, f32[88,128]{1,0:T(8,128)S(1)}, u32[]{:S(2)}, u32[]{:S(2)}) collective-permute-start(f32[88,128]{1,0:T(8,128)S(1)} %add.16), channel_id=1, source_target_pairs={{0,4},{4,0},{8,12},{12,8},{1,5},{5,1},{9,13},{13,9},{2,6},{6,2},{1... | collective-permute-start | bytes 135176 | tf_op jit(solution)/shard_map/ppermute | solution.py:582
  106.1 6.3 %collective-permute-start.21 = (f32[88,128]{1,0:T(8,128)S(1)}, f32[88,128]{1,0:T(8,128)S(1)}, u32[]{:S(2)}, u32[]{:S(2)}) collective-permute-start(f32[88,128]{1,0:T(8,128)S(1)} %add.16), channel_id=1, source_target_pairs={{0,8},{4,12},{8,0},{12,4},{1,9},{5,13},{9,1},{13,5},{2,10},{6,14},... | collective-permute-start | bytes 135176 | tf_op jit(solution)/shard_map/ppermute | solution.py:582
  109.9 5.8 %collective-permute-start.22 = (f32[88,128]{1,0:T(8,128)S(1)}, f32[88,128]{1,0:T(8,128)S(1)}, u32[]{:S(2)}, u32[]{:S(2)}) collective-permute-start(f32[88,128]{1,0:T(8,128)S(1)} %add.16), channel_id=1, source_target_pairs={{0,12},{4,8},{8,4},{12,0},{1,13},{5,9},{9,5},{13,1},{2,14},{6,10},... | collective-permute-start | bytes 135176 | tf_op jit(solution)/shard_map/ppermute | solution.py:582
  115.7 5.1 %collective-permute-start.23 = (f32[88,128]{1,0:T(8,128)S(1)}, f32[88,128]{1,0:T(8,128)S(1)}, u32[]{:S(2)}, u32[]{:S(2)}) collective-permute-start(f32[88,128]{1,0:T(8,128)S(1)} %add_add_fusion), channel_id=1, source_target_pairs={{0,1},{1,0},{2,3},{3,2},{4,5},{5,4},{6,7},{7,6},{8,9},{9,8},{10,11... | collective-permute-start | bytes 135176 | tf_op jit(solution)/shard_map/ppermute | solution.py:773
  115.8 7.0 %collective-permute-start.15 = (f32[4,8,128]{2,1,0:T(8,128)S(1)}, f32[4,8,128]{2,1,0:T(8,128)S(1)}, u32[]{:S(2)}, u32[]{:S(2)}) collective-permute-start(f32[4,8,128]{2,1,0:T(8,128)S(1)} %get-tuple-element.79.rest_0_), channel_id=1, source_target_pairs={{0,4},{4,0},{8,12},{12,8},{1,5},{5,1},{9,13},{13,9},{2,6},{6,2},{1... | collective-permute-start | bytes 49160 | tf_op jit(solution)/shard_map/ppermute | solution.py:552
  115.9 6.9 %collective-permute-start.16 = (f32[4,8,128]{2,1,0:T(8,128)S(1)}, f32[4,8,128]{2,1,0:T(8,128)S(1)}, u32[]{:S(2)}, u32[]{:S(2)}) collective-permute-start(f32[4,8,128]{2,1,0:T(8,128)S(1)} %get-tuple-element.79.rest_0_), channel_id=1, source_target_pairs={{0,8},{4,12},{8,0},{12,4},{1,9},{5,13},{9,1},{13,5},{2,10},{6,14},... | collective-permute-start | bytes 49160 | tf_op jit(solution)/shard_map/ppermute | solution.py:552
  116.9 5.9 %collective-permute-start.17 = (f32[4,8,128]{2,1,0:T(8,128)S(1)}, f32[4,8,128]{2,1,0:T(8,128)S(1)}, u32[]{:S(2)}, u32[]{:S(2)}) collective-permute-start(f32[4,8,128]{2,1,0:T(8,128)S(1)} %get-tuple-element.79.rest_0_), channel_id=1, source_target_pairs={{0,12},{4,8},{8,4},{12,0},{1,13},{5,9},{9,5},{13,1},{2,14},{6,10},... | collective-permute-start | bytes 49160 | tf_op jit(solution)/shard_map/ppermute | solution.py:552
  120.3 7.8 %collective-permute-start.13 = (f32[2,2,8,2048]{3,2,1,0:T(8,128)S(1)}, f32[2,2,8,2048]{3,2,1,0:T(8,128)S(1)}, u32[]{:S(2)}, u32[]{:S(2)}) collective-permute-start(f32[2,2,8,2048]{3,2,1,0:T(8,128)S(1)} %get-tuple-element.77), channel_id=1, source_target_pairs={{0,2},{2,0},{1,3},{3,1},{4,6},{6,4},{5,7},{7,5},{8,10},{10,8},{9,1... | collective-permute-start | bytes 786440 | tf_op jit(solution)/shard_map/ppermute | solution.py:564
  120.8 2.0 %collective-permute-start.14 = (f32[4,8,128]{2,1,0:T(8,128)S(1)}, f32[4,8,128]{2,1,0:T(8,128)S(1)}, u32[]{:S(2)}, u32[]{:S(2)}) collective-permute-start(f32[4,8,128]{2,1,0:T(8,128)S(1)} %get-tuple-element.78), channel_id=1, source_target_pairs={{0,1},{1,0},{2,3},{3,2},{4,5},{5,4},{6,7},{7,6},{8,9},{9,8},{10,11... | collective-permute-start | bytes 49160 | tf_op jit(solution)/shard_map/ppermute | solution.py:558
  (11 other events, 8.0 us)
where the time goes:
time: 130 us
  Pallas kernels  68 us (52%)
  starting transfers between devices  26.4 us (20%)
  waiting for transfers between devices  22.9 us (18%)
  local copies, waits for them, and re-layouts  11.7 us (9%)
    pallas_call x1, Pallas kernels, body(): pl.pallas_call(functools.partial(turn_kernel, peers), grid_spec=pltpu.Pre...  30.9 us
    pallas_call x1, Pallas kernels, body(): pl.pallas_call(functools.partial(back_kernel, peers), grid_spec=pltpu.Pre...  18.9 us
    ppermute x12, starting transfers between devices, from_peers(): lax.ppermute(packs, 'tiles', xor_pairs('tiles', k))  17.7 us
    pallas_call x1, Pallas kernels, body(): pl.pallas_call(functools.partial(forward_kernel, peers), grid_spec=pltpu....  14.1 us
    unnamed x26, local copies, waits for them, and re-layouts  11 us
    ppermute x4, waiting for transfers between devices, sum_over(): lax.ppermute(array, axis, xor_pairs(axis, k))  9.17 us
    ppermute x12, waiting for transfers between devices, from_peers(): lax.ppermute(packs, 'tiles', xor_pairs('tiles', k))  7.26 us
    ppermute x2, waiting for transfers between devices, from_levels(): other = lax.ppermute(sends[0], 'depth', [(0, 1), (1, 0)])  5.29 us
  transfers between devices with their start and end apart: 24, of which 9 were waited for; matrix products, arithmetic and copies ran while one was open for 3% of the time, Pallas kernels for 1%

commit v1 on v0

v1 whole, which is shorter than its diff:
```python
import functools
import math

import jax
import jax.numpy as jnp
from jax import lax
from jax.experimental import pallas as pl
from jax.experimental.pallas import tpu as pltpu
from jax.sharding import PartitionSpec as P

TCOL = 64
LANES = 128
CHUNK = 2048
BF = jnp.bfloat16
F32 = jnp.float32
VMEM_BYTES = 16 * 1024 * 1024
NT = (((1,), (1,)), ((), ()))


def dot(left, right):
    return jnp.dot(left, right, preferred_element_type=F32)


def dot_nt(left, right):
    return lax.dot_general(left, right, NT, preferred_element_type=F32)


def iota(shape, axis):
    return lax.broadcasted_iota(jnp.int32, shape, axis)


def wide(block, copies):
    return jnp.concatenate([block] * copies, axis=1)


def pack_columns(first, last):
    place = iota((8, LANES), 1) & 63
    packed = jnp.zeros((8, LANES), F32)
    for v in range(first.shape[1] // LANES):
        span = slice(v * LANES, (v + 1) * LANES)
        low = pltpu.roll(first[:, span], v, 1) if v else first[:, span]
        high = pltpu.roll(last[:, span], v + 17, 1)
        packed = jnp.where(place == v, low, packed)
        packed = jnp.where(place == 16 + v, high, packed)
    return packed


def pack_lines(first, last):
    cells = first.shape[1]
    lane = iota((8, LANES), 1)
    return jnp.where(lane < TCOL, first[:, :LANES], last[:, cells - LANES :])


def halo_fields(codes, pools, partner, slots, cells):
    lane = iota((8, LANES), 1)
    count = cells // LANES
    east, west, lines = [], [], []

    def chosen(code, blocks):
        found = jnp.zeros((8, LANES), F32)
        for k, block in enumerate(blocks):
            found = jnp.where(code == k, block, found)
        return found

    column_blocks = [pool[s] for pool in pools for s in range(slots)]
    line_blocks = [partner[s] for s in range(slots)]
    for s in range(slots):
        west_pack = chosen(codes[0, s], column_blocks)
        east_pack = chosen(codes[1, s], column_blocks)
        south = pltpu.roll(chosen(codes[2, s], line_blocks), TCOL, 1)
        north = pltpu.roll(chosen(codes[3, s], line_blocks), TCOL, 1)
        east += [pltpu.roll(east_pack, 63 - v, 1) for v in range(count)]
        west += [pltpu.roll(west_pack, 48 - v, 1) for v in range(count)]
        lines += [jnp.where(lane < TCOL, south, north)] * count
    return tuple(jnp.concatenate(part, axis=1) for part in (east, west, lines))


def places(shape, cells):
    lane = iota(shape, 1) & (cells - 1)
    column = lane & (TCOL - 1)
    return column == TCOL - 1, column == 0, lane >= cells - TCOL, lane < TCOL


def neighbours(x, halos, cells):
    total = x.shape[1]
    east_halo, west_halo, lines = halos
    at_east, at_west, at_north, at_south = places(x.shape, cells)
    east = jnp.where(at_east, east_halo, pltpu.roll(x, total - 1, 1))
    west = jnp.where(at_west, west_halo, pltpu.roll(x, 1, 1))
    north = jnp.where(at_north, lines, pltpu.roll(x, total - TCOL, 1))
    south = jnp.where(at_south, lines, pltpu.roll(x, TCOL, 1))
    return east, west, north, south


def halo_sum(halos, cells):
    east_halo, west_halo, lines = halos
    at_east, at_west, at_north, at_south = places(lines.shape, cells)
    columns = jnp.where(at_east, east_halo, jnp.where(at_west, west_halo, 0.0))
    return columns + jnp.where(at_north | at_south, lines, 0.0)


def pull_back(e_east, e_west, e_north, e_south, cells):
    total = e_east.shape[1]
    at_east, at_west, at_north, at_south = places(e_east.shape, cells)
    return (
        jnp.where(at_west, 0.0, pltpu.roll(e_east, 1, 1))
        + jnp.where(at_east, 0.0, pltpu.roll(e_west, total - 1, 1))
    ) + (
        jnp.where(at_south, 0.0, pltpu.roll(e_north, TCOL, 1))
        + jnp.where(at_north, 0.0, pltpu.roll(e_south, total - TCOL, 1))
    )


def write_edges(columns, lines, first_column, last_column, first_line, last_line):
    slots = columns.shape[0]
    cells = first_column.shape[1] // slots
    for s in range(slots):
        span = slice(s * cells, (s + 1) * cells)
        columns[s] = pack_columns(first_column[:, span], last_column[:, span])
        lines[s] = pack_lines(first_line[:, span], last_line[:, span])


def write_sends(sends, kind, x, cells):
    depth = lax.axis_index("depth")
    top = iota((8, cells), 0) < 4
    for i in range(x.shape[1] // (2 * cells)):
        even = x[:, 2 * i * cells : (2 * i + 1) * cells]
        odd = x[:, (2 * i + 1) * cells : (2 * i + 2) * cells]
        down = jnp.where(top, pltpu.roll(even, 4, 0), odd)
        up = jnp.where(top, even, pltpu.roll(odd, 4, 0))
        if len(sends) == 1:
            sends[0][kind, i] = jnp.where(depth == 0, down, up)
        else:
            sends[0][kind, i] = down
            sends[1][kind, i] = up


def level_halo(above_ref, below_ref, kind):
    depth = lax.axis_index("depth")
    last = lax.axis_size("depth") - 1
    parts = []
    for i in range(above_ref.shape[1]):
        above = jnp.where(depth > 0, above_ref[kind, i], 0.0)
        below = jnp.where(depth < last, below_ref[kind, i], 0.0)
        top = iota(above.shape, 0) < 4
        parts.append(jnp.where(top, above, pltpu.roll(below, 4, 0)))
        parts.append(jnp.where(top, pltpu.roll(above, 4, 0), below))
    return jnp.concatenate(parts, axis=1)


def fetch(pairs, sems):
    copies = [
        pltpu.make_async_copy(source, target, sems.at[i])
        for i, (source, target) in enumerate(pairs)
    ]
    for copy in copies:
        copy.start()
    for copy in copies:
        copy.wait()


def prep_kernel(sent, mix_v_in, state_in, cot_in, count_in, *rest):
    x_out, g_out, mask_out, columns, lines = rest[:5]
    sends = rest[5 : 5 + sent]
    mix_v, state, cot, count, sems = rest[5 + sent :]
    fetch(
        [(mix_v_in, mix_v), (count_in, count), (state_in, state), (cot_in, cot)], sems
    )
    slots = state.shape[2]
    cells = state.shape[3]
    depth = lax.axis_index("depth")
    for s in range(slots):
        span = slice(s * cells, (s + 1) * cells)
        for l in range(2):
            for f in range(4):
                r = 4 * l + f
                x_out[r : r + 1, span] = state[f, l, s : s + 1, :]
                g_out[r : r + 1, span] = cot[f, l, s : s + 1, :]
    deep = jnp.concatenate(
        [jnp.broadcast_to(count[s : s + 1, :], (8, cells)) for s in range(slots)], axis=1
    )
    upper = iota(deep.shape, 0) < 4
    mask = jnp.where(2 * depth + jnp.where(upper, 0, 1) < deep, 1.0, 0.0)
    x = mask * x_out[...]
    g = mask * g_out[...]
    mask_out[...] = mask
    x_out[...] = x
    g_out[...] = g
    write_edges(columns, lines, x, x, x, x)
    write_sends(sends, 0, x, cells)
    write_sends(sends, 1, jnp.where(upper, mix_v[0], mix_v[1]) * g, cells)


def weight_kernel(
    mix_h_in, mix_v_in, bias_out_in, we_in, sn_in, w_in_in, b_in_in, w_mid_in, b_mid_in, w_out_in,
    in_all, in_back, mid_all, mid_back, bias_mid, out_all, out_back, rows, codes,
    mix_h, mix_v, bias_out, we, sn, w_in, b_in, w_mid, b_mid, w_out, sems
):
    fetch(
        [
            (mix_h_in, mix_h), (mix_v_in, mix_v), (bias_out_in, bias_out), (we_in, we),
            (sn_in, sn), (w_in_in, w_in), (b_in_in, b_in), (w_mid_in, w_mid), (b_mid_in, b_mid),
            (w_out_in, w_out),
        ],
        sems,
    )
    hidden = w_mid.shape[0]
    feature = w_in.shape[0]
    high = b_in[...].astype(BF).astype(F32)
    low = b_in[...] - high
    row = iota((32, hidden), 0)
    halves = []
    for l in range(2):
        r = iota((32, feature), 0)
        c = iota((32, feature), 1)
        chosen = (r < 24) & (((r >> 2) & 1) == l) & ((r >> 3) * 4 + (r & 3) == c)
        part = dot(jnp.where(chosen, 1.0, 0.0).astype(BF), w_in[...])
        part = jnp.where(row == 24, high, jnp.where(row == 25, low, part))
        halves.append(part)
    both = jnp.concatenate(halves, axis=1)
    in_back[...] = both.astype(BF)
    padded = jnp.concatenate([both, jnp.zeros((96, 2 * hidden), F32)], axis=0)
    in_all[...] = padded.T[:, :32].astype(BF)
    middle = w_mid[...].astype(F32)
    turned = middle.T
    zero = jnp.zeros((hidden, hidden), F32)
    for source, target in ((middle, mid_all), (turned, mid_back)):
        target[...] = jnp.concatenate(
            [jnp.concatenate([source, zero], axis=1), jnp.concatenate([zero, source], axis=1)],
            axis=0,
        ).astype(BF)
    column = jnp.broadcast_to(b_mid[...], (hidden, hidden)).T
    bias_mid[...] = jnp.concatenate([column, column], axis=0)
    out = w_out[...].astype(F32)
    empty = jnp.zeros((4, hidden), F32)
    upper = jnp.concatenate([out, empty], axis=0)
    lower = jnp.concatenate([empty, out], axis=0)
    wide_out = jnp.concatenate(
        [jnp.concatenate([upper, lower], axis=1), jnp.zeros((120, 2 * hidden), F32)], axis=0
    )
    out_all[...] = wide_out[:16].astype(BF)
    out_back[...] = wide_out.T[:, :16].astype(BF)
    r8 = iota((8, LANES), 0)
    f8 = r8 & 3

    def by_field(scalars):
        return jnp.where(
            f8 == 0,
            scalars[0],
            jnp.where(f8 == 1, scalars[1], jnp.where(f8 == 2, scalars[2], scalars[3])),
        )

    rows[0] = by_field(mix_h)
    rows[1] = jnp.where(r8 < 4, mix_v[0], mix_v[1])
    rows[2] = by_field(bias_out)
    here = lax.axis_index("tiles")
    half = lax.axis_index("sub")
    slots = codes.shape[1]
    for s in range(slots):
        for side in range(2):
            tile = we[side, s]
            safe = jnp.maximum(tile, 0)
            owner = jnp.bitwise_xor(lax.div(safe, slots), here)
            code = jnp.where(tile >= 0, owner * slots + lax.rem(safe, slots), -1)
            codes[side, s] = jnp.full((8, LANES), code, jnp.int32)
            code = jnp.where(half == side, sn[side, s], s)
            codes[2 + side, s] = jnp.full((8, LANES), code, jnp.int32)


def stencil(x, halos, cells):
    east, west, north, south = neighbours(x, halos, cells)
    diffuse = (east + west) + (north + south) - 4.0 * x
    ones = jnp.where(iota(x.shape, 0) < 2, 1.0, 0.0)
    features = jnp.concatenate([x, east - west, north - south, ones], axis=0).astype(BF)
    return diffuse, features


def keep_first(first_out, span, first):
    hidden = first.shape[0] // 2
    ones = jnp.ones((16, first.shape[1]), BF)
    for l in range(2):
        base = l * (hidden + 16)
        first_out[base : base + hidden, span] = first[l * hidden : (l + 1) * hidden]
        first_out[base + hidden : base + hidden + 16, span] = ones


def forward_kernel(
    peers, x_in, mask, above, below, partner, codes, in_all, mid_all, bias_mid, out_all, rows,
    *rest
):
    pools = rest[:peers]
    x_out, first_out, second_out, feature_out, columns, lines, closure = rest[peers:]
    slots = partner.shape[0]
    x = x_in[...]
    total = x.shape[1]
    cells = total // slots
    halos = halo_fields(codes, pools, partner, slots, cells)
    diffuse, features = stencil(x, halos, cells)
    feature_out[...] = features
    bias = wide(bias_mid[...], CHUNK // LANES)
    for start in range(0, total, CHUNK):
        span = slice(start, start + CHUNK)
        first = jnp.tanh(dot(in_all[...], feature_out[:, span])).astype(BF)
        keep_first(first_out, span, first)
        second = jnp.tanh(dot(mid_all[...], first) + bias).astype(BF)
        second_out[:, span] = second
        closure[:, span] = dot(out_all[...], second)[:8]
    mh, mv, bo = (wide(rows[k], total // LANES) for k in range(3))
    vertical = pltpu.roll(x, 4, 0) + level_halo(above, below, 0)
    x_new = mask[...] * (x + mh * diffuse + mv * (vertical - 2.0 * x) + (closure[...] + bo))
    x_out[...] = x_new
    write_edges(columns, lines, x_new, x_new, x_new, x_new)


def backward_tail(g, grad_feature, remote, rows, base, columns, lines, g_sum):
    total = g.shape[1]
    many = total // LANES
    cells = total // columns.shape[0]
    mh = wide(rows[0], many)
    mv = wide(rows[1], many)
    along = mh * g
    e_east = along + grad_feature[8:16]
    e_west = along - grad_feature[8:16]
    e_north = along + grad_feature[16:24]
    e_south = along - grad_feature[16:24]
    spread = mv * g
    vertical = pltpu.roll(spread, 4, 0) - 2.0 * spread
    if remote is not None:
        vertical = vertical + remote
    write_edges(columns, lines, e_west, e_east, e_south, e_north)
    base[...] = (
        (g + grad_feature[0:8])
        + (pull_back(e_east, e_west, e_north, e_south, cells) - 4.0 * along)
        + vertical
    )
    sums = [g[:, v * LANES : (v + 1) * LANES] for v in range(many)]
    g_sum[...] = tree_sum(sums)
    return spread


def grad_rows(g):
    return jnp.concatenate([g, jnp.zeros(g.shape, F32)], axis=0).astype(BF)


def turn_kernel(
    peers, x_in, mask, g_in, above, below, partner, codes, in_all, mid_all, bias_mid, out_all,
    rows, out_back, mid_back, in_back, *rest
):
    pools = rest[:peers]
    (
        x_out, base, columns, lines, g_sum, first_out, second_out, feature_out, grad_out,
        second_grad_out, first_grad_out, closure, grad_feature,
    ) = rest[peers:]
    slots = partner.shape[0]
    x = x_in[...]
    g = g_in[...]
    total = x.shape[1]
    cells = total // slots
    halos = halo_fields(codes, pools, partner, slots, cells)
    diffuse, features = stencil(x, halos, cells)
    feature_out[...] = features
    grad_out[...] = grad_rows(g)
    bias = wide(bias_mid[...], CHUNK // LANES)
    for start in range(0, total, CHUNK):
        span = slice(start, start + CHUNK)
        first = jnp.tanh(dot(in_all[...], feature_out[:, span])).astype(BF)
        keep_first(first_out, span, first)
        second = jnp.tanh(dot(mid_all[...], first) + bias).astype(BF)
        second_out[:, span] = second
        closure[:, span] = dot(out_all[...], second)[:8]
        second_grad = times_slope(dot(out_back[...], grad_out[:, span]), second)
        second_grad_out[:, span] = second_grad
        first_grad = times_slope(dot(mid_back[...], second_grad), first)
        first_grad_out[:, span] = first_grad
        grad_feature[:, span] = dot(in_back[...], first_grad)
    remote = level_halo(above, below, 1)
    backward_tail(g, grad_feature[...], remote, rows, base, columns, lines, g_sum)
    mh, mv, bo = (wide(rows[k], total // LANES) for k in range(3))
    x_out[...] = mask[...] * (
        x + mh * diffuse + mv * (pltpu.roll(x, 4, 0) - 2.0 * x) + (closure[...] + bo)
    )


def times_slope(grad, value):
    return grad.astype(BF) * (1.0 - value * value)


def back_kernel(
    peers, base_in, mask, x_in, partner, codes, first_in, second_in, rows, out_back, mid_back,
    in_back, *rest
):
    pools = rest[:peers]
    base, columns, lines, g_sum, grad_out, second_grad_out, first_grad_out = rest[
        peers : peers + 7
    ]
    sends = rest[peers + 7 : -1]
    grad_feature = rest[-1]
    slots = partner.shape[0]
    total = base_in.shape[1]
    cells = total // slots
    hidden = mid_back.shape[0] // 2
    halos = halo_fields(codes, pools, partner, slots, cells)
    g = mask[...] * (base_in[...] + halo_sum(halos, cells))
    grad_out[...] = grad_rows(g)
    for start in range(0, total, CHUNK):
        span = slice(start, start + CHUNK)
        first = jnp.concatenate(
            [first_in[:hidden, span], first_in[hidden + 16 : 2 * hidden + 16, span]], axis=0
        )
        second_grad = times_slope(dot(out_back[...], grad_out[:, span]), second_in[:, span])
        second_grad_out[:, span] = second_grad
        first_grad = times_slope(dot(mid_back[...], second_grad), first)
        first_grad_out[:, span] = first_grad
        grad_feature[:, span] = dot(in_back[...], first_grad)
    spread = backward_tail(g, grad_feature[...], None, rows, base, columns, lines, g_sum)
    write_sends(sends, 0, x_in[...], cells)
    write_sends(sends, 1, spread, cells)


def term_sums(first, second, features, grad, second_grad, first_grad):
    hidden = first.shape[0] // 2 - 16
    side = hidden + 16
    mid = dot_nt(second_grad[:hidden], first[:side]) + dot_nt(second_grad[hidden:], first[side:])
    return mid, dot_nt(first_grad[...], features[...]), dot_nt(second[...], grad[...])


def late_terms_kernel(*refs):
    for value, out in zip(term_sums(*refs[:6]), refs[6:]):
        out[...] = value


def early_terms_kernel(*refs):
    late = refs[6:10]
    g_sum, keep, send = refs[10:]
    mid, wing, out = (a + b[...] for a, b in zip(term_sums(*refs[:6]), late[:3]))
    total = late[3][...] + g_sum[...]
    hidden = mid.shape[0]
    top = iota((8, hidden), 0)

    def turned(block):
        blank = jnp.zeros((block.shape[0], hidden - block.shape[1]), F32)
        return jnp.concatenate([block, blank], axis=1).T

    low, high = turned(wing[:hidden]), turned(wing[hidden:])
    pieces = [mid[:, :hidden]]
    for kind in range(3):
        span = slice(8 * kind, 8 * kind + 8)
        pieces.append(low[span] + pltpu.roll(high[span], 4, 0))
    bias_in = low[24:32] + high[24:32]
    bias_mid = turned(mid[:, hidden:])[:8]
    pieces.append(jnp.where(top == 0, bias_in, pltpu.roll(bias_mid, 1, 0)))
    low, high = turned(out[:hidden]), turned(out[hidden:])
    pieces.append(
        jnp.where(top < 4, low[:8] + pltpu.roll(high[:8], 4, 0), total + pltpu.roll(total, 4, 0))
    )
    pieces.append(jnp.zeros((8, hidden), F32))
    packed = jnp.concatenate(pieces, axis=0)
    half = packed.shape[0] // 2
    core = lax.axis_index("sub")
    keep[...] = jnp.where(core == 0, packed[:half], packed[half:])
    send[...] = jnp.where(core == 0, packed[half:], packed[:half])


def finish_kernel(base_in, mask, x_in, above, below, partner, codes, rows, *rest):
    pools = rest[:-2]
    final, initial = rest[-2:]
    slots = partner.shape[0]
    total = base_in.shape[1]
    cells = total // slots
    mv = wide(rows[1], total // LANES)
    halos = halo_fields(codes, pools, partner, slots, cells)
    last = x_in[...] + mask[...] * (mv * level_halo(above, below, 0))
    early = mask[...] * ((base_in[...] + level_halo(above, below, 1)) + halo_sum(halos, cells))
    for s in range(slots):
        span = slice(s * cells, (s + 1) * cells)
        for l in range(2):
            for f in range(4):
                r = 4 * l + f
                final[f, l, s : s + 1, :] = last[r : r + 1, span]
                initial[f, l, s : s + 1, :] = early[r : r + 1, span]


def grads_kernel(scale, mine, other, w_in, b_in, w_mid, b_mid, w_out, b_out):
    hidden = w_mid.shape[0]
    core = lax.axis_index("sub")
    low = jnp.where(core == 0, mine[...], other[...])
    high = jnp.where(core == 0, other[...], mine[...])
    packed = jnp.concatenate([low, high], axis=0) * scale
    w_mid[...] = packed[:hidden]
    tail = packed[hidden:]
    w_in[0:4] = tail[0:4]
    w_in[4:8] = tail[8:12]
    w_in[8:12] = tail[16:20]
    b_in[...] = tail[24:25]
    b_mid[...] = tail[25:26]
    w_out[...] = tail[32:36]
    sums = jnp.broadcast_to(jnp.sum(tail[36:40], axis=1, keepdims=True), (4, hidden))
    spot = iota((4, hidden), 0) == iota((4, hidden), 1)
    b_out[...] = jnp.sum(jnp.where(spot, sums, 0.0), axis=0, keepdims=True)


def call(kernel, inputs, outs, scratch=(), spaces=None):
    return pl.pallas_call(
        kernel,
        in_specs=[pl.BlockSpec(memory_space=spaces or pltpu.VMEM)] * len(inputs),
        out_specs=[pl.BlockSpec(memory_space=pltpu.VMEM)] * len(outs),
        out_shape=outs,
        scratch_shapes=list(scratch),
        compiler_params=pltpu.CompilerParams(vmem_limit_bytes=VMEM_BYTES),
    )(*(inputs if spaces is None else [pltpu.with_memory_space_constraint(a, spaces) for a in inputs]))


def shape(dims, dtype=F32):
    return jax.ShapeDtypeStruct(tuple(dims), dtype)


def xor_pairs(axis, k):
    return [(i, i ^ k) for i in range(lax.axis_size(axis))]


def from_peers(packs):
    return [packs] + [
        lax.ppermute(packs, "tiles", xor_pairs("tiles", k))
        for k in range(1, lax.axis_size("tiles"))
    ]


def from_partner(lines):
    return lax.ppermute(lines, "sub", xor_pairs("sub", 1))


def from_levels(sends):
    depth = lax.axis_size("depth")
    if len(sends) == 1:
        other = lax.ppermute(sends[0], "depth", [(0, 1), (1, 0)])
        return other, other
    down = [(i, i + 1) for i in range(depth - 1)]
    return (
        lax.ppermute(sends[0], "depth", down),
        lax.ppermute(sends[1], "depth", [(j, i) for i, j in down]),
    )


def tree_sum(parts):
    while len(parts) > 1:
        parts = [parts[i] + parts[i + 1] for i in range(0, len(parts), 2)]
    return parts[0]


def sum_over(array, axis):
    return tree_sum(
        [array]
        + [lax.ppermute(array, axis, xor_pairs(axis, k)) for k in range(1, lax.axis_size(axis))]
    )


def body(
    state_init,
    cotangent,
    level_count,
    west_east,
    south_north,
    weight_in,
    bias_in,
    weight_mid,
    bias_mid,
    weight_out,
    bias_out,
    mix_horizontal,
    mix_vertical,
):
    fields, levels, slots, cells = state_init.shape
    hidden = weight_mid.shape[0]
    both = 2 * hidden
    total = slots * cells
    peers = lax.axis_size("tiles")
    field = shape((8, total))
    pack = shape((slots, 8, LANES))
    sends = [shape((2, slots // 2, 8, cells))] * (1 if lax.axis_size("depth") == 2 else 2)
    hidden_rows = shape((both, total), BF)
    first_rows = shape((both + 32, total), BF)
    vmem, smem = pltpu.VMEM, pltpu.SMEM

    inputs = [mix_vertical, state_init, cotangent, level_count]
    x_zero, g_late, mask, columns, lines, *levels_out = call(
        functools.partial(prep_kernel, len(sends)),
        inputs,
        [field, field, field, pack, pack] + sends,
        [
            smem(mix_vertical.shape, F32),
            vmem(state_init.shape, F32),
            vmem(cotangent.shape, F32),
            vmem(level_count.shape, jnp.int32),
            pltpu.SemaphoreType.DMA((len(inputs),)),
        ],
        pltpu.HBM,
    )
    above, below = from_levels(levels_out)
    pools = from_peers(columns)
    partner = from_partner(lines)

    inputs = [
        mix_horizontal,
        mix_vertical,
        bias_out,
        west_east.T,
        south_north.T,
        weight_in.T,
        bias_in.reshape(1, hidden),
        weight_mid,
        bias_mid.reshape(1, hidden),
        weight_out,
    ]
    in_all, in_back, mid_all, mid_back, mid_bias, out_all, out_back, rows, codes = call(
        weight_kernel,
        inputs,
        [
            shape((both, 32), BF),
            shape((32, both), BF),
            shape((both, both), BF),
            shape((both, both), BF),
            shape((both, hidden)),
            shape((16, both), BF),
            shape((both, 16), BF),
            shape((3, 8, LANES)),
            shape((4, slots, 8, LANES), jnp.int32),
        ],
        [(smem if i < 5 else vmem)(a.shape, a.dtype) for i, a in enumerate(inputs)]
        + [pltpu.SemaphoreType.DMA((len(inputs),))],
        pltpu.HBM,
    )
    forward_weights = [in_all, mid_all, mid_bias, out_all, rows]
    backward_weights = [out_back, mid_back, in_back]

    x_one, first, second, features, columns, lines = call(
        functools.partial(forward_kernel, peers),
        [x_zero, mask, above, below, partner, codes] + forward_weights + pools,
        [field, first_rows, hidden_rows, shape((32, total), BF), pack, pack],
        [vmem((8, total), F32)],
    )
    pools = from_peers(columns)
    partner = from_partner(lines)

    x_two, base, columns, lines, late_sum, *late = call(
        functools.partial(turn_kernel, peers),
        [x_one, mask, g_late, above, below, partner, codes]
        + forward_weights
        + backward_weights
        + pools,
        [
            field, field, pack, pack, shape((8, LANES)), first_rows, hidden_rows,
            shape((32, total), BF), shape((16, total), BF), hidden_rows, hidden_rows,
        ],
        [vmem((8, total), F32), vmem((32, total), F32)],
    )
    pools = from_peers(columns)
    partner = from_partner(lines)
    late = call(
        late_terms_kernel,
        late,
        [shape((hidden, hidden + 16)), shape((both, 32)), shape((both, 16))],
    )

    base, columns, lines, early_sum, grad, second_grad, first_grad, *levels_out = call(
        functools.partial(back_kernel, peers),
        [base, mask, x_one, partner, codes, first, second, rows] + backward_weights + pools,
        [
            field, pack, pack, shape((8, LANES)), shape((16, total), BF), hidden_rows, hidden_rows,
        ]
        + sends,
        [vmem((32, total), F32)],
    )
    above, below = from_levels(levels_out)
    pools = from_peers(columns)
    partner = from_partner(lines)
    half = shape(((hidden + 48) // 2, hidden))
    keep, give = call(
        early_terms_kernel,
        [first, second, features, grad, second_grad, first_grad, *late, late_sum, early_sum],
        [half, half],
    )
    terms = keep + lax.ppermute(give, "sub", xor_pairs("sub", 1))
    terms = sum_over(sum_over(terms, "depth"), "tiles")
    final_state, initial_cot = call(
        finish_kernel,
        [base, mask, x_two, above, below, partner, codes, rows] + pools,
        [shape(state_init.shape)] * 2,
    )
    count = (
        levels
        * lax.axis_size("depth")
        * slots
        * lax.axis_size("tiles")
        * cells
        * lax.axis_size("sub")
    )
    w_in, b_in, w_mid, b_mid, w_out, b_out = call(
        functools.partial(grads_kernel, 1.0 / math.sqrt(count)),
        [terms, lax.ppermute(terms, "sub", xor_pairs("sub", 1))],
        [
            shape(weight_in.T.shape),
            shape((1, hidden)),
            shape((hidden, hidden)),
            shape((1, hidden)),
            shape(weight_out.shape),
            shape((1, hidden)),
        ],
    )
    return (
        final_state,
        initial_cot,
        w_in.T,
        b_in.reshape(hidden),
        w_mid,
        b_mid.reshape(hidden),
        w_out,
        b_out[0, :fields],
    )


def solution(mesh):
    return jax.shard_map(
        body,
        mesh=mesh,
        in_specs=(
            P("groups", "depth", "tiles", "sub"),
            P("groups", "depth", "tiles", "sub"),
            P("tiles", "sub"),
            P("tiles", None),
            P("tiles", None),
            P(),
            P(),
            P(),
            P(),
            P(),
            P(),
            P(),
            P("depth"),
        ),
        out_specs=(
            P("groups", "depth", "tiles", "sub"),
            P("groups", "depth", "tiles", "sub"),
            P("groups", None),
            P("groups"),
            P("groups", None),
            P("groups"),
            P("groups", None),
            P("groups"),
        ),
        check_vma=False,
    )
```

time: 130 us -> 68 us (0.52)
  Pallas kernels: 68 us -> 24.8 us
  local copies, waits for them, and re-layouts: 11.7 us -> 0.51 us
  waiting for transfers between devices: 22.9 us -> 13.6 us
  starting transfers between devices: 26.4 us -> 28.1 us
    pallas_call x7 -> x9, Pallas kernels: 68 us -> 24.8 us  [call(): pl.pallas_call(kernel, in_specs=[pl.BlockSpec(memory_space=spaces or pltp...]
    unnamed x26 -> x0, local copies, waits for them, and re-layouts: 11 us -> none
    ppermute x2, waiting for transfers between devices: 5.29 us -> 0.85 us  [from_levels(): other = lax.ppermute(sends[0], 'depth', [(0, 1), (1, 0)])]
    ppermute x4, waiting for transfers between devices: 9.17 us -> 5.48 us  [sum_over(): lax.ppermute(array, axis, xor_pairs(axis, k))]
  transfers between devices with their start and end apart: 24 -> 24, of which waited for: 9 -> 11; matrix products, arithmetic and copies ran while one was open for 3% -> 1% of each run, Pallas kernels for 1% -> 8%
where the time goes in v1:
time: 68 us; the launch traced here: 67.8 us
  starting transfers between devices  28.1 us (41%)
  Pallas kernels  24.8 us (36%)
  waiting for transfers between devices  13.6 us (20%)
  between operations  0.78 us (1%)
    pallas_call x9, Pallas kernels, call(): pl.pallas_call(kernel, in_specs=[pl.BlockSpec(memory_space=spaces or pltp...  24.8 us
    ppermute x12, starting transfers between devices, from_peers(): lax.ppermute(packs, 'tiles', xor_pairs('tiles', k))  17.7 us
    ppermute x12, waiting for transfers between devices, from_peers(): lax.ppermute(packs, 'tiles', xor_pairs('tiles', k))  6.02 us
    ppermute x4, starting transfers between devices, sum_over(): lax.ppermute(array, axis, xor_pairs(axis, k))  5.98 us
    ppermute x4, waiting for transfers between devices, sum_over(): lax.ppermute(array, axis, xor_pairs(axis, k))  5.48 us
    ppermute x2, starting transfers between devices, from_levels(): other = lax.ppermute(sends[0], 'depth', [(0, 1), (1, 0)])  4.14 us
  transfers between devices with their start and end apart: 24, of which 11 were waited for; matrix products, arithmetic and copies ran while one was open for 1% of the time, Pallas kernels for 8%

profile of v1, /device:TPU:0, one launch (start us, length us, event | category | flops | bytes accessed | tf_op | source)
XLA Modules:
  0.0 67.8 jit_solution(7146797554197820645)
XLA Ops:
  0.6 1.4 %shard_map.188 = (f32[8,8192]{1,0:T(8,128)S(1)}, f32[8,8192]{1,0:T(8,128)S(1)}, f32[8,8192]{1,0:T(8,128)S(1)}, f32[4,8,128]{2,1,0:T(8,128)S(1)}, f32[4,8,128]{2,...) custom-call(f32[2]{0:T(128)} %mix_v_in.3, f32[4,2,4,2048]{3,2,1,0:T(4,128)} %state_in.1, f32[4,2,4,2048]{3,2,1,0:T(4,128)} %cot_in.1, ...), custom_call_target="tpu_custom_call" | custom-call | tf_op jit(solution)/shard_map/pallas_call | solution.py:503
  2.0 3.0 %collective-permute-start = (f32[2,2,8,2048]{3,2,1,0:T(8,128)S(1)}, f32[2,2,8,2048]{3,2,1,0:T(8,128)S(1)}, u32[]{:S(2)}, u32[]{:S(2)}) collective-permute-start(f32[2,2,8,2048]{3,2,1,0:T(8,128)S(1)} %get-tuple-element.63), channel_id=1, source_target_pairs={{0,2},{2,0},{1,3},{3,1},{4,6},{6,4},{5,7},{7,5},{8,10},{10,8},{9,1... | collective-permute-start | bytes 786440 | tf_op jit(solution)/shard_map/ppermute | solution.py:535
  5.0 3.6 %collective-permute-start.4 = (f32[4,8,128]{2,1,0:T(8,128)S(1)}, f32[4,8,128]{2,1,0:T(8,128)S(1)}, u32[]{:S(2)}, u32[]{:S(2)}) collective-permute-start(f32[4,8,128]{2,1,0:T(8,128)S(1)} %get-tuple-element.71.rest_0_), channel_id=1, source_target_pairs={{0,12},{4,8},{8,4},{12,0},{1,13},{5,9},{9,5},{13,1},{2,14},{6,10},... | collective-permute-start | bytes 49160 | tf_op jit(solution)/shard_map/ppermute | solution.py:523
  9.4 1.1 %shard_map.189 = (bf16[256,32]{1,0:T(8,128)(2,1)S(1)}, bf16[32,256]{1,0:T(8,128)(2,1)S(1)}, bf16[256,256]{1,0:T(8,128)(2,1)S(1)}, bf16[256,256]{1,0:T(8,128)(2,1...) custom-call(f32[4]{0:T(128)} %mix_h_in.1, ...), custom_call_target="tpu_custom_call" | custom-call | tf_op jit(solution)/shard_map/pallas_call | solution.py:503
  10.6 2.7 %collective-permute-done.3.rest_2_ = f32[4,8,128]{2,1,0:T(8,128)S(1)} collective-permute-done((f32[4,8,128]{2,1,0:T(8,128)S(1)}, f32[4,8,128]{2,1,0:T(8,128)S(1)}, u32[]{:S(2)}, u32[]{:S(2)}) %collective-permute-start.3) | collective-permute-done | bytes 16416 | tf_op jit(solution)/shard_map/ppermute | solution.py:523
  13.3 3.2 %shard_map.190 = (f32[8,8192]{1,0:T(8,128)S(1)}, bf16[288,8192]{1,0:T(8,128)(2,1)S(1)}, bf16[256,8192]{1,0:T(8,128)(2,1)S(1)}, bf16[32,8192]{1,0:T(8,128)(2,1)S(...) custom-call(f32[8,8192]{1,0:T(8,128)S(1)} %get-tuple-element.61.x_in, f32[8,8192]{1,0:T(8,128)S(1)} %get-tuple-element.62.mask, ...), custom_call_target="tpu_custom_call" | custom-call | tf_op jit(solution)/shard_map/pallas_call | solution.py:503
  16.6 2.0 %collective-permute-start.8 = (f32[4,8,128]{2,1,0:T(8,128)S(1)}, f32[4,8,128]{2,1,0:T(8,128)S(1)}, u32[]{:S(2)}, u32[]{:S(2)}) collective-permute-start(f32[4,8,128]{2,1,0:T(8,128)S(1)} %get-tuple-element.78.rest_0_), channel_id=1, source_target_pairs={{0,12},{4,8},{8,4},{12,0},{1,13},{5,9},{9,5},{13,1},{2,14},{6,10},... | collective-permute-start | bytes 49160 | tf_op jit(solution)/shard_map/ppermute | solution.py:523
  18.7 2.3 %collective-permute-start.6 = (f32[4,8,128]{2,1,0:T(8,128)S(1)}, f32[4,8,128]{2,1,0:T(8,128)S(1)}, u32[]{:S(2)}, u32[]{:S(2)}) collective-permute-start(f32[4,8,128]{2,1,0:T(8,128)S(1)} %get-tuple-element.78.rest_0_), channel_id=1, source_target_pairs={{0,4},{4,0},{8,12},{12,8},{1,5},{5,1},{9,13},{13,9},{2,6},{6,2},{1... | collective-permute-start | bytes 49160 | tf_op jit(solution)/shard_map/ppermute | solution.py:523
  21.0 1.1 %collective-permute-done.8.rest_3_ = f32[4,8,128]{2,1,0:T(8,128)S(1)} collective-permute-done((f32[4,8,128]{2,1,0:T(8,128)S(1)}, f32[4,8,128]{2,1,0:T(8,128)S(1)}, u32[]{:S(2)}, u32[]{:S(2)}) %collective-permute-start.8) | collective-permute-done | bytes 16416 | tf_op jit(solution)/shard_map/ppermute | solution.py:523
  23.2 6.6 %shard_map.191 = (f32[8,8192]{1,0:T(8,128)S(1)}, f32[8,8192]{1,0:T(8,128)S(1)}, f32[4,8,128]{2,1,0:T(8,128)S(1)}, f32[4,8,128]{2,1,0:T(8,128)S(1)}, f32[8,128]{1...) custom-call(f32[8,8192]{1,0:T(8,128)S(1)} %get-tuple-element.72.x_in, ...), custom_call_target="tpu_custom_call" | custom-call | tf_op jit(solution)/shard_map/pallas_call | solution.py:503
  29.9 2.2 %collective-permute-start.12 = (f32[4,8,128]{2,1,0:T(8,128)S(1)}, f32[4,8,128]{2,1,0:T(8,128)S(1)}, u32[]{:S(2)}, u32[]{:S(2)}) collective-permute-start(f32[4,8,128]{2,1,0:T(8,128)S(1)} %get-tuple-element.83.rest_0_), channel_id=1, source_target_pairs={{0,12},{4,8},{8,4},{12,0},{1,13},{5,9},{9,5},{13,1},{2,14},{6,10},... | collective-permute-start | bytes 49160 | tf_op jit(solution)/shard_map/ppermute | solution.py:523
  33.0 1.3 %collective-permute-start.10 = (f32[4,8,128]{2,1,0:T(8,128)S(1)}, f32[4,8,128]{2,1,0:T(8,128)S(1)}, u32[]{:S(2)}, u32[]{:S(2)}) collective-permute-start(f32[4,8,128]{2,1,0:T(8,128)S(1)} %get-tuple-element.83.rest_0_), channel_id=1, source_target_pairs={{0,4},{4,0},{8,12},{12,8},{1,5},{5,1},{9,13},{13,9},{2,6},{6,2},{1... | collective-permute-start | bytes 49160 | tf_op jit(solution)/shard_map/ppermute | solution.py:523
  34.3 3.7 %shard_map.194 = (f32[128,144]{1,0:T(8,128)S(1)}, f32[256,32]{1,0:T(8,128)S(1)}, f32[256,16]{1,0:T(8,128)S(1)}) custom-call(bf16[288,8192]{1,0:T(8,128)(2,1)S(1)} %get-tuple-element.95.refs_0_, bf16[256,8192]{1,0:T(8,128)(2,1)S(1)} %get-tuple-element.96.refs_1_, bf16[32,8192]{1,0:T(8,128)(2,1)S(1)} %get-tuple-element.97.refs_2_, ...), custom_call_target="tpu_custom_call" | custom-call | tf_op jit(solution)/shard_map/pallas_call | solution.py:503
  38.1 3.3 %shard_map.192 = (f32[8,8192]{1,0:T(8,128)S(1)}, f32[4,8,128]{2,1,0:T(8,128)S(1)}, f32[4,8,128]{2,1,0:T(8,128)S(1)}, f32[8,128]{1,0:T(8,128)S(1)}, bf16[16,8192]...) custom-call(f32[8,8192]{1,0:T(8,128)S(1)} %get-tuple-element.79.base, ...), custom_call_target="tpu_custom_call" | custom-call | tf_op jit(solution)/shard_map/pallas_call | solution.py:503
  41.4 3.7 %shard_map.195 = (f32[88,128]{1,0:T(8,128)S(1)}, f32[88,128]{1,0:T(8,128)S(1)}) custom-call(bf16[288,8192]{1,0:T(8,128)(2,1)S(1)} %get-tuple-element.81.first_in.refs_0_, bf16[256,8192]{1,0:T(8,128)(2,1)S(1)} %get-tuple-element.82.second_in.refs_1_, bf16[32,8192]{1,0:T(8,128)(2,1)S(1)} %get-tuple-element.91.refs_2_, ...), custom_call_target="tpu_custom_call" | custom-call | tf_op jit(solution)/shard_map/pallas_call | solution.py:503
  45.1 1.2 %collective-permute-done.18 = f32[88,128]{1,0:T(8,128)S(1)} collective-permute-done((f32[88,128]{1,0:T(8,128)S(1)}, f32[88,128]{1,0:T(8,128)S(1)}, u32[]{:S(2)}, u32[]{:S(2)}) %collective-permute-start.18) | collective-permute-done | bytes 45088 | tf_op jit(solution)/shard_map/ppermute | solution.py:682
  46.4 1.5 %collective-permute-start.19 = (f32[88,128]{1,0:T(8,128)S(1)}, f32[88,128]{1,0:T(8,128)S(1)}, u32[]{:S(2)}, u32[]{:S(2)}) collective-permute-start(f32[88,128]{1,0:T(8,128)S(1)} %add.15), channel_id=1, source_target_pairs={{0,2},{2,0},{1,3},{3,1},{4,6},{6,4},{5,7},{7,5},{8,10},{10,8},{9,1... | collective-permute-start | bytes 135176 | tf_op jit(solution)/shard_map/ppermute | solution.py:553
  47.9 2.6 %collective-permute-done.19 = f32[88,128]{1,0:T(8,128)S(1)} collective-permute-done((f32[88,128]{1,0:T(8,128)S(1)}, f32[88,128]{1,0:T(8,128)S(1)}, u32[]{:S(2)}, u32[]{:S(2)}) %collective-permute-start.19) | collective-permute-done | bytes 45088 | tf_op jit(solution)/shard_map/ppermute | solution.py:553
  50.5 2.2 %collective-permute-start.22 = (f32[88,128]{1,0:T(8,128)S(1)}, f32[88,128]{1,0:T(8,128)S(1)}, u32[]{:S(2)}, u32[]{:S(2)}) collective-permute-start(f32[88,128]{1,0:T(8,128)S(1)} %add.16), channel_id=1, source_target_pairs={{0,12},{4,8},{8,4},{12,0},{1,13},{5,9},{9,5},{13,1},{2,14},{6,10},... | collective-permute-start | bytes 135176 | tf_op jit(solution)/shard_map/ppermute | solution.py:553
  52.7 2.2 %collective-permute-start.20 = (f32[88,128]{1,0:T(8,128)S(1)}, f32[88,128]{1,0:T(8,128)S(1)}, u32[]{:S(2)}, u32[]{:S(2)}) collective-permute-start(f32[88,128]{1,0:T(8,128)S(1)} %add.16), channel_id=1, source_target_pairs={{0,4},{4,0},{8,12},{12,8},{1,5},{5,1},{9,13},{13,9},{2,6},{6,2},{1... | collective-permute-start | bytes 135176 | tf_op jit(solution)/shard_map/ppermute | solution.py:553
  54.9 1.8 %collective-permute-done.22 = f32[88,128]{1,0:T(8,128)S(1)} collective-permute-done((f32[88,128]{1,0:T(8,128)S(1)}, f32[88,128]{1,0:T(8,128)S(1)}, u32[]{:S(2)}, u32[]{:S(2)}) %collective-permute-start.22) | collective-permute-done | bytes 45088 | tf_op jit(solution)/shard_map/ppermute | solution.py:553
  57.9 1.1 %collective-permute-start.13 = (f32[2,2,8,2048]{3,2,1,0:T(8,128)S(1)}, f32[2,2,8,2048]{3,2,1,0:T(8,128)S(1)}, u32[]{:S(2)}, u32[]{:S(2)}) collective-permute-start(f32[2,2,8,2048]{3,2,1,0:T(8,128)S(1)} %get-tuple-element.86), channel_id=1, source_target_pairs={{0,2},{2,0},{1,3},{3,1},{4,6},{6,4},{5,7},{7,5},{8,10},{10,8},{9,1... | collective-permute-start | bytes 786440 | tf_op jit(solution)/shard_map/ppermute | solution.py:535
  59.1 1.9 %collective-permute-start.17 = (f32[4,8,128]{2,1,0:T(8,128)S(1)}, f32[4,8,128]{2,1,0:T(8,128)S(1)}, u32[]{:S(2)}, u32[]{:S(2)}) collective-permute-start(f32[4,8,128]{2,1,0:T(8,128)S(1)} %get-tuple-element.88.rest_0_), channel_id=1, source_target_pairs={{0,12},{4,8},{8,4},{12,0},{1,13},{5,9},{9,5},{13,1},{2,14},{6,10},... | collective-permute-start | bytes 49160 | tf_op jit(solution)/shard_map/ppermute | solution.py:523
  62.1 1.4 %collective-permute-start.15 = (f32[4,8,128]{2,1,0:T(8,128)S(1)}, f32[4,8,128]{2,1,0:T(8,128)S(1)}, u32[]{:S(2)}, u32[]{:S(2)}) collective-permute-start(f32[4,8,128]{2,1,0:T(8,128)S(1)} %get-tuple-element.88.rest_0_), channel_id=1, source_target_pairs={{0,4},{4,0},{8,12},{12,8},{1,5},{5,1},{9,13},{13,9},{2,6},{6,2},{1... | collective-permute-start | bytes 49160 | tf_op jit(solution)/shard_map/ppermute | solution.py:523
  (37 shorter events, 9.8 us)
Async XLA Ops:
  2.0 11.3 %collective-permute-start = (f32[2,2,8,2048]{3,2,1,0:T(8,128)S(1)}, f32[2,2,8,2048]{3,2,1,0:T(8,128)S(1)}, u32[]{:S(2)}, u32[]{:S(2)}) collective-permute-start(f32[2,2,8,2048]{3,2,1,0:T(8,128)S(1)} %get-tuple-element.63), channel_id=1, source_target_pairs={{0,2},{2,0},{1,3},{3,1},{4,6},{6,4},{5,7},{7,5},{8,10},{10,8},{9,1... | collective-permute-start | bytes 786440 | tf_op jit(solution)/shard_map/ppermute | solution.py:535
  5.0 5.5 %collective-permute-start.1 = (f32[4,8,128]{2,1,0:T(8,128)S(1)}, f32[4,8,128]{2,1,0:T(8,128)S(1)}, u32[]{:S(2)}, u32[]{:S(2)}) collective-permute-start(f32[4,8,128]{2,1,0:T(8,128)S(1)} %get-tuple-element.64), channel_id=1, source_target_pairs={{0,1},{1,0},{2,3},{3,2},{4,5},{5,4},{6,7},{7,6},{8,9},{9,8},{10,11... | collective-permute-start | bytes 49160 | tf_op jit(solution)/shard_map/ppermute | solution.py:529
  5.0 5.6 %collective-permute-start.4 = (f32[4,8,128]{2,1,0:T(8,128)S(1)}, f32[4,8,128]{2,1,0:T(8,128)S(1)}, u32[]{:S(2)}, u32[]{:S(2)}) collective-permute-start(f32[4,8,128]{2,1,0:T(8,128)S(1)} %get-tuple-element.71.rest_0_), channel_id=1, source_target_pairs={{0,12},{4,8},{8,4},{12,0},{1,13},{5,9},{9,5},{13,1},{2,14},{6,10},... | collective-permute-start | bytes 49160 | tf_op jit(solution)/shard_map/ppermute | solution.py:523
  8.6 4.6 %collective-permute-start.3 = (f32[4,8,128]{2,1,0:T(8,128)S(1)}, f32[4,8,128]{2,1,0:T(8,128)S(1)}, u32[]{:S(2)}, u32[]{:S(2)}) collective-permute-start(f32[4,8,128]{2,1,0:T(8,128)S(1)} %get-tuple-element.71.rest_0_), channel_id=1, source_target_pairs={{0,8},{4,12},{8,0},{12,4},{1,9},{5,13},{9,1},{13,5},{2,10},{6,14},... | collective-permute-start | bytes 49160 | tf_op jit(solution)/shard_map/ppermute | solution.py:523
  8.6 4.6 %collective-permute-start.2 = (f32[4,8,128]{2,1,0:T(8,128)S(1)}, f32[4,8,128]{2,1,0:T(8,128)S(1)}, u32[]{:S(2)}, u32[]{:S(2)}) collective-permute-start(f32[4,8,128]{2,1,0:T(8,128)S(1)} %get-tuple-element.71.rest_0_), channel_id=1, source_target_pairs={{0,4},{4,0},{8,12},{12,8},{1,5},{5,1},{9,13},{13,9},{2,6},{6,2},{1... | collective-permute-start | bytes 49160 | tf_op jit(solution)/shard_map/ppermute | solution.py:523
  16.5 4.5 %collective-permute-start.5 = (f32[4,8,128]{2,1,0:T(8,128)S(1)}, f32[4,8,128]{2,1,0:T(8,128)S(1)}, u32[]{:S(2)}, u32[]{:S(2)}) collective-permute-start(f32[4,8,128]{2,1,0:T(8,128)S(1)} %get-tuple-element.74), channel_id=1, source_target_pairs={{0,1},{1,0},{2,3},{3,2},{4,5},{5,4},{6,7},{7,6},{8,9},{9,8},{10,11... | collective-permute-start | bytes 49160 | tf_op jit(solution)/shard_map/ppermute | solution.py:529
  16.6 5.6 %collective-permute-start.8 = (f32[4,8,128]{2,1,0:T(8,128)S(1)}, f32[4,8,128]{2,1,0:T(8,128)S(1)}, u32[]{:S(2)}, u32[]{:S(2)}) collective-permute-start(f32[4,8,128]{2,1,0:T(8,128)S(1)} %get-tuple-element.78.rest_0_), channel_id=1, source_target_pairs={{0,12},{4,8},{8,4},{12,0},{1,13},{5,9},{9,5},{13,1},{2,14},{6,10},... | collective-permute-start | bytes 49160 | tf_op jit(solution)/shard_map/ppermute | solution.py:523
  18.6 4.6 %collective-permute-start.7 = (f32[4,8,128]{2,1,0:T(8,128)S(1)}, f32[4,8,128]{2,1,0:T(8,128)S(1)}, u32[]{:S(2)}, u32[]{:S(2)}) collective-permute-start(f32[4,8,128]{2,1,0:T(8,128)S(1)} %get-tuple-element.78.rest_0_), channel_id=1, source_target_pairs={{0,8},{4,12},{8,0},{12,4},{1,9},{5,13},{9,1},{13,5},{2,10},{6,14},... | collective-permute-start | bytes 49160 | tf_op jit(solution)/shard_map/ppermute | solution.py:523
  18.7 4.5 %collective-permute-start.6 = (f32[4,8,128]{2,1,0:T(8,128)S(1)}, f32[4,8,128]{2,1,0:T(8,128)S(1)}, u32[]{:S(2)}, u32[]{:S(2)}) collective-permute-start(f32[4,8,128]{2,1,0:T(8,128)S(1)} %get-tuple-element.78.rest_0_), channel_id=1, source_target_pairs={{0,4},{4,0},{8,12},{12,8},{1,5},{5,1},{9,13},{13,9},{2,6},{6,2},{1... | collective-permute-start | bytes 49160 | tf_op jit(solution)/shard_map/ppermute | solution.py:523
  29.8 8.2 %collective-permute-start.9 = (f32[4,8,128]{2,1,0:T(8,128)S(1)}, f32[4,8,128]{2,1,0:T(8,128)S(1)}, u32[]{:S(2)}, u32[]{:S(2)}) collective-permute-start(f32[4,8,128]{2,1,0:T(8,128)S(1)} %get-tuple-element.80), channel_id=1, source_target_pairs={{0,1},{1,0},{2,3},{3,2},{4,5},{5,4},{6,7},{7,6},{8,9},{9,8},{10,11... | collective-permute-start | bytes 49160 | tf_op jit(solution)/shard_map/ppermute | solution.py:529
  29.9 8.2 %collective-permute-start.12 = (f32[4,8,128]{2,1,0:T(8,128)S(1)}, f32[4,8,128]{2,1,0:T(8,128)S(1)}, u32[]{:S(2)}, u32[]{:S(2)}) collective-permute-start(f32[4,8,128]{2,1,0:T(8,128)S(1)} %get-tuple-element.83.rest_0_), channel_id=1, source_target_pairs={{0,12},{4,8},{8,4},{12,0},{1,13},{5,9},{9,5},{13,1},{2,14},{6,10},... | collective-permute-start | bytes 49160 | tf_op jit(solution)/shard_map/ppermute | solution.py:523
  32.0 6.0 %collective-permute-start.11 = (f32[4,8,128]{2,1,0:T(8,128)S(1)}, f32[4,8,128]{2,1,0:T(8,128)S(1)}, u32[]{:S(2)}, u32[]{:S(2)}) collective-permute-start(f32[4,8,128]{2,1,0:T(8,128)S(1)} %get-tuple-element.83.rest_0_), channel_id=1, source_target_pairs={{0,8},{4,12},{8,0},{12,4},{1,9},{5,13},{9,1},{13,5},{2,10},{6,14},... | collective-permute-start | bytes 49160 | tf_op jit(solution)/shard_map/ppermute | solution.py:523
  33.0 5.1 %collective-permute-start.10 = (f32[4,8,128]{2,1,0:T(8,128)S(1)}, f32[4,8,128]{2,1,0:T(8,128)S(1)}, u32[]{:S(2)}, u32[]{:S(2)}) collective-permute-start(f32[4,8,128]{2,1,0:T(8,128)S(1)} %get-tuple-element.83.rest_0_), channel_id=1, source_target_pairs={{0,4},{4,0},{8,12},{12,8},{1,5},{5,1},{9,13},{13,9},{2,6},{6,2},{1... | collective-permute-start | bytes 49160 | tf_op jit(solution)/shard_map/ppermute | solution.py:523
  45.1 1.3 %collective-permute-start.18 = (f32[88,128]{1,0:T(8,128)S(1)}, f32[88,128]{1,0:T(8,128)S(1)}, u32[]{:S(2)}, u32[]{:S(2)}) collective-permute-start(f32[88,128]{1,0:T(8,128)S(1)} %get-tuple-element.107), channel_id=1, source_target_pairs={{0,1},{1,0},{2,3},{3,2},{4,5},{5,4},{6,7},{7,6},{8,9},{9,8},{10,11... | collective-permute-start | bytes 135176 | tf_op jit(solution)/shard_map/ppermute | solution.py:682
  46.4 4.1 %collective-permute-start.19 = (f32[88,128]{1,0:T(8,128)S(1)}, f32[88,128]{1,0:T(8,128)S(1)}, u32[]{:S(2)}, u32[]{:S(2)}) collective-permute-start(f32[88,128]{1,0:T(8,128)S(1)} %add.15), channel_id=1, source_target_pairs={{0,2},{2,0},{1,3},{3,1},{4,6},{6,4},{5,7},{7,5},{8,10},{10,8},{9,1... | collective-permute-start | bytes 135176 | tf_op jit(solution)/shard_map/ppermute | solution.py:553
  50.5 6.3 %collective-permute-start.22 = (f32[88,128]{1,0:T(8,128)S(1)}, f32[88,128]{1,0:T(8,128)S(1)}, u32[]{:S(2)}, u32[]{:S(2)}) collective-permute-start(f32[88,128]{1,0:T(8,128)S(1)} %add.16), channel_id=1, source_target_pairs={{0,12},{4,8},{8,4},{12,0},{1,13},{5,9},{9,5},{13,1},{2,14},{6,10},... | collective-permute-start | bytes 135176 | tf_op jit(solution)/shard_map/ppermute | solution.py:553
  52.6 5.2 %collective-permute-start.21 = (f32[88,128]{1,0:T(8,128)S(1)}, f32[88,128]{1,0:T(8,128)S(1)}, u32[]{:S(2)}, u32[]{:S(2)}) collective-permute-start(f32[88,128]{1,0:T(8,128)S(1)} %add.16), channel_id=1, source_target_pairs={{0,8},{4,12},{8,0},{12,4},{1,9},{5,13},{9,1},{13,5},{2,10},{6,14},... | collective-permute-start | bytes 135176 | tf_op jit(solution)/shard_map/ppermute | solution.py:553
  52.7 5.2 %collective-permute-start.20 = (f32[88,128]{1,0:T(8,128)S(1)}, f32[88,128]{1,0:T(8,128)S(1)}, u32[]{:S(2)}, u32[]{:S(2)}) collective-permute-start(f32[88,128]{1,0:T(8,128)S(1)} %add.16), channel_id=1, source_target_pairs={{0,4},{4,0},{8,12},{12,8},{1,5},{5,1},{9,13},{13,9},{2,6},{6,2},{1... | collective-permute-start | bytes 135176 | tf_op jit(solution)/shard_map/ppermute | solution.py:553
  57.9 5.6 %collective-permute-start.23 = (f32[88,128]{1,0:T(8,128)S(1)}, f32[88,128]{1,0:T(8,128)S(1)}, u32[]{:S(2)}, u32[]{:S(2)}) collective-permute-start(f32[88,128]{1,0:T(8,128)S(1)} %add_add_fusion.mine), channel_id=1, source_target_pairs={{0,1},{1,0},{2,3},{3,2},{4,5},{5,4},{6,7},{7,6},{8,9},{9,8},{10,11... | collective-permute-start | bytes 135176 | tf_op jit(solution)/shard_map/ppermute | solution.py:699
  57.9 8.7 %collective-permute-start.13 = (f32[2,2,8,2048]{3,2,1,0:T(8,128)S(1)}, f32[2,2,8,2048]{3,2,1,0:T(8,128)S(1)}, u32[]{:S(2)}, u32[]{:S(2)}) collective-permute-start(f32[2,2,8,2048]{3,2,1,0:T(8,128)S(1)} %get-tuple-element.86), channel_id=1, source_target_pairs={{0,2},{2,0},{1,3},{3,1},{4,6},{6,4},{5,7},{7,5},{8,10},{10,8},{9,1... | collective-permute-start | bytes 786440 | tf_op jit(solution)/shard_map/ppermute | solution.py:535
  59.1 5.6 %collective-permute-start.17 = (f32[4,8,128]{2,1,0:T(8,128)S(1)}, f32[4,8,128]{2,1,0:T(8,128)S(1)}, u32[]{:S(2)}, u32[]{:S(2)}) collective-permute-start(f32[4,8,128]{2,1,0:T(8,128)S(1)} %get-tuple-element.88.rest_0_), channel_id=1, source_target_pairs={{0,12},{4,8},{8,4},{12,0},{1,13},{5,9},{9,5},{13,1},{2,14},{6,10},... | collective-permute-start | bytes 49160 | tf_op jit(solution)/shard_map/ppermute | solution.py:523
  61.0 4.6 %collective-permute-start.16 = (f32[4,8,128]{2,1,0:T(8,128)S(1)}, f32[4,8,128]{2,1,0:T(8,128)S(1)}, u32[]{:S(2)}, u32[]{:S(2)}) collective-permute-start(f32[4,8,128]{2,1,0:T(8,128)S(1)} %get-tuple-element.88.rest_0_), channel_id=1, source_target_pairs={{0,8},{4,12},{8,0},{12,4},{1,9},{5,13},{9,1},{13,5},{2,10},{6,14},... | collective-permute-start | bytes 49160 | tf_op jit(solution)/shard_map/ppermute | solution.py:523
  62.1 3.7 %collective-permute-start.15 = (f32[4,8,128]{2,1,0:T(8,128)S(1)}, f32[4,8,128]{2,1,0:T(8,128)S(1)}, u32[]{:S(2)}, u32[]{:S(2)}) collective-permute-start(f32[4,8,128]{2,1,0:T(8,128)S(1)} %get-tuple-element.88.rest_0_), channel_id=1, source_target_pairs={{0,4},{4,0},{8,12},{12,8},{1,5},{5,1},{9,13},{13,9},{2,6},{6,2},{1... | collective-permute-start | bytes 49160 | tf_op jit(solution)/shard_map/ppermute | solution.py:523
  63.5 1.2 %collective-permute-start.14 = (f32[4,8,128]{2,1,0:T(8,128)S(1)}, f32[4,8,128]{2,1,0:T(8,128)S(1)}, u32[]{:S(2)}, u32[]{:S(2)}) collective-permute-start(f32[4,8,128]{2,1,0:T(8,128)S(1)} %get-tuple-element.87), channel_id=1, source_target_pairs={{0,1},{1,0},{2,3},{3,2},{4,5},{5,4},{6,7},{7,6},{8,9},{9,8},{10,11... | collective-permute-start | bytes 49160 | tf_op jit(solution)/shard_map/ppermute | solution.py:529

commit v2 on v1

--- a/solution.py
+++ b/solution.py
@@ -33,15 +33,16 @@
     return jnp.concatenate([block] * copies, axis=1)
 
 
-def pack_columns(first, last):
+def pack_columns(first, last, place_of_slot):
     place = iota((8, LANES), 1) & 63
     packed = jnp.zeros((8, LANES), F32)
     for v in range(first.shape[1] // LANES):
         span = slice(v * LANES, (v + 1) * LANES)
-        low = pltpu.roll(first[:, span], v, 1) if v else first[:, span]
-        high = pltpu.roll(last[:, span], v + 17, 1)
-        packed = jnp.where(place == v, low, packed)
-        packed = jnp.where(place == 16 + v, high, packed)
+        at = v + place_of_slot
+        low = pltpu.roll(first[:, span], at, 1) if at else first[:, span]
+        high = pltpu.roll(last[:, span], at + 17, 1)
+        packed = jnp.where(place == at, low, packed)
+        packed = jnp.where(place == at + 16, high, packed)
     return packed
 
 
@@ -51,7 +52,7 @@
     return jnp.where(lane < TCOL, first[:, :LANES], last[:, cells - LANES :])
 
 
-def halo_fields(codes, pools, partner, slots, cells):
+def halo_fields(codes, pools, partner, slots, cells, skip=None):
     lane = iota((8, LANES), 1)
     count = cells // LANES
     east, west, lines = [], [], []
@@ -62,7 +63,11 @@
             found = jnp.where(code == k, block, found)
         return found
 
-    column_blocks = [pool[s] for pool in pools for s in range(slots)]
+    column_blocks = []
+    for pool in pools:
+        for i in range(slots // 2):
+            both = pool[i] if skip is None else pool[skip + 8 * i : skip + 8 * i + 8]
+            column_blocks += [both, pltpu.roll(both, LANES - 32, 1)]
     line_blocks = [partner[s] for s in range(slots)]
     for s in range(slots):
         west_pack = chosen(codes[0, s], column_blocks)
@@ -112,11 +117,16 @@
 
 
 def write_edges(columns, lines, first_column, last_column, first_line, last_line):
-    slots = columns.shape[0]
+    slots = lines.shape[0]
     cells = first_column.shape[1] // slots
-    for s in range(slots):
-        span = slice(s * cells, (s + 1) * cells)
-        columns[s] = pack_columns(first_column[:, span], last_column[:, span])
+    spans = [slice(s * cells, (s + 1) * cells) for s in range(slots)]
+    packs = [
+        pack_columns(first_column[:, span], last_column[:, span], 32 * (s % 2))
+        for s, span in enumerate(spans)
+    ]
+    for s, span in enumerate(spans):
+        if s % 2 == 0:
+            columns[s // 2] = packs[s] + packs[s + 1]
         lines[s] = pack_lines(first_line[:, span], last_line[:, span])
 
 
@@ -315,7 +325,7 @@
 def backward_tail(g, grad_feature, remote, rows, base, columns, lines, g_sum):
     total = g.shape[1]
     many = total // LANES
-    cells = total // columns.shape[0]
+    cells = total // lines.shape[0]
     mh = wide(rows[0], many)
     mv = wide(rows[1], many)
     along = mh * g
@@ -342,13 +352,21 @@
     return jnp.concatenate([g, jnp.zeros(g.shape, F32)], axis=0).astype(BF)
 
 
+def seed_kernel(g_in, out_back, grad_out, seed_out):
+    grad_out[...] = grad_rows(g_in[...])
+    total = g_in.shape[1]
+    for start in range(0, total, CHUNK):
+        span = slice(start, start + CHUNK)
+        seed_out[:, span] = dot(out_back[...], grad_out[:, span]).astype(BF)
+
+
 def turn_kernel(
-    peers, x_in, mask, g_in, above, below, partner, codes, in_all, mid_all, bias_mid, out_all,
-    rows, out_back, mid_back, in_back, *rest
+    peers, x_in, mask, g_in, seed, above, below, partner, codes, in_all, mid_all, bias_mid,
+    out_all, rows, mid_back, in_back, *rest
 ):
     pools = rest[:peers]
     (
-        x_out, base, columns, lines, g_sum, first_out, second_out, feature_out, grad_out,
+        x_out, base, columns, lines, g_sum, first_out, second_out, feature_out,
         second_grad_out, first_grad_out, closure, grad_feature,
     ) = rest[peers:]
     slots = partner.shape[0]
@@ -359,7 +377,6 @@
     halos = halo_fields(codes, pools, partner, slots, cells)
     diffuse, features = stencil(x, halos, cells)
     feature_out[...] = features
-    grad_out[...] = grad_rows(g)
     bias = wide(bias_mid[...], CHUNK // LANES)
     for start in range(0, total, CHUNK):
         span = slice(start, start + CHUNK)
@@ -368,7 +385,7 @@
         second = jnp.tanh(dot(mid_all[...], first) + bias).astype(BF)
         second_out[:, span] = second
         closure[:, span] = dot(out_all[...], second)[:8]
-        second_grad = times_slope(dot(out_back[...], grad_out[:, span]), second)
+        second_grad = times_slope(seed[:, span], second)
         second_grad_out[:, span] = second_grad
         first_grad = times_slope(dot(mid_back[...], second_grad), first)
         first_grad_out[:, span] = first_grad
@@ -442,18 +459,18 @@
         return jnp.concatenate([block, blank], axis=1).T
 
     low, high = turned(wing[:hidden]), turned(wing[hidden:])
-    pieces = [mid[:, :hidden]]
-    for kind in range(3):
-        span = slice(8 * kind, 8 * kind + 8)
-        pieces.append(low[span] + pltpu.roll(high[span], 4, 0))
+    kinds = [low[8 * k : 8 * k + 8] + pltpu.roll(high[8 * k : 8 * k + 8], 4, 0) for k in range(3)]
     bias_in = low[24:32] + high[24:32]
     bias_mid = turned(mid[:, hidden:])[:8]
-    pieces.append(jnp.where(top == 0, bias_in, pltpu.roll(bias_mid, 1, 0)))
+    biases = jnp.where(top == 4, pltpu.roll(bias_in, 4, 0), pltpu.roll(bias_mid, 5, 0))
     low, high = turned(out[:hidden]), turned(out[hidden:])
-    pieces.append(
-        jnp.where(top < 4, low[:8] + pltpu.roll(high[:8], 4, 0), total + pltpu.roll(total, 4, 0))
-    )
-    pieces.append(jnp.zeros((8, hidden), F32))
+    pieces = [
+        mid[:, :hidden],
+        jnp.where(top < 4, kinds[0], pltpu.roll(kinds[1], 4, 0)),
+        jnp.where(top < 4, kinds[2], biases),
+        jnp.where(top < 4, low[:8] + pltpu.roll(high[:8], 4, 0), total + pltpu.roll(total, 4, 0)),
+        jnp.zeros((8, hidden), F32),
+    ]
     packed = jnp.concatenate(pieces, axis=0)
     half = packed.shape[0] // 2
     core = lax.axis_index("sub")
@@ -461,14 +478,15 @@
     send[...] = jnp.where(core == 0, packed[half:], packed[:half])
 
 
-def finish_kernel(base_in, mask, x_in, above, below, partner, codes, rows, *rest):
-    pools = rest[:-2]
-    final, initial = rest[-2:]
+def finish_kernel(skip, base_in, mask, x_in, above, below, partner, codes, rows, *rest):
+    pools = rest[:-3]
+    final, initial, token = rest[-3:]
+    token[...] = jnp.zeros(token.shape, F32)
     slots = partner.shape[0]
     total = base_in.shape[1]
     cells = total // slots
     mv = wide(rows[1], total // LANES)
-    halos = halo_fields(codes, pools, partner, slots, cells)
+    halos = halo_fields(codes, pools, partner, slots, cells, skip)
     last = x_in[...] + mask[...] * (mv * level_halo(above, below, 0))
     early = mask[...] * ((base_in[...] + level_halo(above, below, 1)) + halo_sum(halos, cells))
     for s in range(slots):
@@ -480,7 +498,7 @@
                 initial[f, l, s : s + 1, :] = early[r : r + 1, span]
 
 
-def grads_kernel(scale, mine, other, w_in, b_in, w_mid, b_mid, w_out, b_out):
+def grads_kernel(scale, mine, other, token, w_in, b_in, w_mid, b_mid, w_out, b_out):
     hidden = w_mid.shape[0]
     core = lax.axis_index("sub")
     low = jnp.where(core == 0, mine[...], other[...])
@@ -488,26 +506,26 @@
     packed = jnp.concatenate([low, high], axis=0) * scale
     w_mid[...] = packed[:hidden]
     tail = packed[hidden:]
-    w_in[0:4] = tail[0:4]
-    w_in[4:8] = tail[8:12]
-    w_in[8:12] = tail[16:20]
-    b_in[...] = tail[24:25]
-    b_mid[...] = tail[25:26]
-    w_out[...] = tail[32:36]
-    sums = jnp.broadcast_to(jnp.sum(tail[36:40], axis=1, keepdims=True), (4, hidden))
-    spot = iota((4, hidden), 0) == iota((4, hidden), 1)
-    b_out[...] = jnp.sum(jnp.where(spot, sums, 0.0), axis=0, keepdims=True)
-
-
-def call(kernel, inputs, outs, scratch=(), spaces=None):
+    w_in[...] = tail[0:12]
+    b_in[...] = tail[12:13]
+    b_mid[...] = tail[13:14]
+    w_out[...] = tail[16:20]
+    for f in range(4):
+        b_out[f] = jnp.sum(tail[20 + f : 21 + f])
+
+
+def call(kernel, inputs, outs, scratch=(), spaces=None, scalars=0):
+    if spaces is not None:
+        inputs = [pltpu.with_memory_space_constraint(array, spaces) for array in inputs]
     return pl.pallas_call(
         kernel,
         in_specs=[pl.BlockSpec(memory_space=spaces or pltpu.VMEM)] * len(inputs),
-        out_specs=[pl.BlockSpec(memory_space=pltpu.VMEM)] * len(outs),
+        out_specs=[pl.BlockSpec(memory_space=pltpu.VMEM)] * (len(outs) - scalars)
+        + [pl.BlockSpec(memory_space=pltpu.SMEM)] * scalars,
         out_shape=outs,
         scratch_shapes=list(scratch),
         compiler_params=pltpu.CompilerParams(vmem_limit_bytes=VMEM_BYTES),
-    )(*(inputs if spaces is None else [pltpu.with_memory_space_constraint(a, spaces) for a in inputs]))
+    )(*inputs)
 
 
 def shape(dims, dtype=F32):
@@ -569,13 +587,14 @@
     mix_horizontal,
     mix_vertical,
 ):
-    fields, levels, slots, cells = state_init.shape
+    _, levels, slots, cells = state_init.shape
     hidden = weight_mid.shape[0]
     both = 2 * hidden
     total = slots * cells
     peers = lax.axis_size("tiles")
     field = shape((8, total))
-    pack = shape((slots, 8, LANES))
+    column_pack = shape((slots // 2, 8, LANES))
+    line_pack = shape((slots, 8, LANES))
     sends = [shape((2, slots // 2, 8, cells))] * (1 if lax.axis_size("depth") == 2 else 2)
     hidden_rows = shape((both, total), BF)
     first_rows = shape((both + 32, total), BF)
@@ -585,7 +604,7 @@
     x_zero, g_late, mask, columns, lines, *levels_out = call(
         functools.partial(prep_kernel, len(sends)),
         inputs,
-        [field, field, field, pack, pack] + sends,
+        [field, field, field, column_pack, line_pack] + sends,
         [
             smem(mix_vertical.shape, F32),
             vmem(state_init.shape, F32),
@@ -632,10 +651,12 @@
     forward_weights = [in_all, mid_all, mid_bias, out_all, rows]
     backward_weights = [out_back, mid_back, in_back]
 
+    late_grad, seed = call(seed_kernel, [g_late, out_back], [shape((16, total), BF), hidden_rows])
+
     x_one, first, second, features, columns, lines = call(
         functools.partial(forward_kernel, peers),
         [x_zero, mask, above, below, partner, codes] + forward_weights + pools,
-        [field, first_rows, hidden_rows, shape((32, total), BF), pack, pack],
+        [field, first_rows, hidden_rows, shape((32, total), BF), column_pack, line_pack],
         [vmem((8, total), F32)],
     )
     pools = from_peers(columns)
@@ -643,13 +664,13 @@
 
     x_two, base, columns, lines, late_sum, *late = call(
         functools.partial(turn_kernel, peers),
-        [x_one, mask, g_late, above, below, partner, codes]
+        [x_one, mask, g_late, seed, above, below, partner, codes]
         + forward_weights
-        + backward_weights
+        + backward_weights[1:]
         + pools,
         [
-            field, field, pack, pack, shape((8, LANES)), first_rows, hidden_rows,
-            shape((32, total), BF), shape((16, total), BF), hidden_rows, hidden_rows,
+            field, field, column_pack, line_pack, shape((8, LANES)), first_rows, hidden_rows,
+            shape((32, total), BF), hidden_rows, hidden_rows,
         ],
         [vmem((8, total), F32), vmem((32, total), F32)],
     )
@@ -657,35 +678,39 @@
     partner = from_partner(lines)
     late = call(
         late_terms_kernel,
-        late,
+        late[:3] + [late_grad] + late[3:],
         [shape((hidden, hidden + 16)), shape((both, 32)), shape((both, 16))],
     )
 
+    late, base = lax.optimization_barrier((late, base))
     base, columns, lines, early_sum, grad, second_grad, first_grad, *levels_out = call(
         functools.partial(back_kernel, peers),
         [base, mask, x_one, partner, codes, first, second, rows] + backward_weights + pools,
         [
-            field, pack, pack, shape((8, LANES)), shape((16, total), BF), hidden_rows, hidden_rows,
+            field, column_pack, line_pack, shape((8, LANES)), shape((16, total), BF), hidden_rows, hidden_rows,
         ]
         + sends,
         [vmem((32, total), F32)],
     )
     above, below = from_levels(levels_out)
-    pools = from_peers(columns)
     partner = from_partner(lines)
-    half = shape(((hidden + 48) // 2, hidden))
+    half = shape(((hidden + 32) // 2, hidden))
     keep, give = call(
         early_terms_kernel,
         [first, second, features, grad, second_grad, first_grad, *late, late_sum, early_sum],
         [half, half],
     )
     terms = keep + lax.ppermute(give, "sub", xor_pairs("sub", 1))
-    terms = sum_over(sum_over(terms, "depth"), "tiles")
-    final_state, initial_cot = call(
-        finish_kernel,
-        [base, mask, x_two, above, below, partner, codes, rows] + pools,
-        [shape(state_init.shape)] * 2,
-    )
+    terms, above, below, partner = lax.optimization_barrier((terms, above, below, partner))
+    parts = from_peers(jnp.concatenate([terms, columns.reshape(slots * 4, LANES)], axis=0))
+    terms = tree_sum([part[: half.shape[0]] for part in parts])
+    terms = sum_over(terms, "depth")
+    final_state, initial_cot, token = call(
+        functools.partial(finish_kernel, half.shape[0]),
+        [base, mask, x_two, above, below, partner, codes, rows] + parts,
+        [shape(state_init.shape)] * 2 + [shape((8, LANES))],
+    )
+    terms, token = lax.optimization_barrier((terms, token))
     count = (
         levels
         * lax.axis_size("depth")
@@ -696,15 +721,16 @@
     )
     w_in, b_in, w_mid, b_mid, w_out, b_out = call(
         functools.partial(grads_kernel, 1.0 / math.sqrt(count)),
-        [terms, lax.ppermute(terms, "sub", xor_pairs("sub", 1))],
+        [terms, lax.ppermute(terms, "sub", xor_pairs("sub", 1)), token],
         [
             shape(weight_in.T.shape),
             shape((1, hidden)),
             shape((hidden, hidden)),
             shape((1, hidden)),
             shape(weight_out.shape),
-            shape((1, hidden)),
+            shape(bias_out.shape),
         ],
+        scalars=1,
     )
     return (
         final_state,
@@ -714,7 +740,7 @@
         w_mid,
         b_mid.reshape(hidden),
         w_out,
-        b_out[0, :fields],
+        b_out,
     )
 
 

time: 68 us -> 62.1 us (0.913)
  starting transfers between devices: 28.1 us -> 24.2 us
  waiting for transfers between devices: 13.6 us -> 11.3 us
    ppermute x4 -> x1, starting transfers between devices: 5.98 us -> 1.29 us  [sum_over(): lax.ppermute(array, axis, xor_pairs(axis, k))]
    ppermute x4 -> x1, waiting for transfers between devices: 5.48 us -> 1.61 us  [sum_over(): lax.ppermute(array, axis, xor_pairs(axis, k))]
    ppermute x1, waiting for transfers between devices: 0.01 us -> 1.21 us  [body(): lax.ppermute(terms, 'sub', xor_pairs('sub', 1))]
    pallas_call x9 -> x10, Pallas kernels: 24.8 us -> 25.3 us  [call(): pl.pallas_call(kernel, in_specs=[pl.BlockSpec(memory_space=spaces or pltp...]
  transfers between devices with their start and end apart: 24 -> 21, of which waited for: 11 -> 9; matrix products, arithmetic and copies ran while one was open for 1% -> 0% of each run, Pallas kernels for 8% -> 18%
where the time goes in v2:
time: 62.1 us; the launch traced here: 61.9 us
  Pallas kernels  25.3 us (41%)
  starting transfers between devices  24.2 us (39%)
  waiting for transfers between devices  11.3 us (18%)
  between operations  0.95 us (2%)
    pallas_call x10, Pallas kernels, call(): pl.pallas_call(kernel, in_specs=[pl.BlockSpec(memory_space=spaces or pltp...  25.3 us
    ppermute x12, starting transfers between devices, from_peers(): lax.ppermute(packs, 'tiles', xor_pairs('tiles', k))  17.7 us
    ppermute x12, waiting for transfers between devices, from_peers(): lax.ppermute(packs, 'tiles', xor_pairs('tiles', k))  6.4 us
    ppermute x2, starting transfers between devices, from_levels(): other = lax.ppermute(sends[0], 'depth', [(0, 1), (1, 0)])  4.57 us
    ppermute x1, waiting for transfers between devices, sum_over(): lax.ppermute(array, axis, xor_pairs(axis, k))  1.61 us
    ppermute x1, starting transfers between devices, sum_over(): lax.ppermute(array, axis, xor_pairs(axis, k))  1.29 us
    ppermute x2, waiting for transfers between devices, from_levels(): other = lax.ppermute(sends[0], 'depth', [(0, 1), (1, 0)])  1.29 us
  transfers between devices with their start and end apart: 21, of which 9 were waited for; matrix products, arithmetic and copies ran while one was open for 0% of the time, Pallas kernels for 18%

profile of v2, /device:TPU:0, one launch (start us, length us, event | category | flops | bytes accessed | tf_op | source)
XLA Modules:
  0.0 61.9 jit_solution(6004119378258188887)
XLA Ops:
  0.6 1.4 %shard_map.188 = (f32[8,8192]{1,0:T(8,128)S(1)}, f32[8,8192]{1,0:T(8,128)S(1)}, f32[8,8192]{1,0:T(8,128)S(1)}, f32[2,8,128]{2,1,0:T(8,128)S(1)}, f32[4,8,128]{2,...) custom-call(f32[2]{0:T(128)} %mix_v_in.3, f32[4,2,4,2048]{3,2,1,0:T(4,128)} %state_in.1, f32[4,2,4,2048]{3,2,1,0:T(4,128)} %cot_in.1, ...), custom_call_target="tpu_custom_call" | custom-call | tf_op jit(solution)/shard_map/pallas_call | solution.py:520
  2.0 3.0 %collective-permute-start = (f32[2,2,8,2048]{3,2,1,0:T(8,128)S(1)}, f32[2,2,8,2048]{3,2,1,0:T(8,128)S(1)}, u32[]{:S(2)}, u32[]{:S(2)}) collective-permute-start(f32[2,2,8,2048]{3,2,1,0:T(8,128)S(1)} %get-tuple-element.75), channel_id=1, source_target_pairs={{0,2},{2,0},{1,3},{3,1},{4,6},{6,4},{5,7},{7,5},{8,10},{10,8},{9,1... | collective-permute-start | bytes 786440 | tf_op jit(solution)/shard_map/ppermute | solution.py:553
  5.0 3.6 %collective-permute-start.4 = (f32[2,8,128]{2,1,0:T(8,128)S(1)}, f32[2,8,128]{2,1,0:T(8,128)S(1)}, u32[]{:S(2)}, u32[]{:S(2)}) collective-permute-start(f32[2,8,128]{2,1,0:T(8,128)S(1)} %get-tuple-element.83.rest_0_), channel_id=1, source_target_pairs={{0,12},{4,8},{8,4},{12,0},{1,13},{5,9},{9,5},{13,1},{2,14},{6,10},... | collective-permute-start | bytes 24584 | tf_op jit(solution)/shard_map/ppermute | solution.py:541
  9.4 1.1 %shard_map.189 = (bf16[256,32]{1,0:T(8,128)(2,1)S(1)}, bf16[32,256]{1,0:T(8,128)(2,1)S(1)}, bf16[256,256]{1,0:T(8,128)(2,1)S(1)}, bf16[256,256]{1,0:T(8,128)(2,1...) custom-call(f32[4]{0:T(128)} %mix_h_in.1, ...), custom_call_target="tpu_custom_call" | custom-call | tf_op jit(solution)/shard_map/pallas_call | solution.py:520
  10.6 2.6 %collective-permute-done.3.rest_2_ = f32[2,8,128]{2,1,0:T(8,128)S(1)} collective-permute-done((f32[2,8,128]{2,1,0:T(8,128)S(1)}, f32[2,8,128]{2,1,0:T(8,128)S(1)}, u32[]{:S(2)}, u32[]{:S(2)}) %collective-permute-start.3) | collective-permute-done | bytes 8224 | tf_op jit(solution)/shard_map/ppermute | solution.py:541
  13.2 3.3 %shard_map.190 = (f32[8,8192]{1,0:T(8,128)S(1)}, bf16[288,8192]{1,0:T(8,128)(2,1)S(1)}, bf16[256,8192]{1,0:T(8,128)(2,1)S(1)}, bf16[32,8192]{1,0:T(8,128)(2,1)S(...) custom-call(f32[8,8192]{1,0:T(8,128)S(1)} %get-tuple-element.73.x_in, f32[8,8192]{1,0:T(8,128)S(1)} %get-tuple-element.74.mask, ...), custom_call_target="tpu_custom_call" | custom-call | tf_op jit(solution)/shard_map/pallas_call | solution.py:520
  16.6 2.0 %collective-permute-start.8 = (f32[2,8,128]{2,1,0:T(8,128)S(1)}, f32[2,8,128]{2,1,0:T(8,128)S(1)}, u32[]{:S(2)}, u32[]{:S(2)}) collective-permute-start(f32[2,8,128]{2,1,0:T(8,128)S(1)} %get-tuple-element.91.rest_0_), channel_id=1, source_target_pairs={{0,12},{4,8},{8,4},{12,0},{1,13},{5,9},{9,5},{13,1},{2,14},{6,10},... | collective-permute-start | bytes 24584 | tf_op jit(solution)/shard_map/ppermute | solution.py:541
  18.8 2.3 %collective-permute-start.6 = (f32[2,8,128]{2,1,0:T(8,128)S(1)}, f32[2,8,128]{2,1,0:T(8,128)S(1)}, u32[]{:S(2)}, u32[]{:S(2)}) collective-permute-start(f32[2,8,128]{2,1,0:T(8,128)S(1)} %get-tuple-element.91.rest_0_), channel_id=1, source_target_pairs={{0,4},{4,0},{8,12},{12,8},{1,5},{5,1},{9,13},{13,9},{2,6},{6,2},{1... | collective-permute-start | bytes 24584 | tf_op jit(solution)/shard_map/ppermute | solution.py:541
  21.1 1.2 %shard_map.191 = (bf16[16,8192]{1,0:T(8,128)(2,1)S(1)}, bf16[256,8192]{1,0:T(8,128)(2,1)S(1)}) custom-call(f32[8,8192]{1,0:T(8,128)S(1)} %get-tuple-element.85.g_in, bf16[256,16]{1,0:T(8,128)(2,1)S(1)} %get-tuple-element.86.out_back), custom_call_target="tpu_custom_call" | custom-call | tf_op jit(solution)/shard_map/pallas_call | solution.py:520
  23.2 5.6 %shard_map.192 = (f32[8,8192]{1,0:T(8,128)S(1)}, f32[8,8192]{1,0:T(8,128)S(1)}, f32[2,8,128]{2,1,0:T(8,128)S(1)}, f32[4,8,128]{2,1,0:T(8,128)S(1)}, f32[8,128]{1...) custom-call(f32[8,8192]{1,0:T(8,128)S(1)} %get-tuple-element.84.x_in, ...), custom_call_target="tpu_custom_call" | custom-call | tf_op jit(solution)/shard_map/pallas_call | solution.py:520
  29.0 2.1 %collective-permute-start.12 = (f32[2,8,128]{2,1,0:T(8,128)S(1)}, f32[2,8,128]{2,1,0:T(8,128)S(1)}, u32[]{:S(2)}, u32[]{:S(2)}) collective-permute-start(f32[2,8,128]{2,1,0:T(8,128)S(1)} %get-tuple-element.106.rest_0_), channel_id=1, source_target_pairs={{0,12},{4,8},{8,4},{12,0},{1,13},{5,9},{9,5},{13,1},{2,14},{6,10},... | collective-permute-start | bytes 24584 | tf_op jit(solution)/shard_map/ppermute | solution.py:541
  32.0 1.4 %collective-permute-start.10 = (f32[2,8,128]{2,1,0:T(8,128)S(1)}, f32[2,8,128]{2,1,0:T(8,128)S(1)}, u32[]{:S(2)}, u32[]{:S(2)}) collective-permute-start(f32[2,8,128]{2,1,0:T(8,128)S(1)} %get-tuple-element.106.rest_0_), channel_id=1, source_target_pairs={{0,4},{4,0},{8,12},{12,8},{1,5},{5,1},{9,13},{13,9},{2,6},{6,2},{1... | collective-permute-start | bytes 24584 | tf_op jit(solution)/shard_map/ppermute | solution.py:541
  33.4 3.7 %shard_map.193 = (f32[128,144]{1,0:T(8,128)S(1)}, f32[256,32]{1,0:T(8,128)S(1)}, f32[256,16]{1,0:T(8,128)S(1)}) custom-call(bf16[288,8192]{1,0:T(8,128)(2,1)S(1)} %get-tuple-element.92.refs_0_, bf16[256,8192]{1,0:T(8,128)(2,1)S(1)} %get-tuple-element.93.refs_1_, bf16[32,8192]{1,0:T(8,128)(2,1)S(1)} %get-tuple-element.94.refs_2_, ...), custom_call_target="tpu_custom_call" | custom-call | tf_op jit(solution)/shard_map/pallas_call | solution.py:520
  37.2 3.4 %shard_map.194 = (f32[8,8192]{1,0:T(8,128)S(1)}, f32[2,8,128]{2,1,0:T(8,128)S(1)}, f32[4,8,128]{2,1,0:T(8,128)S(1)}, f32[8,128]{1,0:T(8,128)S(1)}, bf16[16,8192]...) custom-call(f32[8,8192]{1,0:T(8,128)S(1)} %get-tuple-element.102.bas, ...), custom_call_target="tpu_custom_call" | custom-call | tf_op jit(solution)/shard_map/pallas_call | solution.py:520
  40.6 1.6 %collective-permute-start.14 = (f32[2,2,8,2048]{3,2,1,0:T(8,128)S(1)}, f32[2,2,8,2048]{3,2,1,0:T(8,128)S(1)}, u32[]{:S(2)}, u32[]{:S(2)}) collective-permute-start(f32[2,2,8,2048]{3,2,1,0:T(8,128)S(1)} %get-tuple-element.120), channel_id=1, source_target_pairs={{0,2},{2,0},{1,3},{3,1},{4,6},{6,4},{5,7},{7,5},{8,10},{10,8},{9,1... | collective-permute-start | bytes 786440 | tf_op jit(solution)/shard_map/ppermute | solution.py:553
  42.2 3.6 %shard_map.195 = (f32[80,128]{1,0:T(8,128)S(1)}, f32[80,128]{1,0:T(8,128)S(1)}) custom-call(bf16[288,8192]{1,0:T(8,128)(2,1)S(1)} %get-tuple-element.104.first_in.refs_0_, bf16[256,8192]{1,0:T(8,128)(2,1)S(1)} %get-tuple-element.105.second_in.refs_1_, bf16[32,8192]{1,0:T(8,128)(2,1)S(1)} %get-tuple-element.109.refs_2_, ...), custom_call_target="tpu_custom_call" | custom-call | tf_op jit(solution)/shard_map/pallas_call | solution.py:520
  47.2 1.3 %collective-permute-done.14.above.below = f32[2,2,8,2048]{3,2,1,0:T(8,128)S(1)} collective-permute-done((f32[2,2,8,2048]{3,2,1,0:T(8,128)S(1)}, f32[2,2,8,2048]{3,2,1,0:T(8,128)S(1)}, u32[]{:S(2)}, u32[]{:S(2)}) %collective-permute-start.14) | collective-permute-done | bytes 262176 | tf_op jit(solution)/shard_map/ppermute | solution.py:553
  48.5 2.1 %collective-permute-start.18 = (f32[96,128]{1,0:T(8,128)S(1)}, f32[96,128]{1,0:T(8,128)S(1)}, u32[]{:S(2)}, u32[]{:S(2)}) collective-permute-start(f32[96,128]{1,0:T(8,128)S(1)} %pad_maximum_fusion.rest_0_), channel_id=1, source_target_pairs={{0,12},{4,8},{8,4},{12,0},{1,13},{5,9},{9,5},{13,1},{2,14},{6,10},... | collective-permute-start | bytes 147464 | tf_op jit(solution)/shard_map/ppermute | solution.py:541
  50.6 2.3 %collective-permute-start.16 = (f32[96,128]{1,0:T(8,128)S(1)}, f32[96,128]{1,0:T(8,128)S(1)}, u32[]{:S(2)}, u32[]{:S(2)}) collective-permute-start(f32[96,128]{1,0:T(8,128)S(1)} %pad_maximum_fusion.rest_0_), channel_id=1, source_target_pairs={{0,4},{4,0},{8,12},{12,8},{1,5},{5,1},{9,13},{13,9},{2,6},{6,2},{1... | collective-permute-start | bytes 147464 | tf_op jit(solution)/shard_map/ppermute | solution.py:541
  52.9 1.8 %collective-permute-done.18.rest_3_ = f32[96,128]{1,0:T(8,128)S(1)} collective-permute-done((f32[96,128]{1,0:T(8,128)S(1)}, f32[96,128]{1,0:T(8,128)S(1)}, u32[]{:S(2)}, u32[]{:S(2)}) %collective-permute-start.18) | collective-permute-done | bytes 49184 | tf_op jit(solution)/shard_map/ppermute | solution.py:541
  55.8 1.3 %collective-permute-start.19 = (f32[80,128]{1,0:T(8,128)S(1)}, f32[80,128]{1,0:T(8,128)S(1)}, u32[]{:S(2)}, u32[]{:S(2)}) collective-permute-start(f32[80,128]{1,0:T(8,128)S(1)} %fusion), channel_id=1, source_target_pairs={{0,2},{2,0},{1,3},{3,1},{4,6},{6,4},{5,7},{7,5},{8,10},{10,8},{9,1... | collective-permute-start | bytes 122888 | tf_op jit(solution)/shard_map/ppermute | solution.py:571
  57.1 1.2 %shard_map.196 = (f32[4,2,4,2048]{3,2,1,0:T(4,128)}, f32[4,2,4,2048]{3,2,1,0:T(4,128)}, f32[8,128]{1,0:T(8,128)S(1)}) custom-call(f32[8,8192]{1,0:T(8,128)S(1)} %get-tuple-element.107.base_in, f32[8,8192]{1,0:T(8,128)S(1)} %get-tuple-element.74.mask, f32[8,8192]{1,0:T(8,128)S(1)} %get-tuple-element.108.x_in, ...), custom_call_target="tpu_custom_call" | custom-call | tf_op jit(solution)/shard_map/pallas_call | solution.py:520
  58.2 1.6 %collective-permute-done.19 = f32[80,128]{1,0:T(8,128)S(1)} collective-permute-done((f32[80,128]{1,0:T(8,128)S(1)}, f32[80,128]{1,0:T(8,128)S(1)}, u32[]{:S(2)}, u32[]{:S(2)}) %collective-permute-start.19) | collective-permute-done | bytes 40992 | tf_op jit(solution)/shard_map/ppermute | solution.py:571
  59.9 1.2 %collective-permute-done.20.other = f32[80,128]{1,0:T(8,128)S(1)} collective-permute-done((f32[80,128]{1,0:T(8,128)S(1)}, f32[80,128]{1,0:T(8,128)S(1)}, u32[]{:S(2)}, u32[]{:S(2)}) %collective-permute-start.20) | collective-permute-done | bytes 40992 | tf_op jit(solution)/shard_map/ppermute | solution.py:724
  (32 shorter events, 6.0 us)
Async XLA Ops:
  2.0 11.2 %collective-permute-start = (f32[2,2,8,2048]{3,2,1,0:T(8,128)S(1)}, f32[2,2,8,2048]{3,2,1,0:T(8,128)S(1)}, u32[]{:S(2)}, u32[]{:S(2)}) collective-permute-start(f32[2,2,8,2048]{3,2,1,0:T(8,128)S(1)} %get-tuple-element.75), channel_id=1, source_target_pairs={{0,2},{2,0},{1,3},{3,1},{4,6},{6,4},{5,7},{7,5},{8,10},{10,8},{9,1... | collective-permute-start | bytes 786440 | tf_op jit(solution)/shard_map/ppermute | solution.py:553
  5.0 8.2 %collective-permute-start.1 = (f32[4,8,128]{2,1,0:T(8,128)S(1)}, f32[4,8,128]{2,1,0:T(8,128)S(1)}, u32[]{:S(2)}, u32[]{:S(2)}) collective-permute-start(f32[4,8,128]{2,1,0:T(8,128)S(1)} %get-tuple-element.76), channel_id=1, source_target_pairs={{0,1},{1,0},{2,3},{3,2},{4,5},{5,4},{6,7},{7,6},{8,9},{9,8},{10,11... | collective-permute-start | bytes 49160 | tf_op jit(solution)/shard_map/ppermute | solution.py:547
  5.0 5.5 %collective-permute-start.4 = (f32[2,8,128]{2,1,0:T(8,128)S(1)}, f32[2,8,128]{2,1,0:T(8,128)S(1)}, u32[]{:S(2)}, u32[]{:S(2)}) collective-permute-start(f32[2,8,128]{2,1,0:T(8,128)S(1)} %get-tuple-element.83.rest_0_), channel_id=1, source_target_pairs={{0,12},{4,8},{8,4},{12,0},{1,13},{5,9},{9,5},{13,1},{2,14},{6,10},... | collective-permute-start | bytes 24584 | tf_op jit(solution)/shard_map/ppermute | solution.py:541
  8.6 4.5 %collective-permute-start.3 = (f32[2,8,128]{2,1,0:T(8,128)S(1)}, f32[2,8,128]{2,1,0:T(8,128)S(1)}, u32[]{:S(2)}, u32[]{:S(2)}) collective-permute-start(f32[2,8,128]{2,1,0:T(8,128)S(1)} %get-tuple-element.83.rest_0_), channel_id=1, source_target_pairs={{0,8},{4,12},{8,0},{12,4},{1,9},{5,13},{9,1},{13,5},{2,10},{6,14},... | collective-permute-start | bytes 24584 | tf_op jit(solution)/shard_map/ppermute | solution.py:541
  8.6 4.5 %collective-permute-start.2 = (f32[2,8,128]{2,1,0:T(8,128)S(1)}, f32[2,8,128]{2,1,0:T(8,128)S(1)}, u32[]{:S(2)}, u32[]{:S(2)}) collective-permute-start(f32[2,8,128]{2,1,0:T(8,128)S(1)} %get-tuple-element.83.rest_0_), channel_id=1, source_target_pairs={{0,4},{4,0},{8,12},{12,8},{1,5},{5,1},{9,13},{13,9},{2,6},{6,2},{1... | collective-permute-start | bytes 24584 | tf_op jit(solution)/shard_map/ppermute | solution.py:541
  16.5 6.7 %collective-permute-start.5 = (f32[4,8,128]{2,1,0:T(8,128)S(1)}, f32[4,8,128]{2,1,0:T(8,128)S(1)}, u32[]{:S(2)}, u32[]{:S(2)}) collective-permute-start(f32[4,8,128]{2,1,0:T(8,128)S(1)} %get-tuple-element.88), channel_id=1, source_target_pairs={{0,1},{1,0},{2,3},{3,2},{4,5},{5,4},{6,7},{7,6},{8,9},{9,8},{10,11... | collective-permute-start | bytes 49160 | tf_op jit(solution)/shard_map/ppermute | solution.py:547
  16.6 5.7 %collective-permute-start.8 = (f32[2,8,128]{2,1,0:T(8,128)S(1)}, f32[2,8,128]{2,1,0:T(8,128)S(1)}, u32[]{:S(2)}, u32[]{:S(2)}) collective-permute-start(f32[2,8,128]{2,1,0:T(8,128)S(1)} %get-tuple-element.91.rest_0_), channel_id=1, source_target_pairs={{0,12},{4,8},{8,4},{12,0},{1,13},{5,9},{9,5},{13,1},{2,14},{6,10},... | collective-permute-start | bytes 24584 | tf_op jit(solution)/shard_map/ppermute | solution.py:541
  18.7 4.6 %collective-permute-start.7 = (f32[2,8,128]{2,1,0:T(8,128)S(1)}, f32[2,8,128]{2,1,0:T(8,128)S(1)}, u32[]{:S(2)}, u32[]{:S(2)}) collective-permute-start(f32[2,8,128]{2,1,0:T(8,128)S(1)} %get-tuple-element.91.rest_0_), channel_id=1, source_target_pairs={{0,8},{4,12},{8,0},{12,4},{1,9},{5,13},{9,1},{13,5},{2,10},{6,14},... | collective-permute-start | bytes 24584 | tf_op jit(solution)/shard_map/ppermute | solution.py:541
  18.8 4.4 %collective-permute-start.6 = (f32[2,8,128]{2,1,0:T(8,128)S(1)}, f32[2,8,128]{2,1,0:T(8,128)S(1)}, u32[]{:S(2)}, u32[]{:S(2)}) collective-permute-start(f32[2,8,128]{2,1,0:T(8,128)S(1)} %get-tuple-element.91.rest_0_), channel_id=1, source_target_pairs={{0,4},{4,0},{8,12},{12,8},{1,5},{5,1},{9,13},{13,9},{2,6},{6,2},{1... | collective-permute-start | bytes 24584 | tf_op jit(solution)/shard_map/ppermute | solution.py:541
  28.9 8.3 %collective-permute-start.9 = (f32[4,8,128]{2,1,0:T(8,128)S(1)}, f32[4,8,128]{2,1,0:T(8,128)S(1)}, u32[]{:S(2)}, u32[]{:S(2)}) collective-permute-start(f32[4,8,128]{2,1,0:T(8,128)S(1)} %get-tuple-element.103), channel_id=1, source_target_pairs={{0,1},{1,0},{2,3},{3,2},{4,5},{5,4},{6,7},{7,6},{8,9},{9,8},{10,11... | collective-permute-start | bytes 49160 | tf_op jit(solution)/shard_map/ppermute | solution.py:547
  29.0 8.2 %collective-permute-start.12 = (f32[2,8,128]{2,1,0:T(8,128)S(1)}, f32[2,8,128]{2,1,0:T(8,128)S(1)}, u32[]{:S(2)}, u32[]{:S(2)}) collective-permute-start(f32[2,8,128]{2,1,0:T(8,128)S(1)} %get-tuple-element.106.rest_0_), channel_id=1, source_target_pairs={{0,12},{4,8},{8,4},{12,0},{1,13},{5,9},{9,5},{13,1},{2,14},{6,10},... | collective-permute-start | bytes 24584 | tf_op jit(solution)/shard_map/ppermute | solution.py:541
  31.1 6.0 %collective-permute-start.11 = (f32[2,8,128]{2,1,0:T(8,128)S(1)}, f32[2,8,128]{2,1,0:T(8,128)S(1)}, u32[]{:S(2)}, u32[]{:S(2)}) collective-permute-start(f32[2,8,128]{2,1,0:T(8,128)S(1)} %get-tuple-element.106.rest_0_), channel_id=1, source_target_pairs={{0,8},{4,12},{8,0},{12,4},{1,9},{5,13},{9,1},{13,5},{2,10},{6,14},... | collective-permute-start | bytes 24584 | tf_op jit(solution)/shard_map/ppermute | solution.py:541
  32.0 5.2 %collective-permute-start.10 = (f32[2,8,128]{2,1,0:T(8,128)S(1)}, f32[2,8,128]{2,1,0:T(8,128)S(1)}, u32[]{:S(2)}, u32[]{:S(2)}) collective-permute-start(f32[2,8,128]{2,1,0:T(8,128)S(1)} %get-tuple-element.106.rest_0_), channel_id=1, source_target_pairs={{0,4},{4,0},{8,12},{12,8},{1,5},{5,1},{9,13},{13,9},{2,6},{6,2},{1... | collective-permute-start | bytes 24584 | tf_op jit(solution)/shard_map/ppermute | solution.py:541
  40.6 7.9 %collective-permute-start.14 = (f32[2,2,8,2048]{3,2,1,0:T(8,128)S(1)}, f32[2,2,8,2048]{3,2,1,0:T(8,128)S(1)}, u32[]{:S(2)}, u32[]{:S(2)}) collective-permute-start(f32[2,2,8,2048]{3,2,1,0:T(8,128)S(1)} %get-tuple-element.120), channel_id=1, source_target_pairs={{0,2},{2,0},{1,3},{3,1},{4,6},{6,4},{5,7},{7,5},{8,10},{10,8},{9,1... | collective-permute-start | bytes 786440 | tf_op jit(solution)/shard_map/ppermute | solution.py:553
  45.8 1.3 %collective-permute-start.13 = (f32[80,128]{1,0:T(8,128)S(1)}, f32[80,128]{1,0:T(8,128)S(1)}, u32[]{:S(2)}, u32[]{:S(2)}) collective-permute-start(f32[80,128]{1,0:T(8,128)S(1)} %get-tuple-element.119), channel_id=1, source_target_pairs={{0,1},{1,0},{2,3},{3,2},{4,5},{5,4},{6,7},{7,6},{8,9},{9,8},{10,11... | collective-permute-start | bytes 122888 | tf_op jit(solution)/shard_map/ppermute | solution.py:703
  45.9 1.3 %collective-permute-start.15 = (f32[4,8,128]{2,1,0:T(8,128)S(1)}, f32[4,8,128]{2,1,0:T(8,128)S(1)}, u32[]{:S(2)}, u32[]{:S(2)}) collective-permute-start(f32[4,8,128]{2,1,0:T(8,128)S(1)} %get-tuple-element.121), channel_id=1, source_target_pairs={{0,1},{1,0},{2,3},{3,2},{4,5},{5,4},{6,7},{7,6},{8,9},{9,8},{10,11... | collective-permute-start | bytes 49160 | tf_op jit(solution)/shard_map/ppermute | solution.py:547
  48.5 6.2 %collective-permute-start.18 = (f32[96,128]{1,0:T(8,128)S(1)}, f32[96,128]{1,0:T(8,128)S(1)}, u32[]{:S(2)}, u32[]{:S(2)}) collective-permute-start(f32[96,128]{1,0:T(8,128)S(1)} %pad_maximum_fusion.rest_0_), channel_id=1, source_target_pairs={{0,12},{4,8},{8,4},{12,0},{1,13},{5,9},{9,5},{13,1},{2,14},{6,10},... | collective-permute-start | bytes 147464 | tf_op jit(solution)/shard_map/ppermute | solution.py:541
  50.6 5.2 %collective-permute-start.17 = (f32[96,128]{1,0:T(8,128)S(1)}, f32[96,128]{1,0:T(8,128)S(1)}, u32[]{:S(2)}, u32[]{:S(2)}) collective-permute-start(f32[96,128]{1,0:T(8,128)S(1)} %pad_maximum_fusion.rest_0_), channel_id=1, source_target_pairs={{0,8},{4,12},{8,0},{12,4},{1,9},{5,13},{9,1},{13,5},{2,10},{6,14},... | collective-permute-start | bytes 147464 | tf_op jit(solution)/shard_map/ppermute | solution.py:541
  50.6 5.2 %collective-permute-start.16 = (f32[96,128]{1,0:T(8,128)S(1)}, f32[96,128]{1,0:T(8,128)S(1)}, u32[]{:S(2)}, u32[]{:S(2)}) collective-permute-start(f32[96,128]{1,0:T(8,128)S(1)} %pad_maximum_fusion.rest_0_), channel_id=1, source_target_pairs={{0,4},{4,0},{8,12},{12,8},{1,5},{5,1},{9,13},{13,9},{2,6},{6,2},{1... | collective-permute-start | bytes 147464 | tf_op jit(solution)/shard_map/ppermute | solution.py:541
  55.8 4.1 %collective-permute-start.19 = (f32[80,128]{1,0:T(8,128)S(1)}, f32[80,128]{1,0:T(8,128)S(1)}, u32[]{:S(2)}, u32[]{:S(2)}) collective-permute-start(f32[80,128]{1,0:T(8,128)S(1)} %fusion), channel_id=1, source_target_pairs={{0,2},{2,0},{1,3},{3,1},{4,6},{6,4},{5,7},{7,5},{8,10},{10,8},{9,1... | collective-permute-start | bytes 122888 | tf_op jit(solution)/shard_map/ppermute | solution.py:571
  59.8 1.2 %collective-permute-start.20 = (f32[80,128]{1,0:T(8,128)S(1)}, f32[80,128]{1,0:T(8,128)S(1)}, u32[]{:S(2)}, u32[]{:S(2)}) collective-permute-start(f32[80,128]{1,0:T(8,128)S(1)} %add.19.mine), channel_id=1, source_target_pairs={{0,1},{1,0},{2,3},{3,2},{4,5},{5,4},{6,7},{7,6},{8,9},{9,8},{10,11... | collective-permute-start | bytes 122888 | tf_op jit(solution)/shard_map/ppermute | solution.py:724

commit v3 on v2

--- a/solution.py
+++ b/solution.py
@@ -345,7 +345,6 @@
     )
     sums = [g[:, v * LANES : (v + 1) * LANES] for v in range(many)]
     g_sum[...] = tree_sum(sums)
-    return spread
 
 
 def grad_rows(g):
@@ -402,22 +401,27 @@
     return grad.astype(BF) * (1.0 - value * value)
 
 
-def back_kernel(
-    peers, base_in, mask, x_in, partner, codes, first_in, second_in, rows, out_back, mid_back,
-    in_back, *rest
-):
+def arrive_kernel(peers, base_in, mask, x_in, partner, codes, rows, *rest):
     pools = rest[:peers]
-    base, columns, lines, g_sum, grad_out, second_grad_out, first_grad_out = rest[
-        peers : peers + 7
-    ]
-    sends = rest[peers + 7 : -1]
-    grad_feature = rest[-1]
+    g_out = rest[peers]
+    sends = rest[peers + 1 :]
     slots = partner.shape[0]
     total = base_in.shape[1]
     cells = total // slots
-    hidden = mid_back.shape[0] // 2
     halos = halo_fields(codes, pools, partner, slots, cells)
     g = mask[...] * (base_in[...] + halo_sum(halos, cells))
+    g_out[...] = g
+    write_sends(sends, 0, x_in[...], cells)
+    write_sends(sends, 1, wide(rows[1], total // LANES) * g, cells)
+
+
+def back_kernel(
+    g_in, first_in, second_in, rows, out_back, mid_back, in_back, base, columns, lines, g_sum,
+    grad_out, second_grad_out, first_grad_out, grad_feature
+):
+    g = g_in[...]
+    total = g.shape[1]
+    hidden = mid_back.shape[0] // 2
     grad_out[...] = grad_rows(g)
     for start in range(0, total, CHUNK):
         span = slice(start, start + CHUNK)
@@ -429,29 +433,43 @@
         first_grad = times_slope(dot(mid_back[...], second_grad), first)
         first_grad_out[:, span] = first_grad
         grad_feature[:, span] = dot(in_back[...], first_grad)
-    spread = backward_tail(g, grad_feature[...], None, rows, base, columns, lines, g_sum)
-    write_sends(sends, 0, x_in[...], cells)
-    write_sends(sends, 1, spread, cells)
-
-
-def term_sums(first, second, features, grad, second_grad, first_grad):
+    backward_tail(g, grad_feature[...], None, rows, base, columns, lines, g_sum)
+
+
+def middle_sums(first, second_grad):
     hidden = first.shape[0] // 2 - 16
     side = hidden + 16
-    mid = dot_nt(second_grad[:hidden], first[:side]) + dot_nt(second_grad[hidden:], first[side:])
-    return mid, dot_nt(first_grad[...], features[...]), dot_nt(second[...], grad[...])
-
-
-def late_terms_kernel(*refs):
-    for value, out in zip(term_sums(*refs[:6]), refs[6:]):
-        out[...] = value
-
-
-def early_terms_kernel(*refs):
-    late = refs[6:10]
-    g_sum, keep, send = refs[10:]
-    mid, wing, out = (a + b[...] for a, b in zip(term_sums(*refs[:6]), late[:3]))
-    total = late[3][...] + g_sum[...]
-    hidden = mid.shape[0]
+    return dot_nt(second_grad[:hidden], first[:side]) + dot_nt(second_grad[hidden:], first[side:])
+
+
+def outer_sums(second, features, grad, first_grad):
+    return dot_nt(first_grad[...], features[...]), dot_nt(second[...], grad[...])
+
+
+def late_terms_kernel(first, second, features, grad, second_grad, first_grad, mid, wing, out):
+    mid[...] = middle_sums(first, second_grad)
+    wing[...], out[...] = outer_sums(second, features, grad, first_grad)
+
+
+def middle_kernel(first, second_grad, late, keep, send, bias):
+    total = late[...] + middle_sums(first, second_grad)
+    half, hidden = keep.shape
+    core = lax.axis_index("sub")
+    low, high = total[:half, :hidden], total[half:, :hidden]
+    keep[...] = jnp.where(core == 0, low, high)
+    send[...] = jnp.where(core == 0, high, low)
+    bias[...] = total[:, hidden:]
+
+
+def outer_kernel(
+    second, features, grad, first_grad, late_wing, late_out, late_sum, early_sum, middle_bias,
+    packed
+):
+    wing, out = outer_sums(second, features, grad, first_grad)
+    wing = wing + late_wing[...]
+    out = out + late_out[...]
+    total = late_sum[...] + early_sum[...]
+    hidden = wing.shape[0] // 2
     top = iota((8, hidden), 0)
 
     def turned(block):
@@ -461,21 +479,14 @@
     low, high = turned(wing[:hidden]), turned(wing[hidden:])
     kinds = [low[8 * k : 8 * k + 8] + pltpu.roll(high[8 * k : 8 * k + 8], 4, 0) for k in range(3)]
     bias_in = low[24:32] + high[24:32]
-    bias_mid = turned(mid[:, hidden:])[:8]
+    bias_mid = turned(middle_bias[...])[:8]
     biases = jnp.where(top == 4, pltpu.roll(bias_in, 4, 0), pltpu.roll(bias_mid, 5, 0))
     low, high = turned(out[:hidden]), turned(out[hidden:])
-    pieces = [
-        mid[:, :hidden],
-        jnp.where(top < 4, kinds[0], pltpu.roll(kinds[1], 4, 0)),
-        jnp.where(top < 4, kinds[2], biases),
-        jnp.where(top < 4, low[:8] + pltpu.roll(high[:8], 4, 0), total + pltpu.roll(total, 4, 0)),
-        jnp.zeros((8, hidden), F32),
-    ]
-    packed = jnp.concatenate(pieces, axis=0)
-    half = packed.shape[0] // 2
-    core = lax.axis_index("sub")
-    keep[...] = jnp.where(core == 0, packed[:half], packed[half:])
-    send[...] = jnp.where(core == 0, packed[half:], packed[:half])
+    packed[0:8] = jnp.where(top < 4, kinds[0], pltpu.roll(kinds[1], 4, 0))
+    packed[8:16] = jnp.where(top < 4, kinds[2], biases)
+    packed[16:24] = jnp.where(
+        top < 4, low[:8] + pltpu.roll(high[:8], 4, 0), total + pltpu.roll(total, 4, 0)
+    )
 
 
 def finish_kernel(skip, base_in, mask, x_in, above, below, partner, codes, rows, *rest):
@@ -501,11 +512,10 @@
 def grads_kernel(scale, mine, other, token, w_in, b_in, w_mid, b_mid, w_out, b_out):
     hidden = w_mid.shape[0]
     core = lax.axis_index("sub")
-    low = jnp.where(core == 0, mine[...], other[...])
-    high = jnp.where(core == 0, other[...], mine[...])
-    packed = jnp.concatenate([low, high], axis=0) * scale
-    w_mid[...] = packed[:hidden]
-    tail = packed[hidden:]
+    half = hidden // 2
+    w_mid[:half] = jnp.where(core == 0, mine[:half], other[:half]) * scale
+    w_mid[half:] = jnp.where(core == 0, other[:half], mine[:half]) * scale
+    tail = (mine[half:] + other[half:]) * scale
     w_in[...] = tail[0:12]
     b_in[...] = tail[12:13]
     b_mid[...] = tail[13:14]
@@ -570,6 +580,16 @@
         [array]
         + [lax.ppermute(array, axis, xor_pairs(axis, k)) for k in range(1, lax.axis_size(axis))]
     )
+
+
+def total_halves(terms):
+    if lax.axis_size("depth") > 2:
+        mine = sum_over(terms, "depth")
+        return mine, lax.ppermute(mine, "sub", xor_pairs("sub", 1))
+    crossed = lax.ppermute(terms, ("depth", "sub"), [(i, i ^ 3) for i in range(4)])
+    below = lax.ppermute(terms, "depth", xor_pairs("depth", 1))
+    beside = lax.ppermute(terms, "sub", xor_pairs("sub", 1))
+    return terms + below, beside + crossed
 
 
 def body(
@@ -683,34 +703,46 @@
     )
 
     late, base = lax.optimization_barrier((late, base))
-    base, columns, lines, early_sum, grad, second_grad, first_grad, *levels_out = call(
-        functools.partial(back_kernel, peers),
-        [base, mask, x_one, partner, codes, first, second, rows] + backward_weights + pools,
+    g_early, *levels_out = call(
+        functools.partial(arrive_kernel, peers),
+        [base, mask, x_one, partner, codes, rows] + pools,
+        [field] + sends,
+    )
+    above, below = from_levels(levels_out)
+    base, columns, lines, early_sum, grad, second_grad, first_grad = call(
+        back_kernel,
+        [g_early, first, second, rows] + backward_weights,
         [
-            field, column_pack, line_pack, shape((8, LANES)), shape((16, total), BF), hidden_rows, hidden_rows,
-        ]
-        + sends,
+            field, column_pack, line_pack, shape((8, LANES)), shape((16, total), BF), hidden_rows,
+            hidden_rows,
+        ],
         [vmem((32, total), F32)],
     )
-    above, below = from_levels(levels_out)
     partner = from_partner(lines)
-    half = shape(((hidden + 32) // 2, hidden))
-    keep, give = call(
-        early_terms_kernel,
-        [first, second, features, grad, second_grad, first_grad, *late, late_sum, early_sum],
-        [half, half],
-    )
+    half = shape((hidden // 2, hidden))
+    late_mid, late_wing, late_out = late
+    keep, give, middle_bias = call(
+        middle_kernel, [first, second_grad, late_mid], [half, half, shape((hidden, 16))]
+    )
+    outer = call(
+        outer_kernel,
+        [
+            second, features, grad, first_grad, late_wing, late_out, late_sum, early_sum,
+            middle_bias,
+        ],
+        [shape((24, hidden))],
+    )[0]
     terms = keep + lax.ppermute(give, "sub", xor_pairs("sub", 1))
     terms, above, below, partner = lax.optimization_barrier((terms, above, below, partner))
-    parts = from_peers(jnp.concatenate([terms, columns.reshape(slots * 4, LANES)], axis=0))
-    terms = tree_sum([part[: half.shape[0]] for part in parts])
-    terms = sum_over(terms, "depth")
+    parts = from_peers(jnp.concatenate([terms, outer, columns.reshape(slots * 4, LANES)], axis=0))
+    rows_sent = terms.shape[0] + outer.shape[0]
+    terms = tree_sum([part[:rows_sent] for part in parts])
+    mine, other = total_halves(terms)
     final_state, initial_cot, token = call(
-        functools.partial(finish_kernel, half.shape[0]),
+        functools.partial(finish_kernel, rows_sent),
         [base, mask, x_two, above, below, partner, codes, rows] + parts,
         [shape(state_init.shape)] * 2 + [shape((8, LANES))],
     )
-    terms, token = lax.optimization_barrier((terms, token))
     count = (
         levels
         * lax.axis_size("depth")
@@ -721,7 +753,7 @@
     )
     w_in, b_in, w_mid, b_mid, w_out, b_out = call(
         functools.partial(grads_kernel, 1.0 / math.sqrt(count)),
-        [terms, lax.ppermute(terms, "sub", xor_pairs("sub", 1)), token],
+        [mine, other, token],
         [
             shape(weight_in.T.shape),
             shape((1, hidden)),

time: 62.1 us -> 60.2 us (0.969)
  waiting for transfers between devices: 11.3 us -> 8.27 us
  starting transfers between devices: 24.2 us -> 25.2 us
    ppermute x2 -> x3, waiting for transfers between devices: 2.82 us -> 1.2 us  [the longest x1 1.2 us: total_halves(): below = lax.ppermute(terms, 'depth', xor_pairs('depth', 1))]
    ppermute x2, waiting for transfers between devices: 1.29 us -> 0.01 us  [from_levels(): other = lax.ppermute(sends[0], 'depth', [(0, 1), (1, 0)])]
    ppermute x2 -> x3, starting transfers between devices: 1.3 us -> 2.21 us  [the longest x1 0.83 us: total_halves(): lax.ppermute(terms, ('depth', 'sub'), [(i, i ^ 3) for i in range(4)])]
    ppermute x1, waiting for transfers between devices: 0.71 us -> 0.01 us  [body(): terms = keep + lax.ppermute(give, 'sub', xor_pairs('sub', 1))]
    ppermute x12, waiting for transfers between devices: 6.4 us -> 7.04 us  [from_peers(): lax.ppermute(packs, 'tiles', xor_pairs('tiles', k))]
    pallas_call x10 -> x12, Pallas kernels: 25.3 us -> 25.5 us  [call(): pl.pallas_call(kernel, in_specs=[pl.BlockSpec(memory_space=spaces or pltp...]
  transfers between devices with their start and end apart: 21 -> 22, of which waited for: 9 -> 5; matrix products, arithmetic and copies ran while one was open for 0% -> 0% of each run, Pallas kernels for 18% -> 23%
where the time goes in v3:
time: 60.2 us; the launch traced here: 60 us
  Pallas kernels  25.5 us (42%)
  starting transfers between devices  25.2 us (42%)
  waiting for transfers between devices  8.27 us (14%)
  between operations  1.01 us (2%)
    pallas_call x12, Pallas kernels, call(): pl.pallas_call(kernel, in_specs=[pl.BlockSpec(memory_space=spaces or pltp...  25.5 us
    ppermute x12, starting transfers between devices, from_peers(): lax.ppermute(packs, 'tiles', xor_pairs('tiles', k))  17.7 us
    ppermute x12, waiting for transfers between devices, from_peers(): lax.ppermute(packs, 'tiles', xor_pairs('tiles', k))  7.04 us
    ppermute x2, starting transfers between devices, from_levels(): other = lax.ppermute(sends[0], 'depth', [(0, 1), (1, 0)])  4.56 us
  transfers between devices with their start and end apart: 22, of which 5 were waited for; matrix products, arithmetic and copies ran while one was open for 0% of the time, Pallas kernels for 23%

profile of v3, /device:TPU:0, one launch (start us, length us, event | category | flops | bytes accessed | tf_op | source)
XLA Modules:
  0.0 60.0 jit_solution(17343236751893045785)
XLA Ops:
  0.6 1.4 %shard_map.188 = (f32[8,8192]{1,0:T(8,128)S(1)}, f32[8,8192]{1,0:T(8,128)S(1)}, f32[8,8192]{1,0:T(8,128)S(1)}, f32[2,8,128]{2,1,0:T(8,128)S(1)}, f32[4,8,128]{2,...) custom-call(f32[2]{0:T(128)} %mix_v_in.3, f32[4,2,4,2048]{3,2,1,0:T(4,128)} %state_in.1, f32[4,2,4,2048]{3,2,1,0:T(4,128)} %cot_in.1, ...), custom_call_target="tpu_custom_call" | custom-call | tf_op jit(solution)/shard_map/pallas_call | solution.py:530
  2.0 3.0 %collective-permute-start = (f32[2,2,8,2048]{3,2,1,0:T(8,128)S(1)}, f32[2,2,8,2048]{3,2,1,0:T(8,128)S(1)}, u32[]{:S(2)}, u32[]{:S(2)}) collective-permute-start(f32[2,2,8,2048]{3,2,1,0:T(8,128)S(1)} %get-tuple-element.75), channel_id=1, source_target_pairs={{0,2},{2,0},{1,3},{3,1},{4,6},{6,4},{5,7},{7,5},{8,10},{10,8},{9,1... | collective-permute-start | bytes 786440 | tf_op jit(solution)/shard_map/ppermute | solution.py:563
  5.0 3.6 %collective-permute-start.4 = (f32[2,8,128]{2,1,0:T(8,128)S(1)}, f32[2,8,128]{2,1,0:T(8,128)S(1)}, u32[]{:S(2)}, u32[]{:S(2)}) collective-permute-start(f32[2,8,128]{2,1,0:T(8,128)S(1)} %get-tuple-element.83.rest_0_), channel_id=1, source_target_pairs={{0,12},{4,8},{8,4},{12,0},{1,13},{5,9},{9,5},{13,1},{2,14},{6,10},... | collective-permute-start | bytes 24584 | tf_op jit(solution)/shard_map/ppermute | solution.py:551
  9.4 1.1 %shard_map.189 = (bf16[256,32]{1,0:T(8,128)(2,1)S(1)}, bf16[32,256]{1,0:T(8,128)(2,1)S(1)}, bf16[256,256]{1,0:T(8,128)(2,1)S(1)}, bf16[256,256]{1,0:T(8,128)(2,1...) custom-call(f32[4]{0:T(128)} %mix_h_in.1, ...), custom_call_target="tpu_custom_call" | custom-call | tf_op jit(solution)/shard_map/pallas_call | solution.py:530
  10.6 2.6 %collective-permute-done.3.rest_2_ = f32[2,8,128]{2,1,0:T(8,128)S(1)} collective-permute-done((f32[2,8,128]{2,1,0:T(8,128)S(1)}, f32[2,8,128]{2,1,0:T(8,128)S(1)}, u32[]{:S(2)}, u32[]{:S(2)}) %collective-permute-start.3) | collective-permute-done | bytes 8224 | tf_op jit(solution)/shard_map/ppermute | solution.py:551
  13.2 3.4 %shard_map.190 = (f32[8,8192]{1,0:T(8,128)S(1)}, bf16[288,8192]{1,0:T(8,128)(2,1)S(1)}, bf16[256,8192]{1,0:T(8,128)(2,1)S(1)}, bf16[32,8192]{1,0:T(8,128)(2,1)S(...) custom-call(f32[8,8192]{1,0:T(8,128)S(1)} %get-tuple-element.73.x_in, f32[8,8192]{1,0:T(8,128)S(1)} %get-tuple-element.74.mask, ...), custom_call_target="tpu_custom_call" | custom-call | tf_op jit(solution)/shard_map/pallas_call | solution.py:530
  16.7 2.0 %collective-permute-start.8 = (f32[2,8,128]{2,1,0:T(8,128)S(1)}, f32[2,8,128]{2,1,0:T(8,128)S(1)}, u32[]{:S(2)}, u32[]{:S(2)}) collective-permute-start(f32[2,8,128]{2,1,0:T(8,128)S(1)} %get-tuple-element.91.rest_0_), channel_id=1, source_target_pairs={{0,12},{4,8},{8,4},{12,0},{1,13},{5,9},{9,5},{13,1},{2,14},{6,10},... | collective-permute-start | bytes 24584 | tf_op jit(solution)/shard_map/ppermute | solution.py:551
  18.8 2.3 %collective-permute-start.6 = (f32[2,8,128]{2,1,0:T(8,128)S(1)}, f32[2,8,128]{2,1,0:T(8,128)S(1)}, u32[]{:S(2)}, u32[]{:S(2)}) collective-permute-start(f32[2,8,128]{2,1,0:T(8,128)S(1)} %get-tuple-element.91.rest_0_), channel_id=1, source_target_pairs={{0,4},{4,0},{8,12},{12,8},{1,5},{5,1},{9,13},{13,9},{2,6},{6,2},{1... | collective-permute-start | bytes 24584 | tf_op jit(solution)/shard_map/ppermute | solution.py:551
  21.1 1.2 %shard_map.191 = (bf16[16,8192]{1,0:T(8,128)(2,1)S(1)}, bf16[256,8192]{1,0:T(8,128)(2,1)S(1)}) custom-call(f32[8,8192]{1,0:T(8,128)S(1)} %get-tuple-element.85.g_in, bf16[256,16]{1,0:T(8,128)(2,1)S(1)} %get-tuple-element.86.out_back), custom_call_target="tpu_custom_call" | custom-call | tf_op jit(solution)/shard_map/pallas_call | solution.py:530
  22.4 0.9 %collective-permute-done.7.rest_2_ = f32[2,8,128]{2,1,0:T(8,128)S(1)} collective-permute-done((f32[2,8,128]{2,1,0:T(8,128)S(1)}, f32[2,8,128]{2,1,0:T(8,128)S(1)}, u32[]{:S(2)}, u32[]{:S(2)}) %collective-permute-start.7) | collective-permute-done | bytes 8224 | tf_op jit(solution)/shard_map/ppermute | solution.py:551
  23.3 5.7 %shard_map.192 = (f32[8,8192]{1,0:T(8,128)S(1)}, f32[8,8192]{1,0:T(8,128)S(1)}, f32[2,8,128]{2,1,0:T(8,128)S(1)}, f32[4,8,128]{2,1,0:T(8,128)S(1)}, f32[8,128]{1...) custom-call(f32[8,8192]{1,0:T(8,128)S(1)} %get-tuple-element.84.x_in, ...), custom_call_target="tpu_custom_call" | custom-call | tf_op jit(solution)/shard_map/pallas_call | solution.py:530
  29.0 2.1 %collective-permute-start.12 = (f32[2,8,128]{2,1,0:T(8,128)S(1)}, f32[2,8,128]{2,1,0:T(8,128)S(1)}, u32[]{:S(2)}, u32[]{:S(2)}) collective-permute-start(f32[2,8,128]{2,1,0:T(8,128)S(1)} %get-tuple-element.104.rest_0_), channel_id=1, source_target_pairs={{0,12},{4,8},{8,4},{12,0},{1,13},{5,9},{9,5},{13,1},{2,14},{6,10},... | collective-permute-start | bytes 24584 | tf_op jit(solution)/shard_map/ppermute | solution.py:551
  32.1 1.4 %collective-permute-start.10 = (f32[2,8,128]{2,1,0:T(8,128)S(1)}, f32[2,8,128]{2,1,0:T(8,128)S(1)}, u32[]{:S(2)}, u32[]{:S(2)}) collective-permute-start(f32[2,8,128]{2,1,0:T(8,128)S(1)} %get-tuple-element.104.rest_0_), channel_id=1, source_target_pairs={{0,4},{4,0},{8,12},{12,8},{1,5},{5,1},{9,13},{13,9},{2,6},{6,2},{1... | collective-permute-start | bytes 24584 | tf_op jit(solution)/shard_map/ppermute | solution.py:551
  33.5 3.7 %shard_map.193 = (f32[128,144]{1,0:T(8,128)S(1)}, f32[256,32]{1,0:T(8,128)S(1)}, f32[256,16]{1,0:T(8,128)S(1)}) custom-call(bf16[288,8192]{1,0:T(8,128)(2,1)S(1)} %get-tuple-element.92.first, bf16[256,8192]{1,0:T(8,128)(2,1)S(1)} %get-tuple-element.93.second, bf16[32,8192]{1,0:T(8,128)(2,1)S(1)} %get-tuple-element.94.features, ...), custom_call_target="tpu_custom_call" | custom-call | tf_op jit(solution)/shard_map/pallas_call | solution.py:530
  37.5 1.6 %collective-permute-start.14 = (f32[2,2,8,2048]{3,2,1,0:T(8,128)S(1)}, f32[2,2,8,2048]{3,2,1,0:T(8,128)S(1)}, u32[]{:S(2)}, u32[]{:S(2)}) collective-permute-start(f32[2,2,8,2048]{3,2,1,0:T(8,128)S(1)} %get-tuple-element.114), channel_id=1, source_target_pairs={{0,2},{2,0},{1,3},{3,1},{4,6},{6,4},{5,7},{7,5},{8,10},{10,8},{9,1... | collective-permute-start | bytes 786440 | tf_op jit(solution)/shard_map/ppermute | solution.py:563
  39.1 3.1 %shard_map.195 = (f32[8,8192]{1,0:T(8,128)S(1)}, f32[2,8,128]{2,1,0:T(8,128)S(1)}, f32[4,8,128]{2,1,0:T(8,128)S(1)}, f32[8,128]{1,0:T(8,128)S(1)}, bf16[16,8192]...) custom-call(f32[8,8192]{1,0:T(8,128)S(1)} %get-tuple-element.105.g_in, ...), custom_call_target="tpu_custom_call" | custom-call | tf_op jit(solution)/shard_map/pallas_call | solution.py:530
  42.2 1.4 %shard_map.196 = (f32[64,128]{1,0:T(8,128)S(1)}, f32[64,128]{1,0:T(8,128)S(1)}, f32[128,16]{1,0:T(8,128)S(1)}) custom-call(bf16[288,8192]{1,0:T(8,128)(2,1)S(1)} %get-tuple-element.106.first_in.first, bf16[256,8192]{1,0:T(8,128)(2,1)S(1)} %get-tuple-element.110.second_grad, f32[128,144]{1,0:T(8,128)S(1)} %get-tuple-element.111.late), custom_call_target="tpu_custom_call" | custom-call | tf_op jit(solution)/shard_map/pallas_call | solution.py:530
  44.2 2.4 %shard_map.197 = f32[24,128]{1,0:T(8,128)S(1)} custom-call(bf16[256,8192]{1,0:T(8,128)(2,1)S(1)} %get-tuple-element.107.second_in.second, bf16[32,8192]{1,0:T(8,128)(2,1)S(1)} %get-tuple-element.120.features, bf16[16,8192]{1,0:T(8,128)(2,1)S(1)} %get-tuple-element.121.grad, bf16[256,8192]{1,0:T(8,128)(2,1)S(1)} %get-tuple-element.122.first_grad, ...), custom_call_target="tpu_custom_call" | custom-call | tf_op jit(solution)/shard_map/pallas_call | solution.py:530
  46.6 1.5 %collective-permute-start.18 = (f32[104,128]{1,0:T(8,128)S(1)}, f32[104,128]{1,0:T(8,128)S(1)}, u32[]{:S(2)}, u32[]{:S(2)}) collective-permute-start(f32[104,128]{1,0:T(8,128)S(1)} %pad_maximum_fusion.rest_0_), channel_id=1, source_target_pairs={{0,12},{4,8},{8,4},{12,0},{1,13},{5,9},{9,5},{13,1},{2,14},{6,10},... | collective-permute-start | bytes 159752 | tf_op jit(solution)/shard_map/ppermute | solution.py:551
  48.2 2.9 %collective-permute-start.16 = (f32[104,128]{1,0:T(8,128)S(1)}, f32[104,128]{1,0:T(8,128)S(1)}, u32[]{:S(2)}, u32[]{:S(2)}) collective-permute-start(f32[104,128]{1,0:T(8,128)S(1)} %pad_maximum_fusion.rest_0_), channel_id=1, source_target_pairs={{0,4},{4,0},{8,12},{12,8},{1,5},{5,1},{9,13},{13,9},{2,6},{6,2},{1... | collective-permute-start | bytes 159752 | tf_op jit(solution)/shard_map/ppermute | solution.py:551
  51.1 2.1 %collective-permute-done.18.rest_3_ = f32[104,128]{1,0:T(8,128)S(1)} collective-permute-done((f32[104,128]{1,0:T(8,128)S(1)}, f32[104,128]{1,0:T(8,128)S(1)}, u32[]{:S(2)}, u32[]{:S(2)}) %collective-permute-start.18) | collective-permute-done | bytes 53280 | tf_op jit(solution)/shard_map/ppermute | solution.py:551
  53.2 1.4 %collective-permute-done.17.rest_2_ = f32[104,128]{1,0:T(8,128)S(1)} collective-permute-done((f32[104,128]{1,0:T(8,128)S(1)}, f32[104,128]{1,0:T(8,128)S(1)}, u32[]{:S(2)}, u32[]{:S(2)}) %collective-permute-start.17) | collective-permute-done | bytes 53280 | tf_op jit(solution)/shard_map/ppermute | solution.py:551
  56.8 1.2 %shard_map.198 = (f32[4,2,4,2048]{3,2,1,0:T(4,128)}, f32[4,2,4,2048]{3,2,1,0:T(4,128)}, f32[8,128]{1,0:T(8,128)S(1)}) custom-call(f32[8,8192]{1,0:T(8,128)S(1)} %get-tuple-element.108.base_in, f32[8,8192]{1,0:T(8,128)S(1)} %get-tuple-element.74.mask, f32[8,8192]{1,0:T(8,128)S(1)} %get-tuple-element.109.x_in, ...), custom_call_target="tpu_custom_call" | custom-call | tf_op jit(solution)/shard_map/pallas_call | solution.py:530
  58.0 1.2 %collective-permute-done.19 = f32[88,128]{1,0:T(8,128)S(1)} collective-permute-done((f32[88,128]{1,0:T(8,128)S(1)}, f32[88,128]{1,0:T(8,128)S(1)}, u32[]{:S(2)}, u32[]{:S(2)}) %collective-permute-start.19) | collective-permute-done | bytes 45088 | tf_op jit(solution)/shard_map/ppermute | solution.py:590
  (37 shorter events, 5.8 us)
Async XLA Ops:
  2.0 11.2 %collective-permute-start = (f32[2,2,8,2048]{3,2,1,0:T(8,128)S(1)}, f32[2,2,8,2048]{3,2,1,0:T(8,128)S(1)}, u32[]{:S(2)}, u32[]{:S(2)}) collective-permute-start(f32[2,2,8,2048]{3,2,1,0:T(8,128)S(1)} %get-tuple-element.75), channel_id=1, source_target_pairs={{0,2},{2,0},{1,3},{3,1},{4,6},{6,4},{5,7},{7,5},{8,10},{10,8},{9,1... | collective-permute-start | bytes 786440 | tf_op jit(solution)/shard_map/ppermute | solution.py:563
  5.0 8.2 %collective-permute-start.1 = (f32[4,8,128]{2,1,0:T(8,128)S(1)}, f32[4,8,128]{2,1,0:T(8,128)S(1)}, u32[]{:S(2)}, u32[]{:S(2)}) collective-permute-start(f32[4,8,128]{2,1,0:T(8,128)S(1)} %get-tuple-element.76), channel_id=1, source_target_pairs={{0,1},{1,0},{2,3},{3,2},{4,5},{5,4},{6,7},{7,6},{8,9},{9,8},{10,11... | collective-permute-start | bytes 49160 | tf_op jit(solution)/shard_map/ppermute | solution.py:557
  5.0 5.5 %collective-permute-start.4 = (f32[2,8,128]{2,1,0:T(8,128)S(1)}, f32[2,8,128]{2,1,0:T(8,128)S(1)}, u32[]{:S(2)}, u32[]{:S(2)}) collective-permute-start(f32[2,8,128]{2,1,0:T(8,128)S(1)} %get-tuple-element.83.rest_0_), channel_id=1, source_target_pairs={{0,12},{4,8},{8,4},{12,0},{1,13},{5,9},{9,5},{13,1},{2,14},{6,10},... | collective-permute-start | bytes 24584 | tf_op jit(solution)/shard_map/ppermute | solution.py:551
  8.6 4.5 %collective-permute-start.3 = (f32[2,8,128]{2,1,0:T(8,128)S(1)}, f32[2,8,128]{2,1,0:T(8,128)S(1)}, u32[]{:S(2)}, u32[]{:S(2)}) collective-permute-start(f32[2,8,128]{2,1,0:T(8,128)S(1)} %get-tuple-element.83.rest_0_), channel_id=1, source_target_pairs={{0,8},{4,12},{8,0},{12,4},{1,9},{5,13},{9,1},{13,5},{2,10},{6,14},... | collective-permute-start | bytes 24584 | tf_op jit(solution)/shard_map/ppermute | solution.py:551
  8.6 4.5 %collective-permute-start.2 = (f32[2,8,128]{2,1,0:T(8,128)S(1)}, f32[2,8,128]{2,1,0:T(8,128)S(1)}, u32[]{:S(2)}, u32[]{:S(2)}) collective-permute-start(f32[2,8,128]{2,1,0:T(8,128)S(1)} %get-tuple-element.83.rest_0_), channel_id=1, source_target_pairs={{0,4},{4,0},{8,12},{12,8},{1,5},{5,1},{9,13},{13,9},{2,6},{6,2},{1... | collective-permute-start | bytes 24584 | tf_op jit(solution)/shard_map/ppermute | solution.py:551
  16.6 6.7 %collective-permute-start.5 = (f32[4,8,128]{2,1,0:T(8,128)S(1)}, f32[4,8,128]{2,1,0:T(8,128)S(1)}, u32[]{:S(2)}, u32[]{:S(2)}) collective-permute-start(f32[4,8,128]{2,1,0:T(8,128)S(1)} %get-tuple-element.88), channel_id=1, source_target_pairs={{0,1},{1,0},{2,3},{3,2},{4,5},{5,4},{6,7},{7,6},{8,9},{9,8},{10,11... | collective-permute-start | bytes 49160 | tf_op jit(solution)/shard_map/ppermute | solution.py:557
  16.7 5.7 %collective-permute-start.8 = (f32[2,8,128]{2,1,0:T(8,128)S(1)}, f32[2,8,128]{2,1,0:T(8,128)S(1)}, u32[]{:S(2)}, u32[]{:S(2)}) collective-permute-start(f32[2,8,128]{2,1,0:T(8,128)S(1)} %get-tuple-element.91.rest_0_), channel_id=1, source_target_pairs={{0,12},{4,8},{8,4},{12,0},{1,13},{5,9},{9,5},{13,1},{2,14},{6,10},... | collective-permute-start | bytes 24584 | tf_op jit(solution)/shard_map/ppermute | solution.py:551
  18.7 4.6 %collective-permute-start.7 = (f32[2,8,128]{2,1,0:T(8,128)S(1)}, f32[2,8,128]{2,1,0:T(8,128)S(1)}, u32[]{:S(2)}, u32[]{:S(2)}) collective-permute-start(f32[2,8,128]{2,1,0:T(8,128)S(1)} %get-tuple-element.91.rest_0_), channel_id=1, source_target_pairs={{0,8},{4,12},{8,0},{12,4},{1,9},{5,13},{9,1},{13,5},{2,10},{6,14},... | collective-permute-start | bytes 24584 | tf_op jit(solution)/shard_map/ppermute | solution.py:551
  18.8 4.4 %collective-permute-start.6 = (f32[2,8,128]{2,1,0:T(8,128)S(1)}, f32[2,8,128]{2,1,0:T(8,128)S(1)}, u32[]{:S(2)}, u32[]{:S(2)}) collective-permute-start(f32[2,8,128]{2,1,0:T(8,128)S(1)} %get-tuple-element.91.rest_0_), channel_id=1, source_target_pairs={{0,4},{4,0},{8,12},{12,8},{1,5},{5,1},{9,13},{13,9},{2,6},{6,2},{1... | collective-permute-start | bytes 24584 | tf_op jit(solution)/shard_map/ppermute | solution.py:551
  28.9 8.3 %collective-permute-start.9 = (f32[4,8,128]{2,1,0:T(8,128)S(1)}, f32[4,8,128]{2,1,0:T(8,128)S(1)}, u32[]{:S(2)}, u32[]{:S(2)}) collective-permute-start(f32[4,8,128]{2,1,0:T(8,128)S(1)} %get-tuple-element.103), channel_id=1, source_target_pairs={{0,1},{1,0},{2,3},{3,2},{4,5},{5,4},{6,7},{7,6},{8,9},{9,8},{10,11... | collective-permute-start | bytes 49160 | tf_op jit(solution)/shard_map/ppermute | solution.py:557
  29.0 8.2 %collective-permute-start.12 = (f32[2,8,128]{2,1,0:T(8,128)S(1)}, f32[2,8,128]{2,1,0:T(8,128)S(1)}, u32[]{:S(2)}, u32[]{:S(2)}) collective-permute-start(f32[2,8,128]{2,1,0:T(8,128)S(1)} %get-tuple-element.104.rest_0_), channel_id=1, source_target_pairs={{0,12},{4,8},{8,4},{12,0},{1,13},{5,9},{9,5},{13,1},{2,14},{6,10},... | collective-permute-start | bytes 24584 | tf_op jit(solution)/shard_map/ppermute | solution.py:551
  31.2 6.0 %collective-permute-start.11 = (f32[2,8,128]{2,1,0:T(8,128)S(1)}, f32[2,8,128]{2,1,0:T(8,128)S(1)}, u32[]{:S(2)}, u32[]{:S(2)}) collective-permute-start(f32[2,8,128]{2,1,0:T(8,128)S(1)} %get-tuple-element.104.rest_0_), channel_id=1, source_target_pairs={{0,8},{4,12},{8,0},{12,4},{1,9},{5,13},{9,1},{13,5},{2,10},{6,14},... | collective-permute-start | bytes 24584 | tf_op jit(solution)/shard_map/ppermute | solution.py:551
  32.1 5.2 %collective-permute-start.10 = (f32[2,8,128]{2,1,0:T(8,128)S(1)}, f32[2,8,128]{2,1,0:T(8,128)S(1)}, u32[]{:S(2)}, u32[]{:S(2)}) collective-permute-start(f32[2,8,128]{2,1,0:T(8,128)S(1)} %get-tuple-element.104.rest_0_), channel_id=1, source_target_pairs={{0,4},{4,0},{8,12},{12,8},{1,5},{5,1},{9,13},{13,9},{2,6},{6,2},{1... | collective-permute-start | bytes 24584 | tf_op jit(solution)/shard_map/ppermute | solution.py:551
  37.5 9.1 %collective-permute-start.14 = (f32[2,2,8,2048]{3,2,1,0:T(8,128)S(1)}, f32[2,2,8,2048]{3,2,1,0:T(8,128)S(1)}, u32[]{:S(2)}, u32[]{:S(2)}) collective-permute-start(f32[2,2,8,2048]{3,2,1,0:T(8,128)S(1)} %get-tuple-element.114), channel_id=1, source_target_pairs={{0,2},{2,0},{1,3},{3,1},{4,6},{6,4},{5,7},{7,5},{8,10},{10,8},{9,1... | collective-permute-start | bytes 786440 | tf_op jit(solution)/shard_map/ppermute | solution.py:563
  43.6 2.9 %collective-permute-start.13 = (f32[64,128]{1,0:T(8,128)S(1)}, f32[64,128]{1,0:T(8,128)S(1)}, u32[]{:S(2)}, u32[]{:S(2)}) collective-permute-start(f32[64,128]{1,0:T(8,128)S(1)} %get-tuple-element.113), channel_id=1, source_target_pairs={{0,1},{1,0},{2,3},{3,2},{4,5},{5,4},{6,7},{7,6},{8,9},{9,8},{10,11... | collective-permute-start | bytes 98312 | tf_op jit(solution)/shard_map/ppermute | solution.py:735
  43.7 2.9 %collective-permute-start.15 = (f32[4,8,128]{2,1,0:T(8,128)S(1)}, f32[4,8,128]{2,1,0:T(8,128)S(1)}, u32[]{:S(2)}, u32[]{:S(2)}) collective-permute-start(f32[4,8,128]{2,1,0:T(8,128)S(1)} %get-tuple-element.115), channel_id=1, source_target_pairs={{0,1},{1,0},{2,3},{3,2},{4,5},{5,4},{6,7},{7,6},{8,9},{9,8},{10,11... | collective-permute-start | bytes 49160 | tf_op jit(solution)/shard_map/ppermute | solution.py:557
  46.6 6.5 %collective-permute-start.18 = (f32[104,128]{1,0:T(8,128)S(1)}, f32[104,128]{1,0:T(8,128)S(1)}, u32[]{:S(2)}, u32[]{:S(2)}) collective-permute-start(f32[104,128]{1,0:T(8,128)S(1)} %pad_maximum_fusion.rest_0_), channel_id=1, source_target_pairs={{0,12},{4,8},{8,4},{12,0},{1,13},{5,9},{9,5},{13,1},{2,14},{6,10},... | collective-permute-start | bytes 159752 | tf_op jit(solution)/shard_map/ppermute | solution.py:551
  48.2 6.4 %collective-permute-start.17 = (f32[104,128]{1,0:T(8,128)S(1)}, f32[104,128]{1,0:T(8,128)S(1)}, u32[]{:S(2)}, u32[]{:S(2)}) collective-permute-start(f32[104,128]{1,0:T(8,128)S(1)} %pad_maximum_fusion.rest_0_), channel_id=1, source_target_pairs={{0,8},{4,12},{8,0},{12,4},{1,9},{5,13},{9,1},{13,5},{2,10},{6,14},... | collective-permute-start | bytes 159752 | tf_op jit(solution)/shard_map/ppermute | solution.py:551
  48.2 6.4 %collective-permute-start.16 = (f32[104,128]{1,0:T(8,128)S(1)}, f32[104,128]{1,0:T(8,128)S(1)}, u32[]{:S(2)}, u32[]{:S(2)}) collective-permute-start(f32[104,128]{1,0:T(8,128)S(1)} %pad_maximum_fusion.rest_0_), channel_id=1, source_target_pairs={{0,4},{4,0},{8,12},{12,8},{1,5},{5,1},{9,13},{13,9},{2,6},{6,2},{1... | collective-permute-start | bytes 159752 | tf_op jit(solution)/shard_map/ppermute | solution.py:551
  54.6 4.6 %collective-permute-start.19 = (f32[88,128]{1,0:T(8,128)S(1)}, f32[88,128]{1,0:T(8,128)S(1)}, u32[]{:S(2)}, u32[]{:S(2)}) collective-permute-start(f32[88,128]{1,0:T(8,128)S(1)} %fusion), channel_id=1, source_target_pairs={{0,2},{2,0},{1,3},{3,1},{4,6},{6,4},{5,7},{7,5},{8,10},{10,8},{9,1... | collective-permute-start | bytes 135176 | tf_op jit(solution)/shard_map/ppermute | solution.py:590
  55.2 4.0 %collective-permute-start.21 = (f32[88,128]{1,0:T(8,128)S(1)}, f32[88,128]{1,0:T(8,128)S(1)}, u32[]{:S(2)}, u32[]{:S(2)}) collective-permute-start(f32[88,128]{1,0:T(8,128)S(1)} %fusion), channel_id=1, source_target_pairs={{0,3},{1,2},{2,1},{3,0},{4,7},{5,6},{6,5},{7,4},{8,11},{9,10},{10,... | collective-permute-start | bytes 135176 | tf_op jit(solution)/shard_map/ppermute | solution.py:589
  56.0 3.1 %collective-permute-start.20 = (f32[88,128]{1,0:T(8,128)S(1)}, f32[88,128]{1,0:T(8,128)S(1)}, u32[]{:S(2)}, u32[]{:S(2)}) collective-permute-start(f32[88,128]{1,0:T(8,128)S(1)} %fusion), channel_id=1, source_target_pairs={{0,1},{1,0},{2,3},{3,2},{4,5},{5,4},{6,7},{7,6},{8,9},{9,8},{10,11... | collective-permute-start | bytes 135176 | tf_op jit(solution)/shard_map/ppermute | solution.py:591

commit v4 on v3

--- a/solution.py
+++ b/solution.py
@@ -158,14 +158,18 @@
     return jnp.concatenate(parts, axis=1)
 
 
-def fetch(pairs, sems):
+def start_fetch(pairs, sems):
     copies = [
         pltpu.make_async_copy(source, target, sems.at[i])
         for i, (source, target) in enumerate(pairs)
     ]
     for copy in copies:
         copy.start()
-    for copy in copies:
+    return copies
+
+
+def fetch(pairs, sems):
+    for copy in start_fetch(pairs, sems):
         copy.wait()
 
 
@@ -173,9 +177,11 @@
     x_out, g_out, mask_out, columns, lines = rest[:5]
     sends = rest[5 : 5 + sent]
     mix_v, state, cot, count, sems = rest[5 + sent :]
-    fetch(
+    copies = start_fetch(
         [(mix_v_in, mix_v), (count_in, count), (state_in, state), (cot_in, cot)], sems
     )
+    for copy in copies[:3]:
+        copy.wait()
     slots = state.shape[2]
     cells = state.shape[3]
     depth = lax.axis_index("depth")
@@ -185,19 +191,25 @@
             for f in range(4):
                 r = 4 * l + f
                 x_out[r : r + 1, span] = state[f, l, s : s + 1, :]
-                g_out[r : r + 1, span] = cot[f, l, s : s + 1, :]
     deep = jnp.concatenate(
         [jnp.broadcast_to(count[s : s + 1, :], (8, cells)) for s in range(slots)], axis=1
     )
     upper = iota(deep.shape, 0) < 4
     mask = jnp.where(2 * depth + jnp.where(upper, 0, 1) < deep, 1.0, 0.0)
     x = mask * x_out[...]
-    g = mask * g_out[...]
     mask_out[...] = mask
     x_out[...] = x
-    g_out[...] = g
     write_edges(columns, lines, x, x, x, x)
     write_sends(sends, 0, x, cells)
+    copies[3].wait()
+    for s in range(slots):
+        span = slice(s * cells, (s + 1) * cells)
+        for l in range(2):
+            for f in range(4):
+                r = 4 * l + f
+                g_out[r : r + 1, span] = cot[f, l, s : s + 1, :]
+    g = mask * g_out[...]
+    g_out[...] = g
     write_sends(sends, 1, jnp.where(upper, mix_v[0], mix_v[1]) * g, cells)
 
 

time: 60.2 us -> 60.3 us (level)
  no operation moved by 1% of the time
where the time goes in v4:
time: 60.3 us; the launch traced here: 60.1 us
  Pallas kernels  25.5 us (42%)
  starting transfers between devices  25.2 us (42%)
  waiting for transfers between devices  8.25 us (14%)
  between operations  1.01 us (2%)
    pallas_call x12, Pallas kernels, call(): pl.pallas_call(kernel, in_specs=[pl.BlockSpec(memory_space=spaces or pltp...  25.5 us
    ppermute x12, starting transfers between devices, from_peers(): lax.ppermute(packs, 'tiles', xor_pairs('tiles', k))  17.7 us
    ppermute x12, waiting for transfers between devices, from_peers(): lax.ppermute(packs, 'tiles', xor_pairs('tiles', k))  7.03 us
    ppermute x2, starting transfers between devices, from_levels(): other = lax.ppermute(sends[0], 'depth', [(0, 1), (1, 0)])  4.56 us
  transfers between devices with their start and end apart: 22, of which 5 were waited for; matrix products, arithmetic and copies ran while one was open for 0% of the time, Pallas kernels for 23%

profile of v4, /device:TPU:0, one launch (start us, length us, event | category | flops | bytes accessed | tf_op | source)
XLA Modules:
  0.0 60.1 jit_solution(11579444693016738601)
XLA Ops:
  0.6 1.4 %shard_map.188 = (f32[8,8192]{1,0:T(8,128)S(1)}, f32[8,8192]{1,0:T(8,128)S(1)}, f32[8,8192]{1,0:T(8,128)S(1)}, f32[2,8,128]{2,1,0:T(8,128)S(1)}, f32[4,8,128]{2,...) custom-call(f32[2]{0:T(128)} %mix_v_in.3, f32[4,2,4,2048]{3,2,1,0:T(4,128)} %state_in.1, f32[4,2,4,2048]{3,2,1,0:T(4,128)} %cot_in.1, ...), custom_call_target="tpu_custom_call" | custom-call | tf_op jit(solution)/shard_map/pallas_call | solution.py:542
  2.0 3.0 %collective-permute-start = (f32[2,2,8,2048]{3,2,1,0:T(8,128)S(1)}, f32[2,2,8,2048]{3,2,1,0:T(8,128)S(1)}, u32[]{:S(2)}, u32[]{:S(2)}) collective-permute-start(f32[2,2,8,2048]{3,2,1,0:T(8,128)S(1)} %get-tuple-element.75), channel_id=1, source_target_pairs={{0,2},{2,0},{1,3},{3,1},{4,6},{6,4},{5,7},{7,5},{8,10},{10,8},{9,1... | collective-permute-start | bytes 786440 | tf_op jit(solution)/shard_map/ppermute | solution.py:575
  5.0 3.6 %collective-permute-start.4 = (f32[2,8,128]{2,1,0:T(8,128)S(1)}, f32[2,8,128]{2,1,0:T(8,128)S(1)}, u32[]{:S(2)}, u32[]{:S(2)}) collective-permute-start(f32[2,8,128]{2,1,0:T(8,128)S(1)} %get-tuple-element.83.rest_0_), channel_id=1, source_target_pairs={{0,12},{4,8},{8,4},{12,0},{1,13},{5,9},{9,5},{13,1},{2,14},{6,10},... | collective-permute-start | bytes 24584 | tf_op jit(solution)/shard_map/ppermute | solution.py:563
  9.4 1.1 %shard_map.189 = (bf16[256,32]{1,0:T(8,128)(2,1)S(1)}, bf16[32,256]{1,0:T(8,128)(2,1)S(1)}, bf16[256,256]{1,0:T(8,128)(2,1)S(1)}, bf16[256,256]{1,0:T(8,128)(2,1...) custom-call(f32[4]{0:T(128)} %mix_h_in.1, ...), custom_call_target="tpu_custom_call" | custom-call | tf_op jit(solution)/shard_map/pallas_call | solution.py:542
  10.6 2.6 %collective-permute-done.3.rest_2_ = f32[2,8,128]{2,1,0:T(8,128)S(1)} collective-permute-done((f32[2,8,128]{2,1,0:T(8,128)S(1)}, f32[2,8,128]{2,1,0:T(8,128)S(1)}, u32[]{:S(2)}, u32[]{:S(2)}) %collective-permute-start.3) | collective-permute-done | bytes 8224 | tf_op jit(solution)/shard_map/ppermute | solution.py:563
  13.2 3.4 %shard_map.190 = (f32[8,8192]{1,0:T(8,128)S(1)}, bf16[288,8192]{1,0:T(8,128)(2,1)S(1)}, bf16[256,8192]{1,0:T(8,128)(2,1)S(1)}, bf16[32,8192]{1,0:T(8,128)(2,1)S(...) custom-call(f32[8,8192]{1,0:T(8,128)S(1)} %get-tuple-element.73.x_in, f32[8,8192]{1,0:T(8,128)S(1)} %get-tuple-element.74.mask, ...), custom_call_target="tpu_custom_call" | custom-call | tf_op jit(solution)/shard_map/pallas_call | solution.py:542
  16.7 2.0 %collective-permute-start.8 = (f32[2,8,128]{2,1,0:T(8,128)S(1)}, f32[2,8,128]{2,1,0:T(8,128)S(1)}, u32[]{:S(2)}, u32[]{:S(2)}) collective-permute-start(f32[2,8,128]{2,1,0:T(8,128)S(1)} %get-tuple-element.91.rest_0_), channel_id=1, source_target_pairs={{0,12},{4,8},{8,4},{12,0},{1,13},{5,9},{9,5},{13,1},{2,14},{6,10},... | collective-permute-start | bytes 24584 | tf_op jit(solution)/shard_map/ppermute | solution.py:563
  18.8 2.3 %collective-permute-start.6 = (f32[2,8,128]{2,1,0:T(8,128)S(1)}, f32[2,8,128]{2,1,0:T(8,128)S(1)}, u32[]{:S(2)}, u32[]{:S(2)}) collective-permute-start(f32[2,8,128]{2,1,0:T(8,128)S(1)} %get-tuple-element.91.rest_0_), channel_id=1, source_target_pairs={{0,4},{4,0},{8,12},{12,8},{1,5},{5,1},{9,13},{13,9},{2,6},{6,2},{1... | collective-permute-start | bytes 24584 | tf_op jit(solution)/shard_map/ppermute | solution.py:563
  21.2 1.2 %shard_map.191 = (bf16[16,8192]{1,0:T(8,128)(2,1)S(1)}, bf16[256,8192]{1,0:T(8,128)(2,1)S(1)}) custom-call(f32[8,8192]{1,0:T(8,128)S(1)} %get-tuple-element.85.g_in, bf16[256,16]{1,0:T(8,128)(2,1)S(1)} %get-tuple-element.86.out_back), custom_call_target="tpu_custom_call" | custom-call | tf_op jit(solution)/shard_map/pallas_call | solution.py:542
  23.3 5.7 %shard_map.192 = (f32[8,8192]{1,0:T(8,128)S(1)}, f32[8,8192]{1,0:T(8,128)S(1)}, f32[2,8,128]{2,1,0:T(8,128)S(1)}, f32[4,8,128]{2,1,0:T(8,128)S(1)}, f32[8,128]{1...) custom-call(f32[8,8192]{1,0:T(8,128)S(1)} %get-tuple-element.84.x_in, ...), custom_call_target="tpu_custom_call" | custom-call | tf_op jit(solution)/shard_map/pallas_call | solution.py:542
  29.0 2.1 %collective-permute-start.12 = (f32[2,8,128]{2,1,0:T(8,128)S(1)}, f32[2,8,128]{2,1,0:T(8,128)S(1)}, u32[]{:S(2)}, u32[]{:S(2)}) collective-permute-start(f32[2,8,128]{2,1,0:T(8,128)S(1)} %get-tuple-element.104.rest_0_), channel_id=1, source_target_pairs={{0,12},{4,8},{8,4},{12,0},{1,13},{5,9},{9,5},{13,1},{2,14},{6,10},... | collective-permute-start | bytes 24584 | tf_op jit(solution)/shard_map/ppermute | solution.py:563
  31.2 0.9 %collective-permute-start.11 = (f32[2,8,128]{2,1,0:T(8,128)S(1)}, f32[2,8,128]{2,1,0:T(8,128)S(1)}, u32[]{:S(2)}, u32[]{:S(2)}) collective-permute-start(f32[2,8,128]{2,1,0:T(8,128)S(1)} %get-tuple-element.104.rest_0_), channel_id=1, source_target_pairs={{0,8},{4,12},{8,0},{12,4},{1,9},{5,13},{9,1},{13,5},{2,10},{6,14},... | collective-permute-start | bytes 24584 | tf_op jit(solution)/shard_map/ppermute | solution.py:563
  32.1 1.4 %collective-permute-start.10 = (f32[2,8,128]{2,1,0:T(8,128)S(1)}, f32[2,8,128]{2,1,0:T(8,128)S(1)}, u32[]{:S(2)}, u32[]{:S(2)}) collective-permute-start(f32[2,8,128]{2,1,0:T(8,128)S(1)} %get-tuple-element.104.rest_0_), channel_id=1, source_target_pairs={{0,4},{4,0},{8,12},{12,8},{1,5},{5,1},{9,13},{13,9},{2,6},{6,2},{1... | collective-permute-start | bytes 24584 | tf_op jit(solution)/shard_map/ppermute | solution.py:563
  33.5 3.7 %shard_map.193 = (f32[128,144]{1,0:T(8,128)S(1)}, f32[256,32]{1,0:T(8,128)S(1)}, f32[256,16]{1,0:T(8,128)S(1)}) custom-call(bf16[288,8192]{1,0:T(8,128)(2,1)S(1)} %get-tuple-element.92.first, bf16[256,8192]{1,0:T(8,128)(2,1)S(1)} %get-tuple-element.93.second, bf16[32,8192]{1,0:T(8,128)(2,1)S(1)} %get-tuple-element.94.features, ...), custom_call_target="tpu_custom_call" | custom-call | tf_op jit(solution)/shard_map/pallas_call | solution.py:542
  37.6 1.6 %collective-permute-start.14 = (f32[2,2,8,2048]{3,2,1,0:T(8,128)S(1)}, f32[2,2,8,2048]{3,2,1,0:T(8,128)S(1)}, u32[]{:S(2)}, u32[]{:S(2)}) collective-permute-start(f32[2,2,8,2048]{3,2,1,0:T(8,128)S(1)} %get-tuple-element.114), channel_id=1, source_target_pairs={{0,2},{2,0},{1,3},{3,1},{4,6},{6,4},{5,7},{7,5},{8,10},{10,8},{9,1... | collective-permute-start | bytes 786440 | tf_op jit(solution)/shard_map/ppermute | solution.py:575
  39.1 3.1 %shard_map.195 = (f32[8,8192]{1,0:T(8,128)S(1)}, f32[2,8,128]{2,1,0:T(8,128)S(1)}, f32[4,8,128]{2,1,0:T(8,128)S(1)}, f32[8,128]{1,0:T(8,128)S(1)}, bf16[16,8192]...) custom-call(f32[8,8192]{1,0:T(8,128)S(1)} %get-tuple-element.105.g_in, ...), custom_call_target="tpu_custom_call" | custom-call | tf_op jit(solution)/shard_map/pallas_call | solution.py:542
  42.3 1.4 %shard_map.196 = (f32[64,128]{1,0:T(8,128)S(1)}, f32[64,128]{1,0:T(8,128)S(1)}, f32[128,16]{1,0:T(8,128)S(1)}) custom-call(bf16[288,8192]{1,0:T(8,128)(2,1)S(1)} %get-tuple-element.106.first_in.first, bf16[256,8192]{1,0:T(8,128)(2,1)S(1)} %get-tuple-element.110.second_grad, f32[128,144]{1,0:T(8,128)S(1)} %get-tuple-element.111.late), custom_call_target="tpu_custom_call" | custom-call | tf_op jit(solution)/shard_map/pallas_call | solution.py:542
  44.2 2.4 %shard_map.197 = f32[24,128]{1,0:T(8,128)S(1)} custom-call(bf16[256,8192]{1,0:T(8,128)(2,1)S(1)} %get-tuple-element.107.second_in.second, bf16[32,8192]{1,0:T(8,128)(2,1)S(1)} %get-tuple-element.120.features, bf16[16,8192]{1,0:T(8,128)(2,1)S(1)} %get-tuple-element.121.grad, bf16[256,8192]{1,0:T(8,128)(2,1)S(1)} %get-tuple-element.122.first_grad, ...), custom_call_target="tpu_custom_call" | custom-call | tf_op jit(solution)/shard_map/pallas_call | solution.py:542
  46.6 1.5 %collective-permute-start.18 = (f32[104,128]{1,0:T(8,128)S(1)}, f32[104,128]{1,0:T(8,128)S(1)}, u32[]{:S(2)}, u32[]{:S(2)}) collective-permute-start(f32[104,128]{1,0:T(8,128)S(1)} %pad_maximum_fusion.rest_0_), channel_id=1, source_target_pairs={{0,12},{4,8},{8,4},{12,0},{1,13},{5,9},{9,5},{13,1},{2,14},{6,10},... | collective-permute-start | bytes 159752 | tf_op jit(solution)/shard_map/ppermute | solution.py:563
  48.2 2.9 %collective-permute-start.16 = (f32[104,128]{1,0:T(8,128)S(1)}, f32[104,128]{1,0:T(8,128)S(1)}, u32[]{:S(2)}, u32[]{:S(2)}) collective-permute-start(f32[104,128]{1,0:T(8,128)S(1)} %pad_maximum_fusion.rest_0_), channel_id=1, source_target_pairs={{0,4},{4,0},{8,12},{12,8},{1,5},{5,1},{9,13},{13,9},{2,6},{6,2},{1... | collective-permute-start | bytes 159752 | tf_op jit(solution)/shard_map/ppermute | solution.py:563
  51.1 2.1 %collective-permute-done.18.rest_3_ = f32[104,128]{1,0:T(8,128)S(1)} collective-permute-done((f32[104,128]{1,0:T(8,128)S(1)}, f32[104,128]{1,0:T(8,128)S(1)}, u32[]{:S(2)}, u32[]{:S(2)}) %collective-permute-start.18) | collective-permute-done | bytes 53280 | tf_op jit(solution)/shard_map/ppermute | solution.py:563
  53.2 1.4 %collective-permute-done.17.rest_2_ = f32[104,128]{1,0:T(8,128)S(1)} collective-permute-done((f32[104,128]{1,0:T(8,128)S(1)}, f32[104,128]{1,0:T(8,128)S(1)}, u32[]{:S(2)}, u32[]{:S(2)}) %collective-permute-start.17) | collective-permute-done | bytes 53280 | tf_op jit(solution)/shard_map/ppermute | solution.py:563
  56.8 1.2 %shard_map.198 = (f32[4,2,4,2048]{3,2,1,0:T(4,128)}, f32[4,2,4,2048]{3,2,1,0:T(4,128)}, f32[8,128]{1,0:T(8,128)S(1)}) custom-call(f32[8,8192]{1,0:T(8,128)S(1)} %get-tuple-element.108.base_in, f32[8,8192]{1,0:T(8,128)S(1)} %get-tuple-element.74.mask, f32[8,8192]{1,0:T(8,128)S(1)} %get-tuple-element.109.x_in, ...), custom_call_target="tpu_custom_call" | custom-call | tf_op jit(solution)/shard_map/pallas_call | solution.py:542
  58.0 1.2 %collective-permute-done.19 = f32[88,128]{1,0:T(8,128)S(1)} collective-permute-done((f32[88,128]{1,0:T(8,128)S(1)}, f32[88,128]{1,0:T(8,128)S(1)}, u32[]{:S(2)}, u32[]{:S(2)}) %collective-permute-start.19) | collective-permute-done | bytes 45088 | tf_op jit(solution)/shard_map/ppermute | solution.py:602
  (37 shorter events, 5.8 us)
Async XLA Ops:
  2.0 11.2 %collective-permute-start = (f32[2,2,8,2048]{3,2,1,0:T(8,128)S(1)}, f32[2,2,8,2048]{3,2,1,0:T(8,128)S(1)}, u32[]{:S(2)}, u32[]{:S(2)}) collective-permute-start(f32[2,2,8,2048]{3,2,1,0:T(8,128)S(1)} %get-tuple-element.75), channel_id=1, source_target_pairs={{0,2},{2,0},{1,3},{3,1},{4,6},{6,4},{5,7},{7,5},{8,10},{10,8},{9,1... | collective-permute-start | bytes 786440 | tf_op jit(solution)/shard_map/ppermute | solution.py:575
  5.0 8.2 %collective-permute-start.1 = (f32[4,8,128]{2,1,0:T(8,128)S(1)}, f32[4,8,128]{2,1,0:T(8,128)S(1)}, u32[]{:S(2)}, u32[]{:S(2)}) collective-permute-start(f32[4,8,128]{2,1,0:T(8,128)S(1)} %get-tuple-element.76), channel_id=1, source_target_pairs={{0,1},{1,0},{2,3},{3,2},{4,5},{5,4},{6,7},{7,6},{8,9},{9,8},{10,11... | collective-permute-start | bytes 49160 | tf_op jit(solution)/shard_map/ppermute | solution.py:569
  5.0 5.5 %collective-permute-start.4 = (f32[2,8,128]{2,1,0:T(8,128)S(1)}, f32[2,8,128]{2,1,0:T(8,128)S(1)}, u32[]{:S(2)}, u32[]{:S(2)}) collective-permute-start(f32[2,8,128]{2,1,0:T(8,128)S(1)} %get-tuple-element.83.rest_0_), channel_id=1, source_target_pairs={{0,12},{4,8},{8,4},{12,0},{1,13},{5,9},{9,5},{13,1},{2,14},{6,10},... | collective-permute-start | bytes 24584 | tf_op jit(solution)/shard_map/ppermute | solution.py:563
  8.6 4.5 %collective-permute-start.3 = (f32[2,8,128]{2,1,0:T(8,128)S(1)}, f32[2,8,128]{2,1,0:T(8,128)S(1)}, u32[]{:S(2)}, u32[]{:S(2)}) collective-permute-start(f32[2,8,128]{2,1,0:T(8,128)S(1)} %get-tuple-element.83.rest_0_), channel_id=1, source_target_pairs={{0,8},{4,12},{8,0},{12,4},{1,9},{5,13},{9,1},{13,5},{2,10},{6,14},... | collective-permute-start | bytes 24584 | tf_op jit(solution)/shard_map/ppermute | solution.py:563
  8.6 4.5 %collective-permute-start.2 = (f32[2,8,128]{2,1,0:T(8,128)S(1)}, f32[2,8,128]{2,1,0:T(8,128)S(1)}, u32[]{:S(2)}, u32[]{:S(2)}) collective-permute-start(f32[2,8,128]{2,1,0:T(8,128)S(1)} %get-tuple-element.83.rest_0_), channel_id=1, source_target_pairs={{0,4},{4,0},{8,12},{12,8},{1,5},{5,1},{9,13},{13,9},{2,6},{6,2},{1... | collective-permute-start | bytes 24584 | tf_op jit(solution)/shard_map/ppermute | solution.py:563
  16.6 6.7 %collective-permute-start.5 = (f32[4,8,128]{2,1,0:T(8,128)S(1)}, f32[4,8,128]{2,1,0:T(8,128)S(1)}, u32[]{:S(2)}, u32[]{:S(2)}) collective-permute-start(f32[4,8,128]{2,1,0:T(8,128)S(1)} %get-tuple-element.88), channel_id=1, source_target_pairs={{0,1},{1,0},{2,3},{3,2},{4,5},{5,4},{6,7},{7,6},{8,9},{9,8},{10,11... | collective-permute-start | bytes 49160 | tf_op jit(solution)/shard_map/ppermute | solution.py:569
  16.7 5.7 %collective-permute-start.8 = (f32[2,8,128]{2,1,0:T(8,128)S(1)}, f32[2,8,128]{2,1,0:T(8,128)S(1)}, u32[]{:S(2)}, u32[]{:S(2)}) collective-permute-start(f32[2,8,128]{2,1,0:T(8,128)S(1)} %get-tuple-element.91.rest_0_), channel_id=1, source_target_pairs={{0,12},{4,8},{8,4},{12,0},{1,13},{5,9},{9,5},{13,1},{2,14},{6,10},... | collective-permute-start | bytes 24584 | tf_op jit(solution)/shard_map/ppermute | solution.py:563
  18.7 4.6 %collective-permute-start.7 = (f32[2,8,128]{2,1,0:T(8,128)S(1)}, f32[2,8,128]{2,1,0:T(8,128)S(1)}, u32[]{:S(2)}, u32[]{:S(2)}) collective-permute-start(f32[2,8,128]{2,1,0:T(8,128)S(1)} %get-tuple-element.91.rest_0_), channel_id=1, source_target_pairs={{0,8},{4,12},{8,0},{12,4},{1,9},{5,13},{9,1},{13,5},{2,10},{6,14},... | collective-permute-start | bytes 24584 | tf_op jit(solution)/shard_map/ppermute | solution.py:563
  18.8 4.5 %collective-permute-start.6 = (f32[2,8,128]{2,1,0:T(8,128)S(1)}, f32[2,8,128]{2,1,0:T(8,128)S(1)}, u32[]{:S(2)}, u32[]{:S(2)}) collective-permute-start(f32[2,8,128]{2,1,0:T(8,128)S(1)} %get-tuple-element.91.rest_0_), channel_id=1, source_target_pairs={{0,4},{4,0},{8,12},{12,8},{1,5},{5,1},{9,13},{13,9},{2,6},{6,2},{1... | collective-permute-start | bytes 24584 | tf_op jit(solution)/shard_map/ppermute | solution.py:563
  29.0 8.3 %collective-permute-start.9 = (f32[4,8,128]{2,1,0:T(8,128)S(1)}, f32[4,8,128]{2,1,0:T(8,128)S(1)}, u32[]{:S(2)}, u32[]{:S(2)}) collective-permute-start(f32[4,8,128]{2,1,0:T(8,128)S(1)} %get-tuple-element.103), channel_id=1, source_target_pairs={{0,1},{1,0},{2,3},{3,2},{4,5},{5,4},{6,7},{7,6},{8,9},{9,8},{10,11... | collective-permute-start | bytes 49160 | tf_op jit(solution)/shard_map/ppermute | solution.py:569
  29.0 8.2 %collective-permute-start.12 = (f32[2,8,128]{2,1,0:T(8,128)S(1)}, f32[2,8,128]{2,1,0:T(8,128)S(1)}, u32[]{:S(2)}, u32[]{:S(2)}) collective-permute-start(f32[2,8,128]{2,1,0:T(8,128)S(1)} %get-tuple-element.104.rest_0_), channel_id=1, source_target_pairs={{0,12},{4,8},{8,4},{12,0},{1,13},{5,9},{9,5},{13,1},{2,14},{6,10},... | collective-permute-start | bytes 24584 | tf_op jit(solution)/shard_map/ppermute | solution.py:563
  31.2 6.1 %collective-permute-start.11 = (f32[2,8,128]{2,1,0:T(8,128)S(1)}, f32[2,8,128]{2,1,0:T(8,128)S(1)}, u32[]{:S(2)}, u32[]{:S(2)}) collective-permute-start(f32[2,8,128]{2,1,0:T(8,128)S(1)} %get-tuple-element.104.rest_0_), channel_id=1, source_target_pairs={{0,8},{4,12},{8,0},{12,4},{1,9},{5,13},{9,1},{13,5},{2,10},{6,14},... | collective-permute-start | bytes 24584 | tf_op jit(solution)/shard_map/ppermute | solution.py:563
  32.1 5.1 %collective-permute-start.10 = (f32[2,8,128]{2,1,0:T(8,128)S(1)}, f32[2,8,128]{2,1,0:T(8,128)S(1)}, u32[]{:S(2)}, u32[]{:S(2)}) collective-permute-start(f32[2,8,128]{2,1,0:T(8,128)S(1)} %get-tuple-element.104.rest_0_), channel_id=1, source_target_pairs={{0,4},{4,0},{8,12},{12,8},{1,5},{5,1},{9,13},{13,9},{2,6},{6,2},{1... | collective-permute-start | bytes 24584 | tf_op jit(solution)/shard_map/ppermute | solution.py:563
  37.6 9.1 %collective-permute-start.14 = (f32[2,2,8,2048]{3,2,1,0:T(8,128)S(1)}, f32[2,2,8,2048]{3,2,1,0:T(8,128)S(1)}, u32[]{:S(2)}, u32[]{:S(2)}) collective-permute-start(f32[2,2,8,2048]{3,2,1,0:T(8,128)S(1)} %get-tuple-element.114), channel_id=1, source_target_pairs={{0,2},{2,0},{1,3},{3,1},{4,6},{6,4},{5,7},{7,5},{8,10},{10,8},{9,1... | collective-permute-start | bytes 786440 | tf_op jit(solution)/shard_map/ppermute | solution.py:575
  43.7 2.9 %collective-permute-start.13 = (f32[64,128]{1,0:T(8,128)S(1)}, f32[64,128]{1,0:T(8,128)S(1)}, u32[]{:S(2)}, u32[]{:S(2)}) collective-permute-start(f32[64,128]{1,0:T(8,128)S(1)} %get-tuple-element.113), channel_id=1, source_target_pairs={{0,1},{1,0},{2,3},{3,2},{4,5},{5,4},{6,7},{7,6},{8,9},{9,8},{10,11... | collective-permute-start | bytes 98312 | tf_op jit(solution)/shard_map/ppermute | solution.py:747
  43.7 2.9 %collective-permute-start.15 = (f32[4,8,128]{2,1,0:T(8,128)S(1)}, f32[4,8,128]{2,1,0:T(8,128)S(1)}, u32[]{:S(2)}, u32[]{:S(2)}) collective-permute-start(f32[4,8,128]{2,1,0:T(8,128)S(1)} %get-tuple-element.115), channel_id=1, source_target_pairs={{0,1},{1,0},{2,3},{3,2},{4,5},{5,4},{6,7},{7,6},{8,9},{9,8},{10,11... | collective-permute-start | bytes 49160 | tf_op jit(solution)/shard_map/ppermute | solution.py:569
  46.6 6.5 %collective-permute-start.18 = (f32[104,128]{1,0:T(8,128)S(1)}, f32[104,128]{1,0:T(8,128)S(1)}, u32[]{:S(2)}, u32[]{:S(2)}) collective-permute-start(f32[104,128]{1,0:T(8,128)S(1)} %pad_maximum_fusion.rest_0_), channel_id=1, source_target_pairs={{0,12},{4,8},{8,4},{12,0},{1,13},{5,9},{9,5},{13,1},{2,14},{6,10},... | collective-permute-start | bytes 159752 | tf_op jit(solution)/shard_map/ppermute | solution.py:563
  48.2 6.4 %collective-permute-start.17 = (f32[104,128]{1,0:T(8,128)S(1)}, f32[104,128]{1,0:T(8,128)S(1)}, u32[]{:S(2)}, u32[]{:S(2)}) collective-permute-start(f32[104,128]{1,0:T(8,128)S(1)} %pad_maximum_fusion.rest_0_), channel_id=1, source_target_pairs={{0,8},{4,12},{8,0},{12,4},{1,9},{5,13},{9,1},{13,5},{2,10},{6,14},... | collective-permute-start | bytes 159752 | tf_op jit(solution)/shard_map/ppermute | solution.py:563
  48.2 6.4 %collective-permute-start.16 = (f32[104,128]{1,0:T(8,128)S(1)}, f32[104,128]{1,0:T(8,128)S(1)}, u32[]{:S(2)}, u32[]{:S(2)}) collective-permute-start(f32[104,128]{1,0:T(8,128)S(1)} %pad_maximum_fusion.rest_0_), channel_id=1, source_target_pairs={{0,4},{4,0},{8,12},{12,8},{1,5},{5,1},{9,13},{13,9},{2,6},{6,2},{1... | collective-permute-start | bytes 159752 | tf_op jit(solution)/shard_map/ppermute | solution.py:563
  54.6 4.6 %collective-permute-start.19 = (f32[88,128]{1,0:T(8,128)S(1)}, f32[88,128]{1,0:T(8,128)S(1)}, u32[]{:S(2)}, u32[]{:S(2)}) collective-permute-start(f32[88,128]{1,0:T(8,128)S(1)} %fusion), channel_id=1, source_target_pairs={{0,2},{2,0},{1,3},{3,1},{4,6},{6,4},{5,7},{7,5},{8,10},{10,8},{9,1... | collective-permute-start | bytes 135176 | tf_op jit(solution)/shard_map/ppermute | solution.py:602
  55.2 4.0 %collective-permute-start.21 = (f32[88,128]{1,0:T(8,128)S(1)}, f32[88,128]{1,0:T(8,128)S(1)}, u32[]{:S(2)}, u32[]{:S(2)}) collective-permute-start(f32[88,128]{1,0:T(8,128)S(1)} %fusion), channel_id=1, source_target_pairs={{0,3},{1,2},{2,1},{3,0},{4,7},{5,6},{6,5},{7,4},{8,11},{9,10},{10,... | collective-permute-start | bytes 135176 | tf_op jit(solution)/shard_map/ppermute | solution.py:601
  56.1 3.1 %collective-permute-start.20 = (f32[88,128]{1,0:T(8,128)S(1)}, f32[88,128]{1,0:T(8,128)S(1)}, u32[]{:S(2)}, u32[]{:S(2)}) collective-permute-start(f32[88,128]{1,0:T(8,128)S(1)} %fusion), channel_id=1, source_target_pairs={{0,1},{1,0},{2,3},{3,2},{4,5},{5,4},{6,7},{7,6},{8,9},{9,8},{10,11... | collective-permute-start | bytes 135176 | tf_op jit(solution)/shard_map/ppermute | solution.py:603
